TPU v7x, 32 devices: a whole 2x2x4 slice. The times are simulated.
32 devices in a mesh: dp: 16 (over z, y, x), heads: 2 (over core).
Axes of the slice: x: 2, y: 2, z: 4, core: 2. Of those that a mesh axis runs over, the one named last changes fastest.
Arguments:
- tokens: bfloat16 [38912, 256], P(('dp', 'heads')), may hold values from -6 to 6
- cotangent: bfloat16 [38912, 256], P(('dp', 'heads')), may hold values from -6 to 6
- counts: int32 [64], P('dp'), may hold values from 2 to 6, as said below
- ln1_gain: float32 [2, 256], replicated, may hold values from 0.5 to 1.5
- ln1_bias: float32 [2, 256], replicated, may hold values from -1.75 to 1.75
- w_qkv: bfloat16 [2, 2, 256, 384], P(None, 'heads'), may hold values from -0.375 to 0.375
- lepe_w: float32 [2, 2, 9, 128], P(None, 'heads'), may hold values from -2 to 2
- lepe_b: float32 [2, 2, 128], P(None, 'heads'), may hold values from -1.75 to 1.75
- w_proj: bfloat16 [2, 256, 256], replicated, may hold values from -0.375 to 0.375
- b_proj: float32 [2, 256], replicated, may hold values from -1.75 to 1.75
- ln2_gain: float32 [2, 256], replicated, may hold values from 0.5 to 1.5
- ln2_bias: float32 [2, 256], replicated, may hold values from -1.75 to 1.75
- w_fc1: bfloat16 [2, 256, 1024], replicated, may hold values from -0.375 to 0.375
- b_fc1: float32 [2, 1024], replicated, may hold values from -1.75 to 1.75
- w_fc2: bfloat16 [2, 1024, 256], replicated, may hold values from -0.25 to 0.25
- b_fc2: float32 [2, 256], replicated, may hold values from -1.75 to 1.75
Outputs:
- output: bfloat16 [38912, 256], P(('dp', 'heads'))
- grad_tokens: float32 [38912, 256], P(('dp', 'heads'))
- g_ln1_gain: float32 [2, 256], replicated
- g_ln1_bias: float32 [2, 256], replicated
- g_w_qkv: float32 [2, 2, 256, 384], P(None, 'heads')
- g_lepe_w: float32 [2, 2, 9, 128], P(None, 'heads')
- g_lepe_b: float32 [2, 2, 128], P(None, 'heads')
- g_w_proj: float32 [2, 256, 256], replicated
- g_b_proj: float32 [2, 256], replicated
- g_ln2_gain: float32 [2, 256], replicated
- g_ln2_bias: float32 [2, 256], replicated
- g_w_fc1: float32 [2, 256, 1024], replicated
- g_b_fc1: float32 [2, 1024], replicated
- g_w_fc2: float32 [2, 1024, 256], replicated
- g_b_fc2: float32 [2, 256], replicated
Inputs may be any that keep to these rules, and one draw needn't show every extreme that they name: Local crop slots from counts on are padding and are masked from the output; some image has 6 local crops and some has 2.
All inputs are finite; a program needn't handle non-finite values.
Results may differ from a plain program's by a relative error of at most 0.018.
Values may be sent and summed in bfloat16 or wider, within the bound.
No kernel may reach another device: no remote copies, remote signals or barrier semaphores. Data moves between devices by JAX's collectives and lax.ppermute only.
A program may use at most 192 MiB of HBM per device.

v0:
```python
from functools import partial

import jax
import jax.numpy as jnp
from jax import lax
from jax.sharding import PartitionSpec as P

SW = 7
HD = 32
GH = 4
HW = 128
G1 = 14
G2 = 6
SW2 = 6
NG = 2
NL = 6
LAYERS = 2
TOK_IMG = 608


EPSILON = 1e-05


def layer_norm(value, gain, bias):
    center = value - jnp.mean(value, axis=-1, keepdims=True)
    spread = jnp.mean(center * center, axis=-1, keepdims=True)
    return center * lax.rsqrt(spread + EPSILON) * gain + bias


def keep_rows(counts, first, rows):
    index = first + jnp.arange(rows, dtype=jnp.int32)
    image = index // TOK_IMG
    place = index % TOK_IMG
    split = NG * G1 * G1
    crop = (place - split) // (G2 * G2)
    table = image[:, None] == jnp.arange(counts.shape[0], dtype=jnp.int32)[None, :]
    limit = jnp.sum(jnp.where(table, counts[None, :], 0), axis=1)
    return jnp.where((place < split) | (crop < limit), 1.0, 0.0).astype(jnp.float32)[:, None]


def orient(field, vertical):
    return jnp.where(vertical, jnp.swapaxes(field, 1, 2), field)


def to_windows(flat, vertical):
    total, width = flat.shape
    images = total // TOK_IMG
    split = NG * G1 * G1
    per_image = flat.reshape(images, TOK_IMG, width)
    parts = []
    for grid, stripe, count, start, stop in ((G1, SW, NG, 0, split), (G2, SW2, NL, split, TOK_IMG)):
        field = orient(
            per_image[:, start:stop].reshape(images * count, grid, grid, width), vertical
        )
        parts.append(field.reshape(images * count * (grid // stripe), stripe * grid, width))
    return parts


def from_windows(parts, vertical, images):
    pieces = []
    for part, grid, count in zip(parts, (G1, G2), (NG, NL)):
        width = part.shape[-1]
        field = orient(part.reshape(images * count, grid, grid, width), vertical)
        pieces.append(field.reshape(images, count * grid * grid, width))
    joined = jnp.concatenate(pieces, axis=1)
    return joined.reshape(images * TOK_IMG, joined.shape[-1])


def lepe_apply(values, weight, bias, grid, stripe):
    nwin = values.shape[0]
    padded = jnp.pad(values.reshape(nwin, stripe, grid, HW), ((0, 0), (1, 1), (1, 1), (0, 0)))
    local = jnp.zeros((nwin, stripe, grid, HW), jnp.float32) + bias
    for first in range(3):
        for second in range(3):
            local = (
                local
                + weight[3 * first + second]
                * padded[:, first : first + stripe, second : second + grid]
            )
    return local.reshape(nwin, stripe * grid, HW)


def split_heads(wins):
    nwin, span = (wins.shape[0], wins.shape[1])
    query = wins[:, :, :HW].reshape(nwin, span, GH, HD)
    keyset = wins[:, :, HW : 2 * HW].reshape(nwin, span, GH, HD)
    values = wins[:, :, 2 * HW :].reshape(nwin, span, GH, HD)
    return (query, keyset, values)


def attend_forward(wins, weight, bias, grid, stripe):
    nwin, span = (wins.shape[0], wins.shape[1])
    query, keyset, values = split_heads(wins)
    scores = jnp.einsum(
        "wqhd,wkhd->whqk", query, keyset, preferred_element_type=jnp.float32
    ) * HD ** (-0.5)
    top = jnp.max(scores, axis=-1, keepdims=True)
    expo = jnp.exp(scores - top)
    total = jnp.sum(expo, axis=-1, keepdims=True)
    probs = (expo / total).astype(jnp.bfloat16)
    mixed = jnp.einsum(
        "whqk,wkhd->wqhd", probs, values, preferred_element_type=jnp.float32
    ).reshape(nwin, span, HW)
    local = lepe_apply(wins[:, :, 2 * HW :].astype(jnp.float32), weight, bias, grid, stripe)
    return (mixed + local, top + jnp.log(total))


def attend_backward(grad, wins, logsum, weight, bias, grid, stripe):
    nwin, span = (wins.shape[0], wins.shape[1])
    query, keyset, values = split_heads(wins)
    scores = jnp.einsum(
        "wqhd,wkhd->whqk", query, keyset, preferred_element_type=jnp.float32
    ) * HD ** (-0.5)
    probs = jnp.exp(scores - logsum)
    grad_heads = grad.reshape(nwin, span, GH, HD)
    dvalues = jnp.einsum(
        "whqk,wqhd->wkhd",
        probs.astype(jnp.bfloat16),
        grad_heads,
        preferred_element_type=jnp.float32,
    )
    dprobs = jnp.einsum("wqhd,wkhd->whqk", grad_heads, values, preferred_element_type=jnp.float32)
    inner = jnp.sum(dprobs * probs, axis=-1, keepdims=True)
    dscores = (probs * (dprobs - inner)).astype(jnp.bfloat16)
    dquery = jnp.einsum(
        "whqk,wkhd->wqhd", dscores, keyset, preferred_element_type=jnp.float32
    ) * HD ** (-0.5)
    dkeys = jnp.einsum(
        "whqk,wqhd->wkhd", dscores, query, preferred_element_type=jnp.float32
    ) * HD ** (-0.5)
    unused, pull = jax.vjp(
        partial(lepe_apply, grid=grid, stripe=stripe),
        wins[:, :, 2 * HW :].astype(jnp.float32),
        weight,
        bias,
    )
    dlocal, dweight, dbias = pull(grad.astype(jnp.float32))
    joined = jnp.concatenate(
        [
            dquery.reshape(nwin, span, HW),
            dkeys.reshape(nwin, span, HW),
            dvalues.reshape(nwin, span, HW) + dlocal,
        ],
        axis=-1,
    )
    return (joined, dweight, dbias)


def forward_block(value, layer, vertical):
    (
        gain1,
        bias1,
        w_qkv,
        lepe_w,
        lepe_b,
        w_proj,
        b_proj,
        gain2,
        bias2,
        w_fc1,
        b_fc1,
        w_fc2,
        b_fc2,
    ) = layer
    normed_rows = layer_norm(value, gain1, bias1).astype(jnp.bfloat16)
    normed = lax.all_gather(normed_rows, "heads", axis=0, tiled=True)
    images = normed.shape[0] // TOK_IMG
    qkv = jnp.dot(normed, w_qkv, preferred_element_type=jnp.float32).astype(jnp.bfloat16)
    parts = to_windows(qkv, vertical)
    results, logsums = ([], [])
    for part, grid, stripe in zip(parts, (G1, G2), (SW, SW2)):
        result, logsum = attend_forward(part, lepe_w, lepe_b, grid, stripe)
        results.append(result)
        logsums.append(logsum)
    heads = from_windows(results, vertical, images).astype(jnp.bfloat16)
    kept_heads = lax.all_to_all(heads, "heads", split_axis=0, concat_axis=1, tiled=True)
    branch = jnp.dot(kept_heads, w_proj, preferred_element_type=jnp.float32) + b_proj
    inner = value + branch
    normed2 = layer_norm(inner, gain2, bias2).astype(jnp.bfloat16)
    hidden = jnp.dot(normed2, w_fc1, preferred_element_type=jnp.float32) + b_fc1
    act = jax.nn.gelu(hidden, approximate=False).astype(jnp.bfloat16)
    result = inner + jnp.dot(act, w_fc2, preferred_element_type=jnp.float32) + b_fc2
    return (result, (value, normed, parts, logsums, kept_heads, inner, normed2, hidden, act))


def backward_block(grad, kept, layer, vertical):
    (
        gain1,
        bias1,
        w_qkv,
        lepe_w,
        lepe_b,
        w_proj,
        b_proj,
        gain2,
        bias2,
        w_fc1,
        b_fc1,
        w_fc2,
        b_fc2,
    ) = layer
    value, normed, parts, logsums, kept_heads, inner, normed2, hidden, act = kept
    images = normed.shape[0] // TOK_IMG
    grad_out = grad.astype(jnp.bfloat16)
    g_fc2 = jnp.einsum("tf,td->fd", act, grad_out, preferred_element_type=jnp.float32)
    g_bfc2 = jnp.sum(grad_out.astype(jnp.float32), axis=0)
    dact = jnp.einsum("td,fd->tf", grad_out, w_fc2, preferred_element_type=jnp.float32)
    unused, pull = jax.vjp(partial(jax.nn.gelu, approximate=False), hidden)
    dhidden = pull(dact)[0].astype(jnp.bfloat16)
    g_fc1 = jnp.einsum("td,tf->df", normed2, dhidden, preferred_element_type=jnp.float32)
    g_bfc1 = jnp.sum(dhidden.astype(jnp.float32), axis=0)
    dnormed2 = jnp.einsum("tf,df->td", dhidden, w_fc1, preferred_element_type=jnp.float32)
    unused, pull = jax.vjp(layer_norm, inner, gain2, bias2)
    dinner_norm, g_gain2, g_bias2 = pull(dnormed2)
    dinner = grad + dinner_norm
    dbranch = dinner.astype(jnp.bfloat16)
    g_bproj = jnp.sum(dbranch.astype(jnp.float32), axis=0)
    g_proj = jnp.einsum("tc,td->cd", kept_heads, dbranch, preferred_element_type=jnp.float32)
    dheads_rows = jnp.einsum(
        "td,cd->tc", dbranch, w_proj, preferred_element_type=jnp.float32
    ).astype(jnp.bfloat16)
    dheads = lax.all_to_all(dheads_rows, "heads", split_axis=1, concat_axis=0, tiled=True)
    grad_parts = to_windows(dheads, vertical)
    dparts = []
    g_lepe_w = jnp.zeros(lepe_w.shape, jnp.float32)
    g_lepe_b = jnp.zeros(lepe_b.shape, jnp.float32)
    for grad_part, part, logsum, grid, stripe in zip(
        grad_parts, parts, logsums, (G1, G2), (SW, SW2)
    ):
        dpart, dweight, dbias = attend_backward(
            grad_part, part, logsum, lepe_w, lepe_b, grid, stripe
        )
        dparts.append(dpart)
        g_lepe_w = g_lepe_w + dweight
        g_lepe_b = g_lepe_b + dbias
    dqkv = from_windows(dparts, vertical, images).astype(jnp.bfloat16)
    g_qkv = jnp.einsum("tc,tk->ck", normed, dqkv, preferred_element_type=jnp.float32)
    dnormed = lax.psum_scatter(
        jnp.einsum("tk,ck->tc", dqkv, w_qkv, preferred_element_type=jnp.float32).astype(
            jnp.bfloat16
        ),
        "heads",
        scatter_dimension=0,
        tiled=True,
    ).astype(jnp.float32)
    unused, pull = jax.vjp(layer_norm, value, gain1, bias1)
    dvalue_norm, g_gain1, g_bias1 = pull(dnormed)
    shared = (g_gain1, g_bias1, g_proj, g_bproj, g_gain2, g_bias2, g_fc1, g_bfc1, g_fc2, g_bfc2)
    group = (g_qkv, g_lepe_w, g_lepe_b)
    return (dinner + dvalue_norm, shared, group)


def layer_params(stack, layer):
    return (
        stack[0][layer],
        stack[1][layer],
        stack[2][layer, 0],
        stack[3][layer, 0],
        stack[4][layer, 0],
        stack[5][layer],
        stack[6][layer],
        stack[7][layer],
        stack[8][layer],
        stack[9][layer],
        stack[10][layer],
        stack[11][layer],
        stack[12][layer],
    )


def shards(
    tokens,
    cotangent,
    counts,
    ln1_gain,
    ln1_bias,
    w_qkv,
    lepe_w,
    lepe_b,
    w_proj,
    b_proj,
    ln2_gain,
    ln2_bias,
    w_fc1,
    b_fc1,
    w_fc2,
    b_fc2,
):
    rows = tokens.shape[0]
    hindex = lax.axis_index("heads")
    vertical = hindex == 1
    keep = keep_rows(counts, hindex * rows, rows)
    stack = (
        ln1_gain,
        ln1_bias,
        w_qkv,
        lepe_w,
        lepe_b,
        w_proj,
        b_proj,
        ln2_gain,
        ln2_bias,
        w_fc1,
        b_fc1,
        w_fc2,
        b_fc2,
    )
    value = tokens.astype(jnp.float32)
    saved = []
    for layer in range(LAYERS):
        value, kept = forward_block(value, layer_params(stack, layer), vertical)
        saved.append(kept)
    result = (value * keep).astype(jnp.bfloat16)
    grad = cotangent.astype(jnp.float32) * keep
    shared_list = []
    group_list = []
    for layer in reversed(range(LAYERS)):
        grad, shared, group = backward_block(
            grad, saved[layer], layer_params(stack, layer), vertical
        )
        shared_list.insert(0, shared)
        group_list.insert(0, group)
    shared_all = tuple((jnp.stack([entry[place] for entry in shared_list]) for place in range(10)))
    group_all = tuple(
        (jnp.stack([entry[place] for entry in group_list])[:, None] for place in range(3))
    )
    shared_all = lax.psum(shared_all, ("dp", "heads"))
    group_all = lax.psum(group_all, "dp")
    return (
        result,
        grad,
        shared_all[0],
        shared_all[1],
        group_all[0],
        group_all[1],
        group_all[2],
        shared_all[2],
        shared_all[3],
        shared_all[4],
        shared_all[5],
        shared_all[6],
        shared_all[7],
        shared_all[8],
        shared_all[9],
    )


def solution(mesh):
    in_specs = (
        P(("dp", "heads"), None),
        P(("dp", "heads"), None),
        P("dp"),
        P(),
        P(),
        P(None, "heads", None, None),
        P(None, "heads", None, None),
        P(None, "heads", None),
        P(),
        P(),
        P(),
        P(),
        P(),
        P(),
        P(),
        P(),
    )
    out_specs = (
        P(("dp", "heads"), None),
        P(("dp", "heads"), None),
        P(),
        P(),
        P(None, "heads", None, None),
        P(None, "heads", None, None),
        P(None, "heads", None),
        P(),
        P(),
        P(),
        P(),
        P(),
        P(),
        P(),
        P(),
    )
    return jax.shard_map(shards, mesh=mesh, in_specs=in_specs, out_specs=out_specs, check_vma=False)
```

profile of v0, /device:TPU:0, one launch (start us, length us, event | category | flops | bytes accessed | tf_op | source)
XLA Modules:
  0.0 669.0 jit_solution(16704782607864541561)
XLA Ops:
  13.5 2.3 fusion.62
  19.6 8.4 %all-gather.3.cloned.1.call-done = bf16[2432,256]{1,0:T(8,128)(2,1)} async-done(((bf16[1216,256]{1,0:T(8,128)(2,1)}), bf16[2432,256]{1,0:T(8,128)(2,1)}) %all-gather.3.cloned.1.call-update) | async-done | bytes 1245200 | tf_op jit(solution)/shard_map/all_gather | solution.py:166
  28.0 2.1 convolution_convert_fusion.1
  33.4 2.3 reshape.756
  43.2 2.0 copy.484
  46.9 4.4 add_add_fusion.9
  62.2 3.6 copy.340
  65.8 2.3 reshape.760
  70.1 4.3 all_to_all.64
  76.3 13.4 %multiply_convert_fusion.1 = (bf16[1216,1024]{1,0:T(8,128)(2,1)S(1)}, f32[1216,1024]{1,0:T(8,128)}, f32[1216,1024]{1,0:T(8,128)}) fusion(f32[1024]{0:T(1024)S(1)} %bitcast.528, bf16[2,256,1024]{2,1,0:T(8,128)(2,1)S(1)} %copy-done.251, f32[1216,256]{1,0:T(8,128)S(1)} %get-tuple-element.249, f32[256]{0:T(256)S(1)} %bitcast.509, f32[256]{0:T(256)S(1)} %bitcast.501, ...), kind=kOutput, calls=%fused_computation.21 | convolution fusion | flops 721272832 | bytes 14243840 | tf_op jit(solution)/shard_map/dot_general | solution.py:180
  93.5 10.6 %all-gather.5.cloned.1.call-done = bf16[2432,256]{1,0:T(8,128)(2,1)} async-done(((bf16[1216,256]{1,0:T(8,128)(2,1)}), bf16[2432,256]{1,0:T(8,128)(2,1)}) %all-gather.5.cloned.1.call-update) | async-done | bytes 1245200 | tf_op jit(solution)/shard_map/all_gather | solution.py:166
  104.1 2.1 convolution_convert_fusion
  112.0 2.2 reshape.775
  119.0 2.0 copy.485
  122.6 3.9 add_add_fusion.8
  128.6 2.3 copy.359
  139.5 3.9 copy.361
  143.5 4.2 reshape.779
  150.6 1.9 reshape.782
  153.7 5.0 all_to_all.65
  158.7 2.2 copy.376
  160.9 2.1 fusion.186
  163.6 12.5 %multiply_convert_fusion = (bf16[1216,1024]{1,0:T(8,128)(2,1)}, f32[1216,1024]{1,0:T(8,128)S(1)}, f32[1216,1024]{1,0:T(8,128)S(1)}) fusion(f32[1024]{0:T(1024)S(1)} %bitcast.527, bf16[2,256,1024]{2,1,0:T(8,128)(2,1)S(1)} %copy-done.252, f32[1216,256]{1,0:T(8,128)S(1)} %get-tuple-element.258, f32[256]{0:T(256)S(1)} %bitcast.511, f32[256]{0:T(256)S(1)} %bitcast.505, ...), kind=kOutput, calls=%fused_computation.8 | convolution fusion | flops 721272832 | bytes 14243840 | tf_op jit(solution)/shard_map/dot_general | solution.py:180
  176.1 3.5 convert_reduce_fusion
  183.7 4.4 all_to_all.66
  189.5 1.9 reshape.793
  194.6 3.5 reshape_reshape.12
  199.8 5.4 fusion.83
  205.2 2.7 reshape.832
  207.9 2.5 copy.400
  211.3 3.0 multiply_reduce_fusion.5
  220.1 3.5 copy.379
  223.7 3.1 fusion.46
  232.4 3.2 convert_multiply_fusion.35
  235.6 2.0 multiply_reduce_fusion.24
  244.3 3.4 copy.386
  247.7 2.3 reshape.794
  250.0 3.1 copy.381
  254.0 2.7 copy.383
  270.2 1.9 convolution_convert_fusion.3
  275.3 2.1 multiply_reduce_fusion.15
  277.4 2.1 convolution_bitcast_fusion.10
  282.2 2.3 convert_reduce_fusion.5
  287.7 6.3 convert_reduce_fusion.1
  298.0 4.4 all_to_all.67
  307.0 3.5 fusion.92
  310.6 2.7 reshape.833
  322.6 3.3 copy.414
  326.0 3.1 fusion.49
  334.8 2.5 convert_multiply_fusion.17
  345.7 3.4 copy.421
  349.0 2.3 reshape.802
  351.4 3.1 copy.416
  355.3 2.3 copy.418
  369.6 1.9 convolution_convert_fusion.2
  372.1 3.9 convolution_bitcast_fusion.4
  376.1 2.2 convolution_bitcast_fusion.6
  386.5 2.7 convolution_bitcast_fusion.5
  391.1 3.0 convolution_bitcast_fusion.7
  396.2 77.2 %all-reduce.78 = (f32[2,1,9,128]{3,2,0,1:T(8,128)S(1)}, f32[2,1,128]{2,0,1:T(2,128)}) all-reduce(f32[2,1,9,128]{3,2,0,1:T(8,128)S(1)} %maximum_bitcast_fusion.1, f32[2,1,128]{2,0,1:T(2,128)S(1)} %maximum_bitcast_fusion.2), channel_id=1, replica_groups=mesh['dp'=16,'heads'=2] {'dp'}, use_global_device_ids=true, to_apply=%region_74.75 | all-reduce | flops 2560 | bytes 20480 | tf_op jit(solution)/shard_map/psum | solution.py:328
  477.9 37.8 %all-reduce.76 = (f32[2,256]{1,0:T(2,128)}, f32[2,256]{1,0:T(2,128)}, f32[2,256]{1,0:T(2,128)}, f32[2,256]{1,0:T(2,128)}, f32[2,256]{1,0:T(2,128)}, /*index=5*/f32[2,1024]{1,0:T(2,128)}, f32[2,256]{1,0:T(2,128)}) all-reduce(f32[2,256]{1,0:T(2,128)S(1)} %pad_maximum_fusion.10, ...), channel_id=1, replica_groups=mesh['dp'=16,'heads'=2] {'dp','heads'}, use_global_device_ids=true, to_apply=%region_33.34 | all-reduce | flops 5120 | bytes 40960 | tf_op jit(solution)/shard_map/psum | solution.py:327
  515.7 2.8 add_add_fusion.4
  518.6 135.6 %all-reduce.84.cloned.1.call-done = (f32[2,256,256]{2,1,0:T(8,128)}, f32[2,256,1024]{2,1,0:T(8,128)}, f32[2,1024,256]{2,1,0:T(8,128)}) async-done(((f32[2,256,256]{2,1,0:T(8,128)}, f32[2,256,1024]{2,1,0:T(8,128)}, f32[2,1024,256]{2,1,0:T(8,128)}), (f32[2,256,256]{2,1,0:T(8,128)}, f32[2,256,1024]{2,1,0:T(8,128)}, f32[2,1024,256]{2,1,0:T(8,128)})) %all-reduce.84.cloned.1.call-update) | async-done | bytes 4718608 | tf_op jit(solution)/shard_map/psum | solution.py:327
  654.1 2.2 copy.540
  (756 shorter events, 186.2 us)
Async XLA Ops:
  7.2 8.7 %copy-start.239 = (f32[2,1,128]{2,1,0:T(1,128)S(1)}, f32[2,1,128]{2,1,0:T(1,128)}, u32[]{:S(2)}) copy-start(f32[2,1,128]{2,1,0:T(1,128)} %param.23) | copy-start | bytes 3076
  7.2 8.7 %copy-start.235 = (f32[2,256]{1,0:T(2,128)S(1)}, f32[2,256]{1,0:T(2,128)}, u32[]{:S(2)}) copy-start(f32[2,256]{1,0:T(2,128)} %param.25) | copy-start | bytes 6148
  7.2 9.3 %copy-start.249 = (s32[4]{0:T(128)S(1)}, s32[4]{0:T(128)}, u32[]{:S(2)}) copy-start(s32[4]{0:T(128)} %param.18) | copy-start | bytes 52
  7.2 9.3 %copy-start.236 = (f32[2,256]{1,0:T(2,128)S(1)}, f32[2,256]{1,0:T(2,128)}, u32[]{:S(2)}) copy-start(f32[2,256]{1,0:T(2,128)} %param.26) | copy-start | bytes 6148
  7.2 9.9 %copy-start.237 = (f32[2,256]{1,0:T(2,128)S(1)}, f32[2,256]{1,0:T(2,128)}, u32[]{:S(2)}) copy-start(f32[2,256]{1,0:T(2,128)} %param.27) | copy-start | bytes 6148
  7.2 10.5 %copy-start.238 = (f32[2,256]{1,0:T(2,128)S(1)}, f32[2,256]{1,0:T(2,128)}, u32[]{:S(2)}) copy-start(f32[2,256]{1,0:T(2,128)} %param.31) | copy-start | bytes 6148
  7.2 11.0 %copy-start.194 = (f32[2,1,9,128]{3,1,2,0:T(1,128)S(1)}, f32[2,1,9,128]{3,1,2,0:T(1,128)}, u32[]{:S(2)}) copy-start(f32[2,1,9,128]{3,1,2,0:T(1,128)} %param.22) | copy-start | bytes 27652
  7.3 11.6 %copy-start.195 = (f32[2,1024]{1,0:T(2,128)S(1)}, f32[2,1024]{1,0:T(2,128)}, u32[]{:S(2)}) copy-start(f32[2,1024]{1,0:T(2,128)} %param.29) | copy-start | bytes 24580
  7.3 20.7 %copy-start.109 = (bf16[2,1,256,384]{3,2,1,0:T(8,128)(2,1)S(1)}, bf16[2,1,256,384]{3,2,1,0:T(8,128)(2,1)}, u32[]{:S(2)}) copy-start(bf16[2,1,256,384]{3,2,1,0:T(8,128)(2,1)} %param.21) | copy-start | bytes 1179652
  7.3 20.7 %all-gather.3.cloned.1.call-start = ((), (), s32[]{:S(2)}) async-start(), calls=%async_computation.6 | async-start | bytes 1867776 | tf_op jit(solution)/shard_map/all_gather | solution.py:166
  8.1 8.3 %copy-start.163 = (f32[1,256]{1,0:T(1,128)}, f32[1,256]{1,0:T(1,128)S(1)}, u32[]{:S(2)}) copy-start(f32[1,256]{1,0:T(1,128)S(1)} %get-tuple-element.239) | copy-start | bytes 3076
  8.1 84.1 %copy-start.161 = (f32[1,256]{1,0:T(1,128)}, f32[1,256]{1,0:T(1,128)S(1)}, u32[]{:S(2)}) copy-start(f32[1,256]{1,0:T(1,128)S(1)} %get-tuple-element.238) | copy-start | bytes 3076
  15.8 88.3 %all-gather.5.cloned.1.call-start = ((), (), s32[]{:S(2)}) async-start(), calls=%async_computation.7 | async-start | bytes 1867776 | tf_op jit(solution)/shard_map/all_gather | solution.py:166
  17.1 59.1 %copy-start.165 = (f32[1,256]{1,0:T(1,128)}, f32[1,256]{1,0:T(1,128)S(1)}, u32[]{:S(2)}) copy-start(f32[1,256]{1,0:T(1,128)S(1)} %get-tuple-element.233) | copy-start | bytes 3076
  17.7 58.6 %copy-start.190 = (f32[1,256]{1,0:T(1,128)}, f32[1,256]{1,0:T(1,128)S(1)}, u32[]{:S(2)}) copy-start(f32[1,256]{1,0:T(1,128)S(1)} %get-tuple-element.235) | copy-start | bytes 3076
  18.9 36.8 %copy-start.170 = (f32[128]{0:T(128)}, f32[128]{0:T(128)S(1)}, u32[]{:S(2)}) copy-start(f32[128]{0:T(128)S(1)} %get-tuple-element.217) | copy-start | bytes 1540
  18.9 36.8 %copy-start.172 = (f32[128]{0:T(128)}, f32[128]{0:T(128)S(1)}, u32[]{:S(2)}) copy-start(f32[128]{0:T(128)S(1)} %get-tuple-element.218) | copy-start | bytes 1540
  18.9 36.8 %copy-start.174 = (f32[128]{0:T(128)}, f32[128]{0:T(128)S(1)}, u32[]{:S(2)}) copy-start(f32[128]{0:T(128)S(1)} %get-tuple-element.219) | copy-start | bytes 1540
  18.9 36.8 %copy-start.176 = (f32[128]{0:T(128)}, f32[128]{0:T(128)S(1)}, u32[]{:S(2)}) copy-start(f32[128]{0:T(128)S(1)} %get-tuple-element.220) | copy-start | bytes 1540
  18.9 36.8 %copy-start.178 = (f32[128]{0:T(128)}, f32[128]{0:T(128)S(1)}, u32[]{:S(2)}) copy-start(f32[128]{0:T(128)S(1)} %get-tuple-element.221) | copy-start | bytes 1540
  18.9 36.8 %copy-start.180 = (f32[128]{0:T(128)}, f32[128]{0:T(128)S(1)}, u32[]{:S(2)}) copy-start(f32[128]{0:T(128)S(1)} %get-tuple-element.222) | copy-start | bytes 1540
  18.9 36.8 %copy-start.182 = (f32[128]{0:T(128)}, f32[128]{0:T(128)S(1)}, u32[]{:S(2)}) copy-start(f32[128]{0:T(128)S(1)} %get-tuple-element.223) | copy-start | bytes 1540
  19.0 36.8 %copy-start.184 = (f32[128]{0:T(128)}, f32[128]{0:T(128)S(1)}, u32[]{:S(2)}) copy-start(f32[128]{0:T(128)S(1)} %get-tuple-element.224) | copy-start | bytes 1540
  19.0 36.8 %copy-start.186 = (f32[128]{0:T(128)}, f32[128]{0:T(128)S(1)}, u32[]{:S(2)}) copy-start(f32[128]{0:T(128)S(1)} %get-tuple-element.225) | copy-start | bytes 1540
  19.0 114.1 %copy-start.188 = (f32[128]{0:T(128)}, f32[128]{0:T(128)S(1)}, u32[]{:S(2)}) copy-start(f32[128]{0:T(128)S(1)} %get-tuple-element.210) | copy-start | bytes 1540
  35.7 16.4 %copy-start.40 = (bf16[16,98,384]{2,1,0:T(8,128)(2,1)}, bf16[16,98,384]{2,1,0:T(8,128)(2,1)S(1)}, u32[]{:S(2)}) copy-start(bf16[16,98,384]{2,1,0:T(8,128)(2,1)S(1)} %reshape.756) | copy-start | bytes 3612676
  75.2 14.5 %copy-start.10 = (f32[1216,256]{1,0:T(8,128)}, f32[1216,256]{1,0:T(8,128)S(1)}, u32[]{:S(2)}) copy-start(f32[1216,256]{1,0:T(8,128)S(1)} %get-tuple-element.249) | copy-start | bytes 3735556
  75.2 14.5 %copy-start.132 = (f32[1216]{0:T(1024)}, f32[1216]{0:T(1024)S(1)}, u32[]{:S(2)}) copy-start(f32[1216]{0:T(1024)S(1)} %broadcast_multiply_fusion.20) | copy-start | bytes 14596
  76.3 13.4 %copy-start.139 = (f32[1216]{0:T(1024)}, f32[1216]{0:T(1024)S(1)}, u32[]{:S(2)}) copy-start(f32[1216]{0:T(1024)S(1)} %fusion.153) | copy-start | bytes 14596
  76.3 13.4 %copy-start.245 = (f32[1,256]{1,0:T(1,128)S(1)}, f32[1,256]{1,0:T(1,128)}, u32[]{:S(2)}) copy-start(f32[1,256]{1,0:T(1,128)} %get-tuple-element.231) | copy-start | bytes 3076
  76.3 13.4 %copy-start.254 = (bf16[2,1024,256]{2,1,0:T(8,128)(2,1)S(1)}, bf16[2,1024,256]{2,1,0:T(8,128)(2,1)}, u32[]{:S(2)}) copy-start(bf16[2,1024,256]{2,1,0:T(8,128)(2,1)} %param.30) | copy-start | bytes 3145732
  91.1 13.0 %copy-start.110 = (bf16[2,1,256,384]{3,2,1,0:T(8,128)(2,1)S(1)}, bf16[2,1,256,384]{3,2,1,0:T(8,128)(2,1)}, u32[]{:S(2)}) copy-start(bf16[2,1,256,384]{3,2,1,0:T(8,128)(2,1)} %param.21) | copy-start | bytes 1179652
  91.6 14.7 %copy-start.159 = (f32[1216]{0:T(1024)}, f32[1216]{0:T(1024)S(1)}, u32[]{:S(2)}) copy-start(f32[1216]{0:T(1024)S(1)} %multiply_reduce_fusion.13) | copy-start | bytes 14596
  93.5 188.7 %reduce-scatter.3.cloned.1.call-start = ((), (), s32[]{:S(2)}) async-start(), calls=%async_computation.8 | async-start | bytes 1867776 | tf_op jit(solution)/shard_map/reduce_scatter | solution.py:238
  114.2 13.1 %copy-start.41 = (bf16[16,98,384]{2,1,0:T(8,128)(2,1)}, bf16[16,98,384]{2,1,0:T(8,128)(2,1)S(1)}, u32[]{:S(2)}) copy-start(bf16[16,98,384]{2,1,0:T(8,128)(2,1)S(1)} %reshape.775) | copy-start | bytes 3612676
  152.5 8.4 %copy-start.203 = (f32[1,256]{1,0:T(1,128)S(1)}, f32[1,256]{1,0:T(1,128)}, u32[]{:S(2)}) copy-start(f32[1,256]{1,0:T(1,128)} %get-tuple-element.236) | copy-start | bytes 3076
  163.1 18.2 %copy-start.13 = (f32[1216,256]{1,0:T(8,128)}, f32[1216,256]{1,0:T(8,128)S(1)}, u32[]{:S(2)}) copy-start(f32[1216,256]{1,0:T(8,128)S(1)} %get-tuple-element.258) | copy-start | bytes 3735556
  163.5 17.8 %copy-start.142 = (f32[1216]{0:T(1024)}, f32[1216]{0:T(1024)S(1)}, u32[]{:S(2)}) copy-start(f32[1216]{0:T(1024)S(1)} %fusion.155) | copy-start | bytes 14596
  163.6 12.5 %copy-start.83 = (bf16[1216,256]{1,0:T(8,128)(2,1)S(1)}, bf16[1216,256]{1,0:T(8,128)(2,1)}, u32[]{:S(2)}) copy-start(bf16[1216,256]{1,0:T(8,128)(2,1)} %param.17) | copy-start | bytes 1867780
  163.6 12.5 %copy-start.152 = (f32[1216]{0:T(1024)S(1)}, f32[1216]{0:T(1024)}, u32[]{:S(2)}) copy-start(f32[1216]{0:T(1024)} %get-tuple-element.274) | copy-start | bytes 14596
  163.6 12.5 %copy-start.255 = (bf16[2,1024,256]{2,1,0:T(8,128)(2,1)S(1)}, bf16[2,1024,256]{2,1,0:T(8,128)(2,1)}, u32[]{:S(2)}) copy-start(bf16[2,1024,256]{2,1,0:T(8,128)(2,1)} %param.30) | copy-start | bytes 3145732
  272.1 202.0 %reduce-scatter.5.cloned.1.call-start = ((), (), s32[]{:S(2)}) async-start(), calls=%async_computation.9 | async-start | bytes 1867776 | tf_op jit(solution)/shard_map/reduce_scatter | solution.py:238
  287.6 8.9 %copy-start.15 = (f32[1216,256]{1,0:T(8,128)}, f32[1216,256]{1,0:T(8,128)S(1)}, u32[]{:S(2)}) copy-start(f32[1216,256]{1,0:T(8,128)S(1)} %get-tuple-element.146) | copy-start | bytes 3735556
  371.5 147.1 %all-reduce.82.cloned.1.call-start = ((), (), s32[]{:S(2)}) async-start(), calls=%async_computation.10 | async-start | bytes 1572864 | tf_op jit(solution)/shard_map/psum | solution.py:328
  390.8 263.3 %all-reduce.84.cloned.1.call-start = ((), (), s32[]{:S(2)}) async-start(), calls=%async_computation.11 | async-start | bytes 9437184 | tf_op jit(solution)/shard_map/psum | solution.py:327
  395.6 78.4 %copy-start.198 = (f32[256]{0:T(256)S(1)}, f32[256]{0:T(256)}, u32[]{:S(2)}) copy-start(f32[256]{0:T(256)} %get-tuple-element.191) | copy-start | bytes 3076
  395.6 78.4 %copy-start.201 = (f32[256]{0:T(256)S(1)}, f32[256]{0:T(256)}, u32[]{:S(2)}) copy-start(f32[256]{0:T(256)} %get-tuple-element.145) | copy-start | bytes 3076
  395.6 78.4 %copy-start.242 = (f32[256]{0:T(256)S(1)}, f32[256]{0:T(256)}, u32[]{:S(2)}) copy-start(f32[256]{0:T(256)} %get-tuple-element.77) | copy-start | bytes 3076
  395.6 78.4 %copy-start.244 = (f32[256]{0:T(256)S(1)}, f32[256]{0:T(256)}, u32[]{:S(2)}) copy-start(f32[256]{0:T(256)} %get-tuple-element.75) | copy-start | bytes 3076
  395.6 78.4 %copy-start.241 = (f32[256]{0:T(256)S(1)}, f32[256]{0:T(256)}, u32[]{:S(2)}) copy-start(f32[256]{0:T(256)} %get-tuple-element.100) | copy-start | bytes 3076
  395.6 78.4 %copy-start.243 = (f32[256]{0:T(256)S(1)}, f32[256]{0:T(256)}, u32[]{:S(2)}) copy-start(f32[256]{0:T(256)} %get-tuple-element.99) | copy-start | bytes 3076
  395.7 78.4 %copy-start.197 = (f32[256]{0:T(256)S(1)}, f32[256]{0:T(256)}, u32[]{:S(2)}) copy-start(f32[256]{0:T(256)} %get-tuple-element.149) | copy-start | bytes 3076
  395.7 78.4 %copy-start.202 = (f32[256]{0:T(256)S(1)}, f32[256]{0:T(256)}, u32[]{:S(2)}) copy-start(f32[256]{0:T(256)} %get-tuple-element.147) | copy-start | bytes 3076
  395.7 78.4 %copy-start.205 = (f32[1024]{0:T(1024)S(1)}, f32[1024]{0:T(1024)}, u32[]{:S(2)}) copy-start(f32[1024]{0:T(1024)} %get-tuple-element.270) | copy-start | bytes 12292
  395.7 78.4 %copy-start.206 = (f32[1024]{0:T(1024)S(1)}, f32[1024]{0:T(1024)}, u32[]{:S(2)}) copy-start(f32[1024]{0:T(1024)} %get-tuple-element.272) | copy-start | bytes 12292
  395.7 78.5 %copy-start.9 = (bf16[1216,256]{1,0:T(8,128)(2,1)S(1)}, bf16[1216,256]{1,0:T(8,128)(2,1)}, u32[]{:S(2)}) copy-start(bf16[1216,256]{1,0:T(8,128)(2,1)} %param.16) | copy-start | bytes 1867780
  395.7 78.5 %copy-start.129 = (f32[1216]{0:T(1024)S(1)}, f32[1216]{0:T(1024)}, u32[]{:S(2)}) copy-start(f32[1216]{0:T(1024)} %copy-done.128) | copy-start | bytes 14596
  395.7 78.5 %copy-start.164 = (f32[1,256]{1,0:T(1,128)S(1)}, f32[1,256]{1,0:T(1,128)}, u32[]{:S(2)}) copy-start(f32[1,256]{1,0:T(1,128)} %copy-done.163) | copy-start | bytes 3076
  395.7 80.2 %copy-start.200 = (f32[256]{0:T(256)S(1)}, f32[256]{0:T(256)}, u32[]{:S(2)}) copy-start(f32[256]{0:T(256)} %get-tuple-element.119) | copy-start | bytes 3076
  395.7 80.3 %copy-start.156 = (f32[1216]{0:T(1024)S(1)}, f32[1216]{0:T(1024)}, u32[]{:S(2)}) copy-start(f32[1216]{0:T(1024)} %copy-done.155) | copy-start | bytes 14596
  395.7 80.3 %copy-start.138 = (f32[1216]{0:T(1024)S(1)}, f32[1216]{0:T(1024)}, u32[]{:S(2)}) copy-start(f32[1216]{0:T(1024)} %copy-done.137) | copy-start | bytes 14596
  396.2 81.7 %copy-start.199 = (f32[256]{0:T(256)S(1)}, f32[256]{0:T(256)}, u32[]{:S(2)}) copy-start(f32[256]{0:T(256)} %get-tuple-element.79) | copy-start | bytes 3076
  396.2 119.6 %copy-start.18 = (f32[1216,256]{1,0:T(8,128)S(1)}, f32[1216,256]{1,0:T(8,128)}, u32[]{:S(2)}) copy-start(f32[1216,256]{1,0:T(8,128)} %copy-done.17) | copy-start | bytes 3735556
  396.2 119.6 %copy-start.149 = (f32[1216]{0:T(1024)S(1)}, f32[1216]{0:T(1024)}, u32[]{:S(2)}) copy-start(f32[1216]{0:T(1024)} %copy-done.148) | copy-start | bytes 14596
  (202 other events, 497.4 us)
Sparse Core Ops, SparseCore 0:
  15.9 12.0 all-gather.2
  93.6 10.4 all-gather.4
  272.2 9.8 reduce-scatter.2
  371.6 9.8 reduce-scatter.4
  391.0 111.6 all-reduce.81
  509.7 144.3 all-reduce.83
where the time goes:
time: 674 us; the launch traced here: 669 us
  waiting for transfers between devices  155 us (23%)
  local copies, waits for them, and re-layouts  149 us (22%)
  blocking collectives  133 us (20%)
  matrix products  111 us (16%)
  other arithmetic  102 us (15%)
  between operations  17.8 us (3%)
    psum x1, waiting for transfers between devices, shards(): shared_all = lax.psum(shared_all, ('dp', 'heads'))  136 us
    psum x1, blocking collectives, shards(): group_all = lax.psum(group_all, 'dp')  77.2 us
    psum x1, blocking collectives, shards(): shared_all = lax.psum(shared_all, ('dp', 'heads'))  37.8 us
    dot_general x2, matrix products, forward_block(): hidden = jnp.dot(normed2, w_fc1, preferred_element_type=jnp.float32) + b_fc1  25.9 us
    another operation x8, local copies, waits for them, and re-layouts, attend_backward(): grad_heads = grad.reshape(nwin, span, GH, HD)  21.8 us
    unnamed x525, local copies, waits for them, and re-layouts  19.1 us
    all_gather x2, waiting for transfers between devices, forward_block(): normed = lax.all_gather(normed_rows, 'heads', axis=0, tiled=True)  19 us
    reduce_sum x6, other arithmetic, lepe_apply(): weight[3 * first + second]  15.6 us
  transfers between devices with their start and end apart: 6, of which 4 were waited for; matrix products, arithmetic and copies ran while one was open for 6% of the time, Pallas kernels for 0%

commit v1 on v0

v1 whole, which is shorter than its diff:
```python
import functools
import math

import jax
import jax.numpy as jnp
import numpy as np
from jax import lax
from jax.experimental import pallas as pl
from jax.experimental.pallas import tpu as pltpu
from jax.sharding import PartitionSpec as P

D = 256
FF = 1024
HD = 32
GH = 4
HW = 128
LAYERS = 2
TOK_IMG = 608
SPLIT = 392
EPSILON = 1e-05

QUAD = 56
BLOCK = 2 * QUAD
CHUNK = 2 * BLOCK
IMG = 6 * BLOCK
KEYS = 128
SPAN = GH * KEYS
TAPS = 9
SCALE = HD**-0.5
EXP_SCALE = SCALE * math.log2(math.e)
BF = jnp.bfloat16
F32 = jnp.float32

FC1_AT = 0
FC2_AT = 1024
PROJ_AT = 2048
QKV_AT = 2304
SMALL_AT = 3072
SMALL = 32
PACKED = SMALL_AT + SMALL


def place_table():
    table = np.zeros((IMG, TOK_IMG), np.float32)
    for crop in range(2):
        for quad in range(4):
            for cell in range(49):
                row = (quad // 2) * 7 + cell // 7
                col = (quad % 2) * 7 + cell % 7
                table[crop * 224 + quad * QUAD + cell, crop * 196 + row * 14 + col] = 1
    for group in range(2):
        for cell in range(108):
            table[448 + group * BLOCK + cell, SPLIT + group * 108 + cell] = 1
    return table


def block_cells(kind):
    cells = [None] * BLOCK
    if kind == 2:
        for cell in range(108):
            cells[cell] = (cell // 36, (cell % 36) // 6, cell % 6)
    else:
        for half in range(2):
            for cell in range(49):
                row, col = cell // 7, cell % 7
                shifted = (0, row, col + 7 * half) if kind == 0 else (0, row + 7 * half, col)
                cells[half * QUAD + cell] = shifted
    return cells


def shift_tables():
    wide = np.zeros((3, BLOCK, TAPS * KEYS), np.float32)
    tall = np.zeros((3, TAPS * BLOCK, KEYS), np.float32)
    for kind in range(3):
        cells = block_cells(kind)
        where = {cell: place for place, cell in enumerate(cells) if cell is not None}
        for tap in range(TAPS):
            for place, cell in enumerate(cells):
                if cell is None:
                    continue
                other = where.get((cell[0], cell[1] + tap // 3 - 1, cell[2] + tap % 3 - 1))
                if other is not None:
                    wide[kind, place, tap * KEYS + other] = 1
                    tall[kind, tap * BLOCK + place, other] = 1
    return wide, tall


def bias_table():
    bias = np.full((2, BLOCK, KEYS), -1e30, np.float32)
    bias[0, :, :49] = 0
    bias[0, :, QUAD : QUAD + 49] = 0
    for row in range(BLOCK):
        if row < 108:
            first = 36 * (row // 36)
            bias[1, row, first : first + 36] = 0
        else:
            bias[1, row, :108] = 0
    return bias


def head_table():
    table = np.zeros((SPAN, HW), np.float32)
    for head in range(GH):
        table[head * KEYS : (head + 1) * KEYS, head * HD : (head + 1) * HD] = 1
    return table


def dot(left, right):
    return lax.dot_general(left, right, (((1,), (0,)), ((), ())), preferred_element_type=F32)


def dot_nt(left, right):
    return lax.dot_general(left, right, (((1,), (1,)), ((), ())), preferred_element_type=F32)


def dot_tn(left, right):
    return lax.dot_general(left, right, (((0,), (0,)), ((), ())), preferred_element_type=F32)


def norm_parts(value):
    center = value - jnp.mean(value, axis=-1, keepdims=True)
    scale = lax.rsqrt(jnp.mean(center * center, axis=-1, keepdims=True) + EPSILON)
    return center * scale, scale


def norm_back(dout, value, gain):
    xhat, scale = norm_parts(value)
    grown = dout * gain
    mean = jnp.mean(grown, axis=-1, keepdims=True)
    cross = jnp.mean(grown * xhat, axis=-1, keepdims=True)
    return scale * (grown - mean - xhat * cross), dout * xhat


def fold_rows(value):
    return jnp.sum(value.reshape(value.shape[0] // 8, 8, value.shape[1]), axis=0)


def head_stack(value, heads_ref):
    rows = []
    pad = jnp.zeros((KEYS - BLOCK, HW), BF)
    for head in range(GH):
        rows.append(value * heads_ref[head * KEYS : head * KEYS + 1, :])
        rows.append(pad)
    return jnp.concatenate(rows, axis=0)


def swap_quads(value):
    return jnp.concatenate(
        [value[:QUAD], value[2 * QUAD : 3 * QUAD], value[QUAD : 2 * QUAD], value[3 * QUAD :]], axis=0
    )


def halves(block, direction):
    inside = lax.rem(block, 6)
    first = block * BLOCK
    second = first + QUAD
    if direction == 1:
        crop = (block - lax.rem(inside, 2)) * BLOCK
        large = inside < 4
        first = jnp.where(large, crop + QUAD * lax.rem(inside, 2), first)
        second = jnp.where(large, crop + BLOCK + QUAD * lax.rem(inside, 2), second)
    return pl.multiple_of(first, 8), pl.multiple_of(second, 8)


def tap_row(direction, tap):
    return tap if direction == 0 else 3 * (tap % 3) + tap // 3


def step_kernel(
    meta,
    tok_ref,
    cot_ref,
    g1_ref,
    b1_ref,
    wqkv_ref,
    lepe_ref,
    wproj_ref,
    bproj_ref,
    g2_ref,
    b2_ref,
    wfc1_ref,
    bfc1_ref,
    wfc2_ref,
    bfc2_ref,
    place_ref,
    wide_ref,
    tall_ref,
    bias_ref,
    heads_ref,
    out_ref,
    dtok_ref,
    packed_ref,
    h_ref,
    normed_ref,
    qkv_ref,
    expo_ref,
    mixed_ref,
    hf_ref,
    hb_ref,
    inner_ref,
    normed2_ref,
    act_ref,
    slope_ref,
    dh_ref,
    dz_ref,
    dhid_ref,
    acc_ref,
    accff_ref,
    acclepe_ref,
    small_ref,
    stage_ref,
):
    rows_all = h_ref.shape[1]
    images = rows_all // IMG
    chunks = rows_all // CHUNK
    blocks = rows_all // BLOCK
    parts = packed_ref.shape[1]
    part_rows = packed_ref.shape[3]
    core = meta[0]
    mine = meta[1]

    def chunk_rows(index):
        return pl.ds(pl.multiple_of(index * CHUNK, 16), CHUNK)

    def block_rows(index):
        return pl.ds(pl.multiple_of(index * BLOCK, 16), BLOCK)

    def keep_of(image):
        place = lax.broadcasted_iota(jnp.int32, (IMG, 1), 0)
        limit = meta[2 + image]
        group = (place - 448) // BLOCK
        inside = (place - 448) % BLOCK
        return (place < 448) | (inside < 36 * (limit - 3 * group))

    for image in range(images):
        spot = pl.ds(image * TOK_IMG, TOK_IMG)
        h_ref[0, pl.ds(image * IMG, IMG), :] = dot(place_ref[...], tok_ref[spot, :])

    def forward(layer, carry):
        def project(index, carry):
            rows = chunk_rows(index)
            xhat, _ = norm_parts(h_ref[layer, rows, :])
            normed = xhat * g1_ref[pl.ds(layer, 1), :] + b1_ref[pl.ds(layer, 1), :]
            large = lax.rem(index, 3) < 2
            turned = jnp.where(large, swap_quads(normed), normed)
            for direction, value in enumerate((normed, turned)):
                value = value.astype(BF)
                normed_ref[layer, direction, rows, :] = value
                qkv_ref[layer, direction, rows, :] = dot(value, wqkv_ref[direction, layer]).astype(BF)
            return carry

        lax.fori_loop(0, chunks, project, 0)

        def attend(index, carry):
            rows = block_rows(index)
            large = lax.rem(index, 6) < 4
            bias = bias_ref[jnp.where(large, 0, 1)]
            for direction in range(2):
                kind = jnp.where(large, direction, 2)
                query = qkv_ref[layer, direction, rows, :HW]
                keyset = qkv_ref[layer, direction, rows, HW : 2 * HW]
                values = qkv_ref[layer, direction, rows, 2 * HW :]
                scores = dot_nt(query, head_stack(keyset, heads_ref))
                expo = []
                for head in range(GH):
                    part = scores[:, head * KEYS : (head + 1) * KEYS] + bias
                    top = jnp.max(part, axis=-1, keepdims=True)
                    expo.append(jnp.exp2((part - top) * EXP_SCALE).astype(BF))
                expo = jnp.concatenate(expo, axis=1)
                expo_ref[layer, direction, rows, :] = expo
                both = dot(expo, jnp.concatenate([head_stack(values, heads_ref), heads_ref[...]], axis=1))
                recip = 1.0 / both[:, HW:]
                mixed = both[:, :HW] * recip
                mixed_ref[layer, direction, rows, :] = mixed
                wide_values = jnp.concatenate([values.astype(F32), jnp.zeros((KEYS - BLOCK, HW), F32)], axis=0)
                scaled = [
                    (wide_values * lepe_ref[direction, layer, pl.ds(tap_row(direction, tap), 1), :]).astype(BF)
                    for tap in range(TAPS)
                ]
                local = dot(wide_ref[kind], jnp.concatenate(scaled, axis=0))
                result = mixed + local + lepe_ref[direction, layer, TAPS : TAPS + 1, :]
                first, second = halves(index, direction)
                lanes = slice(direction * HW, (direction + 1) * HW)
                hf_ref[pl.ds(first, QUAD), lanes] = result[:QUAD]
                hf_ref[pl.ds(second, QUAD), lanes] = result[QUAD:]
            return carry

        lax.fori_loop(0, blocks, attend, 0)

        def feed(index, carry):
            rows = chunk_rows(index)
            heads = hf_ref[rows, :].astype(BF)
            hb_ref[layer, rows, :] = heads
            inner = h_ref[layer, rows, :] + dot(heads, wproj_ref[layer]) + bproj_ref[pl.ds(layer, 1), :]
            inner_ref[layer, rows, :] = inner
            xhat, _ = norm_parts(inner)
            normed2 = (xhat * g2_ref[pl.ds(layer, 1), :] + b2_ref[pl.ds(layer, 1), :]).astype(BF)
            normed2_ref[layer, rows, :] = normed2
            hidden = dot(normed2, wfc1_ref[layer]) + bfc1_ref[pl.ds(layer, 1), :]
            cdf = 0.5 + 0.5 * lax.erf(hidden * math.sqrt(0.5))
            act = (hidden * cdf).astype(BF)
            act_ref[layer, rows, :] = act
            slope = cdf + hidden * jnp.exp(-0.5 * hidden * hidden) * (1.0 / math.sqrt(2 * math.pi))
            slope_ref[layer, rows, :] = slope.astype(BF)
            h_ref[layer + 1, rows, :] = inner + dot(act, wfc2_ref[layer]) + bfc2_ref[pl.ds(layer, 1), :]
            return carry

        lax.fori_loop(0, chunks, feed, 0)
        return carry

    lax.fori_loop(0, LAYERS, forward, 0)

    for image in range(images):
        spot = pl.ds(image * TOK_IMG, TOK_IMG)
        wide = pl.ds(image * IMG, IMG)
        keep = keep_of(image)
        result = jnp.where(keep, h_ref[LAYERS, wide, :], 0.0).astype(BF)
        out_ref[spot, :] = dot_tn(place_ref[...], result).astype(BF)
        dh_ref[wide, :] = jnp.where(keep, dot(place_ref[...], cot_ref[spot, :]), 0.0)

    def backward(step, carry):
        layer = LAYERS - 1 - step
        acc_ref[...] = jnp.zeros_like(acc_ref)
        accff_ref[...] = jnp.zeros_like(accff_ref)
        acclepe_ref[...] = jnp.zeros_like(acclepe_ref)

        def feed(index, carry):
            rows = chunk_rows(index)
            grad = dh_ref[rows, :]
            dz = grad.astype(BF)
            dz_ref[rows, :] = dz
            acc_ref[5] += fold_rows(dz.astype(F32))
            dhid = (dot_nt(dz, wfc2_ref[layer]) * slope_ref[layer, rows, :].astype(F32)).astype(BF)
            dhid_ref[rows, :] = dhid
            accff_ref[...] += fold_rows(dhid.astype(F32))
            dnormed = dot_nt(dhid, wfc1_ref[layer])
            dvalue, dgain = norm_back(dnormed, inner_ref[layer, rows, :], g2_ref[pl.ds(layer, 1), :])
            acc_ref[3] += fold_rows(dgain)
            acc_ref[4] += fold_rows(dnormed)
            dinner = grad + dvalue
            dh_ref[rows, :] = dinner
            return carry

        lax.fori_loop(0, chunks, feed, 0)

        def feed_weights(index, carry):
            cols = pl.ds(pl.multiple_of(index * 256, 256), 256)
            half = index // 2
            first = dot_tn(normed2_ref[layer], dhid_ref[:, cols]).astype(BF)
            second = dot_tn(dz_ref[...], act_ref[layer, :, cols]).astype(BF)
            for piece in range(2):
                at = pl.multiple_of((lax.rem(index, 2) * 2 + piece) * 256, 256)
                lanes = slice(piece * HW, (piece + 1) * HW)
                stage_ref[half, pl.ds(FC1_AT + at, 256), :] = first[:, lanes]
                stage_ref[half, pl.ds(FC2_AT + at, 256), :] = second[:, lanes]
            return carry

        lax.fori_loop(0, 4, feed_weights, 0)

        def project(index, carry):
            rows = chunk_rows(index)
            dy = dh_ref[rows, :].astype(BF)
            dz_ref[rows, :] = dy
            acc_ref[2] += fold_rows(dy.astype(F32))
            hf_ref[rows, :] = dot_nt(dy, wproj_ref[layer])
            return carry

        lax.fori_loop(0, chunks, project, 0)
        gproj = dot_tn(hb_ref[layer], dz_ref[...]).astype(BF)
        for half in range(2):
            stage_ref[half, PROJ_AT : PROJ_AT + D, :] = gproj[:, half * HW : (half + 1) * HW]

        def attend(index, carry):
            rows = block_rows(index)
            large = lax.rem(index, 6) < 4
            for direction in range(2):
                kind = jnp.where(large, direction, 2)
                first, second = halves(index, direction)
                lanes = slice(direction * HW, (direction + 1) * HW)
                grad = jnp.concatenate(
                    [hf_ref[pl.ds(first, QUAD), lanes], hf_ref[pl.ds(second, QUAD), lanes]], axis=0
                ).astype(BF)
                grad32 = grad.astype(F32)
                query = qkv_ref[layer, direction, rows, :HW]
                keyset = qkv_ref[layer, direction, rows, HW : 2 * HW]
                values = qkv_ref[layer, direction, rows, 2 * HW :]
                expo = expo_ref[layer, direction, rows, :]
                recip = 1.0 / dot(expo, heads_ref[...])
                inner = grad32 * mixed_ref[layer, direction, rows, :]
                inner_high = inner.astype(BF)
                inner_low = (inner - inner_high.astype(F32)).astype(BF)
                masks = heads_ref[...]
                dprobs = dot_nt(
                    jnp.concatenate([grad, -inner_high, -inner_low], axis=1),
                    jnp.concatenate([head_stack(values, heads_ref), masks, masks], axis=1),
                )
                dscores = (expo.astype(F32) * dprobs).astype(BF)
                dquery = dot(dscores, head_stack(keyset, heads_ref)) * recip * SCALE
                dkeys_all = dot_tn((query.astype(F32) * recip * SCALE).astype(BF), dscores)
                dvalues_all = dot_tn((grad32 * recip).astype(BF), expo)
                dkeys = jnp.concatenate(
                    [
                        dkeys_all[head * HD : (head + 1) * HD, head * KEYS : (head + 1) * KEYS]
                        for head in range(GH)
                    ],
                    axis=0,
                ).T[:BLOCK]
                dvalues = jnp.concatenate(
                    [
                        dvalues_all[head * HD : (head + 1) * HD, head * KEYS : (head + 1) * KEYS]
                        for head in range(GH)
                    ],
                    axis=0,
                ).T[:BLOCK]
                wide_grad = jnp.concatenate([grad32, jnp.zeros((KEYS - BLOCK, HW), F32)], axis=0)
                scaled = [
                    (
                        wide_grad * lepe_ref[direction, layer, pl.ds(tap_row(direction, TAPS - 1 - tap), 1), :]
                    ).astype(BF)
                    for tap in range(TAPS)
                ]
                dvalues = dvalues + dot(wide_ref[kind], jnp.concatenate(scaled, axis=0))
                dhid_ref[rows, direction * 3 * HW : direction * 3 * HW + HW] = dquery.astype(BF)
                dhid_ref[rows, direction * 3 * HW + HW : direction * 3 * HW + 2 * HW] = dkeys.astype(BF)
                dhid_ref[rows, direction * 3 * HW + 2 * HW : direction * 3 * HW + 3 * HW] = dvalues.astype(BF)
                shifted = dot(
                    tall_ref[kind], jnp.concatenate([values, jnp.zeros((KEYS - BLOCK, HW), BF)], axis=0)
                )
                for tap in range(TAPS):
                    acclepe_ref[direction, tap_row(direction, tap)] += fold_rows(
                        grad32 * shifted[tap * BLOCK : (tap + 1) * BLOCK]
                    )
                acclepe_ref[direction, TAPS] += fold_rows(grad32)
            return carry

        lax.fori_loop(0, blocks, attend, 0)

        def normalize(index, carry):
            rows = chunk_rows(index)
            turned = dot_nt(dhid_ref[rows, 3 * HW : 6 * HW], wqkv_ref[1, layer])
            turned = jnp.where(lax.rem(index, 3) < 2, swap_quads(turned), turned)
            dnormed = dot_nt(dhid_ref[rows, : 3 * HW], wqkv_ref[0, layer]) + turned
            dvalue, dgain = norm_back(dnormed, h_ref[layer, rows, :], g1_ref[pl.ds(layer, 1), :])
            acc_ref[0] += fold_rows(dgain)
            acc_ref[1] += fold_rows(dnormed)
            dh_ref[rows, :] = dh_ref[rows, :] + dvalue
            return carry

        lax.fori_loop(0, chunks, normalize, 0)
        small_ref[...] = jnp.zeros_like(small_ref)
        for direction in range(2):
            gqkv = dot_tn(normed_ref[layer, direction], dhid_ref[:, direction * 3 * HW : (direction + 1) * 3 * HW]).astype(BF)
            for piece in range(3):
                at = QKV_AT + 256 * piece
                stage_ref[direction, at : at + 256, :] = gqkv[:, piece * HW : (piece + 1) * HW]
            small_ref[direction, :10, :] = jnp.sum(acclepe_ref[direction], axis=1)
        sums = jnp.sum(acc_ref[...], axis=1)
        for piece in range(2):
            small_ref[0, 10 + 6 * piece : 16 + 6 * piece, :] = sums[:, piece * HW : (piece + 1) * HW]
        sums = jnp.sum(accff_ref[...], axis=0, keepdims=True)
        for piece in range(8):
            small_ref[1, 10 + piece : 11 + piece, :] = sums[:, piece * HW : (piece + 1) * HW]
        stage_ref[:, SMALL_AT:PACKED, :] = small_ref[...].astype(BF)

        for half in range(2):
            slot = jnp.bitwise_xor(core, half)

            def hand_out(part, carry):
                place = digits_reversed(jnp.bitwise_xor(part, mine), parts)
                at = pl.ds(pl.multiple_of(part * part_rows, 16), part_rows)
                packed_ref[slot, place, layer] = stage_ref[half, at, :]
                return carry

            lax.fori_loop(0, parts, hand_out, 0)
        return carry

    stage_ref[:, PACKED:, :] = jnp.zeros((2, stage_ref.shape[1] - PACKED, HW), BF)
    lax.fori_loop(0, LAYERS, backward, 0)

    for image in range(images):
        value = dh_ref[pl.ds(image * IMG, IMG), :]
        high = value.astype(BF)
        low = (value - high.astype(F32)).astype(BF)
        spot = pl.ds(image * TOK_IMG, TOK_IMG)
        dtok_ref[spot, :] = dot_tn(place_ref[...], high) + dot_tn(place_ref[...], low)


def digit_sizes(parts):
    sizes = []
    while parts > 1:
        size = 4 if parts % 4 == 0 else 2
        sizes.append(size)
        parts //= size
    return sizes


def digits_reversed(index, parts):
    place = 0
    for size in digit_sizes(parts):
        place = place * size + lax.rem(index, size)
        index = index // size
    return place


def unpack_kernel(
    meta,
    own_ref,
    other_ref,
    g1_ref,
    b1_ref,
    gqkv_ref,
    glepe_ref,
    glepeb_ref,
    gproj_ref,
    gbproj_ref,
    g2_ref,
    b2_ref,
    gfc1_ref,
    gbfc1_ref,
    gfc2_ref,
    gbfc2_ref,
    stage_ref,
):
    parts = own_ref.shape[0]
    part_rows = own_ref.shape[2]
    core = meta[0]
    mine = meta[1]

    for layer in range(LAYERS):

        def collect(part, carry):
            place = digits_reversed(jnp.bitwise_xor(part, mine), parts)
            at = pl.ds(pl.multiple_of(part * part_rows, 16), part_rows)
            stage_ref[core, at, :] = own_ref[place, layer]
            stage_ref[1 - core, at, :] = other_ref[place, layer]
            return carry

        lax.fori_loop(0, parts, collect, 0)
        for half in range(2):
            for piece in range(4):
                lanes = slice(half * 512 + piece * HW, half * 512 + (piece + 1) * HW)
                at = FC1_AT + 256 * piece
                gfc1_ref[layer, :, lanes] = stage_ref[half, at : at + 256, :].astype(F32)
                at = FC2_AT + 256 * piece
                gfc2_ref[layer, lanes, :] = stage_ref[half, at : at + 256, :].astype(F32).T
            gproj_ref[layer, :, half * HW : (half + 1) * HW] = stage_ref[
                half, PROJ_AT : PROJ_AT + 256, :
            ].astype(F32)
        for piece in range(3):
            at = QKV_AT + 256 * piece
            gqkv_ref[layer, 0, :, piece * HW : (piece + 1) * HW] = stage_ref[core, at : at + 256, :].astype(F32)
        small = stage_ref[core, SMALL_AT:PACKED, :].astype(F32)
        glepe_ref[layer, 0] = small[:TAPS]
        glepeb_ref[layer] = small[TAPS : TAPS + 1]
        small = stage_ref[0, SMALL_AT:PACKED, :].astype(F32)
        for place, ref in enumerate((g1_ref, b1_ref, gbproj_ref, g2_ref, b2_ref, gbfc2_ref)):
            for piece in range(2):
                row = 10 + 6 * piece + place
                ref[layer : layer + 1, piece * HW : (piece + 1) * HW] = small[row : row + 1]
        small = stage_ref[1, SMALL_AT:PACKED, :].astype(F32)
        for piece in range(8):
            gbfc1_ref[layer : layer + 1, piece * HW : (piece + 1) * HW] = small[10 + piece : 11 + piece]


SMEM = pl.BlockSpec(memory_space=pltpu.SMEM)
VMEM = pl.BlockSpec(memory_space=pltpu.VMEM)


def shards(
    dp,
    tokens,
    cotangent,
    counts,
    ln1_gain,
    ln1_bias,
    w_qkv,
    lepe_w,
    lepe_b,
    w_proj,
    b_proj,
    ln2_gain,
    ln2_bias,
    w_fc1,
    b_fc1,
    w_fc2,
    b_fc2,
):
    tokens_here = tokens.shape[0]
    images = tokens_here // TOK_IMG
    rows = images * IMG
    core = lax.axis_index("heads")
    mine = lax.axis_index("dp")
    own_counts = lax.dynamic_slice(counts, (core * images,), (images,))
    meta = jnp.concatenate([jnp.stack([core, mine]).astype(jnp.int32), own_counts])
    wqkv_all = lax.all_gather(w_qkv.reshape(LAYERS, D, 3 * HW), "heads", axis=0)
    lepe = jnp.concatenate([lepe_w[:, 0], lepe_b], axis=1)
    lepe_all = lax.all_gather(lepe, "heads", axis=0)
    part_rows = -(-PACKED // (16 * dp)) * 16
    wide, tall = shift_tables()
    table = place_table()
    scratch = [
        pltpu.VMEM((LAYERS + 1, rows, D), F32),
        pltpu.VMEM((LAYERS, 2, rows, D), BF),
        pltpu.VMEM((LAYERS, 2, rows, 3 * HW), BF),
        pltpu.VMEM((LAYERS, 2, rows, SPAN), BF),
        pltpu.VMEM((LAYERS, 2, rows, HW), F32),
        pltpu.VMEM((rows, D), F32),
        pltpu.VMEM((LAYERS, rows, D), BF),
        pltpu.VMEM((LAYERS, rows, D), F32),
        pltpu.VMEM((LAYERS, rows, D), BF),
        pltpu.VMEM((LAYERS, rows, FF), BF),
        pltpu.VMEM((LAYERS, rows, FF), BF),
        pltpu.VMEM((rows, D), F32),
        pltpu.VMEM((rows, D), BF),
        pltpu.VMEM((rows, FF), BF),
        pltpu.VMEM((6, 8, D), F32),
        pltpu.VMEM((8, FF), F32),
        pltpu.VMEM((2, TAPS + 1, 8, HW), F32),
        pltpu.VMEM((2, SMALL, HW), F32),
        pltpu.VMEM((2, part_rows * dp, HW), BF),
    ]
    result, grad, packed = pl.pallas_call(
        step_kernel,
        out_shape=(
            jax.ShapeDtypeStruct((tokens_here, D), BF),
            jax.ShapeDtypeStruct((tokens_here, D), F32),
            jax.ShapeDtypeStruct((2, dp, LAYERS, part_rows, HW), BF),
        ),
        in_specs=[SMEM] + [VMEM] * 19,
        out_specs=(VMEM,) * 3,
        scratch_shapes=scratch,
        compiler_params=pltpu.CompilerParams(vmem_limit_bytes=60 * 1024 * 1024),
        name="step",
    )(
        meta,
        tokens,
        cotangent,
        ln1_gain,
        ln1_bias,
        wqkv_all,
        lepe_all,
        w_proj,
        b_proj,
        ln2_gain,
        ln2_bias,
        w_fc1,
        b_fc1,
        w_fc2,
        b_fc2,
        jnp.asarray(table, BF),
        jnp.asarray(wide, BF),
        jnp.asarray(tall, BF),
        jnp.asarray(bias_table()),
        jnp.asarray(head_table(), BF),
    )

    def add(first, *rest):
        total = first.astype(F32)
        for item in rest:
            total = total + item.astype(F32)
        return total.astype(BF)

    swap = [(0, 1), (1, 0)]
    own = add(packed[0], lax.ppermute(packed[1], "heads", swap))
    digits = []
    stride = 1
    for size in digit_sizes(dp):
        digits.append((size, stride))
        stride *= size
    for size, stride in digits:
        pieces = own.reshape((size, own.shape[0] // size) + own.shape[1:])
        arrived = [
            lax.ppermute(pieces[step], "dp", [(i, i ^ (step * stride)) for i in range(dp)])
            for step in range(1, size)
        ]
        own = add(pieces[0], *arrived)
    for size, stride in reversed(digits):
        own = jnp.concatenate(
            [own]
            + [
                lax.ppermute(own, "dp", [(i, i ^ (step * stride)) for i in range(dp)])
                for step in range(1, size)
            ],
            axis=0,
        )
    other = lax.ppermute(own, "heads", swap)
    grads = pl.pallas_call(
        unpack_kernel,
        out_shape=(
            jax.ShapeDtypeStruct((LAYERS, D), F32),
            jax.ShapeDtypeStruct((LAYERS, D), F32),
            jax.ShapeDtypeStruct((LAYERS, 1, D, 3 * HW), F32),
            jax.ShapeDtypeStruct((LAYERS, 1, TAPS, HW), F32),
            jax.ShapeDtypeStruct((LAYERS, 1, HW), F32),
            jax.ShapeDtypeStruct((LAYERS, D, D), F32),
            jax.ShapeDtypeStruct((LAYERS, D), F32),
            jax.ShapeDtypeStruct((LAYERS, D), F32),
            jax.ShapeDtypeStruct((LAYERS, D), F32),
            jax.ShapeDtypeStruct((LAYERS, D, FF), F32),
            jax.ShapeDtypeStruct((LAYERS, FF), F32),
            jax.ShapeDtypeStruct((LAYERS, FF, D), F32),
            jax.ShapeDtypeStruct((LAYERS, D), F32),
        ),
        in_specs=[SMEM] + [VMEM] * 2,
        out_specs=(VMEM,) * 13,
        scratch_shapes=[pltpu.VMEM((2, part_rows * dp, HW), BF)],
        compiler_params=pltpu.CompilerParams(vmem_limit_bytes=48 * 1024 * 1024),
        name="unpack",
    )(meta, own, other)
    return (result, grad) + tuple(grads)


def solution(mesh):
    spread = P(("dp", "heads"), None)
    group = (P(None, "heads", None, None), P(None, "heads", None, None), P(None, "heads", None))
    in_specs = (spread, spread, P("dp"), P(), P()) + group + (P(),) * 8
    out_specs = (spread, spread, P(), P()) + group + (P(),) * 8
    return jax.shard_map(
        functools.partial(shards, mesh.shape["dp"]),
        mesh=mesh,
        in_specs=in_specs,
        out_specs=out_specs,
        check_vma=False,
    )
```

time: 674 us -> 200 us (0.30)
  local copies, waits for them, and re-layouts: 149 us -> 4.11 us
  blocking collectives: 133 us -> 8.44 us
  matrix products: 111 us -> 0 us
  Pallas kernels: 0 us -> 106 us
  other arithmetic: 102 us -> 2.06 us
  waiting for transfers between devices: 155 us -> 60.9 us
  between operations: 17.8 us -> 0.76 us
  starting transfers between devices: 0.5 us -> 16.8 us
    psum x2 -> x0, waiting for transfers between devices: 136 us -> none  [the longest x1 136 us: shards(): shared_all = lax.psum(shared_all, ('dp', 'heads'))]
    psum x2 -> x0, blocking collectives: 115 us -> none  [the longest x1 77.2 us: shards(): group_all = lax.psum(group_all, 'dp')]
    dot_general x48 -> x0, matrix products: 111 us -> none  [the longest x2 25.9 us: forward_block(): hidden = jnp.dot(normed2, w_fc1, preferred_element_type=jnp.float32) + b_fc1]
    pallas_call x0 -> x2, Pallas kernels: none -> 106 us  [the longest x1 102 us: shards(): pl.pallas_call(step_kernel, out_shape=(jax.ShapeDtypeStruct((tokens_here,...]
    ppermute x0 -> x14, waiting for transfers between devices: none -> 60.9 us  [the longest x6 29.2 us: shards(): lax.ppermute(pieces[step], 'dp', [(i, i ^ step * stride) for i in range(d...]
    reshape x32 -> x0, local copies, waits for them, and re-layouts: 43.6 us -> none  [the longest x6 13.8 us: attend_forward(): mixed = jnp.einsum('whqk,wkhd->wqhd', probs, values, preferred_element_ty...]
    reduce_sum x27 -> x0, other arithmetic: 37.6 us -> none  [the longest x6 15.6 us: lepe_apply(): weight[3 * first + second]]
    another operation x8 -> x0, local copies, waits for them, and re-layouts: 21.8 us -> none  [attend_backward(): grad_heads = grad.reshape(nwin, span, GH, HD)]
  transfers between devices with their start and end apart: 6 -> 14, of which waited for: 4 -> 12; matrix products, arithmetic and copies ran while one was open for 6% -> 0% of each run, Pallas kernels for 0% -> 0%
where the time goes in v1:
time: 200 us; the launch traced here: 199 us
  Pallas kernels  106 us (53%)
  waiting for transfers between devices  60.9 us (30%)
  starting transfers between devices  16.8 us (8%)
  blocking collectives  8.44 us (4%)
  local copies, waits for them, and re-layouts  4.11 us (2%)
  other arithmetic  2.06 us (1%)
    pallas_call x1, Pallas kernels, shards(): pl.pallas_call(step_kernel, out_shape=(jax.ShapeDtypeStruct((tokens_here,...  102 us
    ppermute x6, waiting for transfers between devices, shards(): lax.ppermute(pieces[step], 'dp', [(i, i ^ step * stride) for i in range(d...  29.2 us
    ppermute x6, waiting for transfers between devices, shards(): lax.ppermute(own, 'dp', [(i, i ^ step * stride) for i in range(dp)])  24.7 us
    ppermute x6, starting transfers between devices, shards(): lax.ppermute(pieces[step], 'dp', [(i, i ^ step * stride) for i in range(d...  8.52 us
    ppermute x6, starting transfers between devices, shards(): lax.ppermute(own, 'dp', [(i, i ^ step * stride) for i in range(dp)])  8.01 us
    all_gather x1, blocking collectives, shards(): wqkv_all = lax.all_gather(w_qkv.reshape(LAYERS, D, 3 * HW), 'heads', axis=0)  6.36 us
    pallas_call x1, Pallas kernels, shards(): pl.pallas_call(unpack_kernel, out_shape=(jax.ShapeDtypeStruct((LAYERS, D)...  4.21 us
  transfers between devices with their start and end apart: 14, of which 12 were waited for; matrix products, arithmetic and copies ran while one was open for 0% of the time, Pallas kernels for 0%

profile of v1, /device:TPU:0, one launch (start us, length us, event | category | flops | bytes accessed | tf_op | source)
XLA Modules:
  0.0 199.5 jit_solution(15262285733276438588)
XLA Ops:
  0.6 0.7 copy.46
  1.4 0.7 pad_maximum_fusion.1
  2.0 2.1 %all-gather.1 = f32[4,10,128]{2,1,0:T(8,128)} all-gather(f32[2,10,128]{2,1,0:T(8,128)S(1)} %copy.43), channel_id=3, replica_groups=mesh['dp'=16,'heads'=2] {'heads'}, dimensions={0}, use_global_device_ids=true | all-gather | bytes 30720 | tf_op jit(solution)/shard_map/all_gather | solution.py:597
  4.1 6.4 %all-gather = bf16[4,1,256,384]{3,2,1,0:T(8,128)(2,1)} all-gather(bf16[2,1,256,384]{3,2,1,0:T(8,128)(2,1)} %param.26), channel_id=2, replica_groups=mesh['dp'=16,'heads'=2] {'heads'}, dimensions={0}, use_global_device_ids=true | all-gather | bytes 1179648 | tf_op jit(solution)/shard_map/all_gather | solution.py:595
  10.5 0.7 dynamic_slice.3
  11.2 0.6 pad_add_fusion.meta
  11.8 102.2 %step.1 = (bf16[1216,256]{1,0:T(8,128)(2,1)}, f32[1216,256]{1,0:T(8,128)}, bf16[2,16,2,208,128]{4,3,2,1,0:T(8,128)(2,1)}) custom-call(s32[4]{0:T(128)} %pad_add_fusion.meta, bf16[1216,256]{1,0:T(8,128)(2,1)} %tok_ref.1, bf16[1216,256]{1,0:T(8,128)(2,1)} %cot_ref.1, f32[2,256]{1,0:T(2,128)} %g1_ref.1, f32[2,256]{1,0:T(2,128)} %b1_ref.1, ...), custom_call_target="tpu_custom_call" | custom-call | tf_op jit(solution)/shard_map/step/pallas_call | solution.py:622
  114.0 0.0 copy-start.1
  114.0 1.7 slice_bitcast_fusion
  115.7 0.3 collective-permute-start
  116.0 3.4 %collective-permute-done = bf16[16,2,208,128]{3,2,1,0:T(8,128)(2,1)S(1)} collective-permute-done((bf16[16,2,208,128]{3,2,1,0:T(8,128)(2,1)S(1)}, bf16[16,2,208,128]{3,2,1,0:T(8,128)(2,1)S(1)}, u32[]{:S(2)}, u32[]{:S(2)}) %collective-permute-start) | collective-permute-done | bytes 1703968 | tf_op jit(solution)/shard_map/ppermute | solution.py:664
  119.4 0.0 copy-done.1
  119.4 0.4 fusion
  119.8 0.1 fusion.1
  119.9 2.7 %collective-permute-start.1 = (bf16[4,2,208,128]{3,2,1,0:T(8,128)(2,1)S(1)}, bf16[4,2,208,128]{3,2,1,0:T(8,128)(2,1)S(1)}, u32[]{:S(2)}, u32[]{:S(2)}) collective-permute-start(bf16[4,2,208,128]{3,2,1,0:T(8,128)(2,1)S(1)} %get-tuple-element.94), channel_id=1, source_target_pairs={{0,2},{2,0},{4,6},{6,4},{8,10},{10,8},{12,14},{14,12},{16,18},{18,... | collective-permute-start | bytes 1277960 | tf_op jit(solution)/shard_map/ppermute | solution.py:673
  122.7 1.5 collective-permute-start.3
  124.1 0.1 collective-permute-start.2
  124.2 9.1 %collective-permute-done.1 = bf16[4,2,208,128]{3,2,1,0:T(8,128)(2,1)S(1)} collective-permute-done((bf16[4,2,208,128]{3,2,1,0:T(8,128)(2,1)S(1)}, bf16[4,2,208,128]{3,2,1,0:T(8,128)(2,1)S(1)}, u32[]{:S(2)}, u32[]{:S(2)}) %collective-permute-start.1) | collective-permute-done | bytes 426016 | tf_op jit(solution)/shard_map/ppermute | solution.py:673
  133.3 10.1 %collective-permute-done.3 = bf16[4,2,208,128]{3,2,1,0:T(8,128)(2,1)S(1)} collective-permute-done((bf16[4,2,208,128]{3,2,1,0:T(8,128)(2,1)S(1)}, bf16[4,2,208,128]{3,2,1,0:T(8,128)(2,1)S(1)}, u32[]{:S(2)}, u32[]{:S(2)}) %collective-permute-start.3) | collective-permute-done | bytes 426016 | tf_op jit(solution)/shard_map/ppermute | solution.py:673
  143.4 1.4 collective-permute-done.2
  144.8 0.2 add_convert_fusion
  145.0 1.6 collective-permute-start.4
  146.7 2.5 %collective-permute-start.6 = (bf16[1,2,208,128]{3,2,1,0:T(8,128)(2,1)S(1)}, bf16[1,2,208,128]{3,2,1,0:T(8,128)(2,1)S(1)}, u32[]{:S(2)}, u32[]{:S(2)}) collective-permute-start(bf16[1,2,208,128]{3,2,1,0:T(8,128)(2,1)S(1)} %get-tuple-element.98), channel_id=1, source_target_pairs={{0,24},{2,26},{4,28},{6,30},{8,16},{10,18},{12,20},{14,22},{16,8},... | collective-permute-start | bytes 319496 | tf_op jit(solution)/shard_map/ppermute | solution.py:673
  149.2 0.1 collective-permute-start.5
  149.3 0.6 collective-permute-done.4
  149.9 4.5 %collective-permute-done.6 = bf16[1,2,208,128]{3,2,1,0:T(8,128)(2,1)S(1)} collective-permute-done((bf16[1,2,208,128]{3,2,1,0:T(8,128)(2,1)S(1)}, bf16[1,2,208,128]{3,2,1,0:T(8,128)(2,1)S(1)}, u32[]{:S(2)}, u32[]{:S(2)}) %collective-permute-start.6) | collective-permute-done | bytes 106528 | tf_op jit(solution)/shard_map/ppermute | solution.py:673
  154.4 3.5 %collective-permute-done.5 = bf16[1,2,208,128]{3,2,1,0:T(8,128)(2,1)S(1)} collective-permute-done((bf16[1,2,208,128]{3,2,1,0:T(8,128)(2,1)S(1)}, bf16[1,2,208,128]{3,2,1,0:T(8,128)(2,1)S(1)}, u32[]{:S(2)}, u32[]{:S(2)}) %collective-permute-start.5) | collective-permute-done | bytes 106528 | tf_op jit(solution)/shard_map/ppermute | solution.py:673
  157.9 0.1 constant_dynamic-update-slice_fusion.6
  158.0 3.2 %collective-permute-start.9 = (bf16[1,2,208,128]{3,2,1,0:T(8,128)(2,1)S(1)}, bf16[1,2,208,128]{3,2,1,0:T(8,128)(2,1)S(1)}, u32[]{:S(2)}, u32[]{:S(2)}) collective-permute-start(bf16[1,2,208,128]{3,2,1,0:T(8,128)(2,1)S(1)} %get-tuple-element.93), channel_id=1, source_target_pairs={{0,24},{2,26},{4,28},{6,30},{8,16},{10,18},{12,20},{14,22},{16,8},... | collective-permute-start | bytes 319496 | tf_op jit(solution)/shard_map/ppermute | solution.py:681
  161.2 0.0 collective-permute-start.8
  161.2 1.2 collective-permute-start.7
  162.4 3.3 %collective-permute-done.9 = bf16[1,2,208,128]{3,2,1,0:T(8,128)(2,1)S(1)} collective-permute-done((bf16[1,2,208,128]{3,2,1,0:T(8,128)(2,1)S(1)}, bf16[1,2,208,128]{3,2,1,0:T(8,128)(2,1)S(1)}, u32[]{:S(2)}, u32[]{:S(2)}) %collective-permute-start.9) | collective-permute-done | bytes 106528 | tf_op jit(solution)/shard_map/ppermute | solution.py:681
  165.7 3.6 %collective-permute-done.8 = bf16[1,2,208,128]{3,2,1,0:T(8,128)(2,1)S(1)} collective-permute-done((bf16[1,2,208,128]{3,2,1,0:T(8,128)(2,1)S(1)}, bf16[1,2,208,128]{3,2,1,0:T(8,128)(2,1)S(1)}, u32[]{:S(2)}, u32[]{:S(2)}) %collective-permute-start.8) | collective-permute-done | bytes 106528 | tf_op jit(solution)/shard_map/ppermute | solution.py:681
  169.3 0.0 collective-permute-done.7
  169.3 0.1 pad_maximum_fusion
  169.4 0.0 copy-start
  169.4 1.6 collective-permute-start.10
  171.0 0.5 collective-permute-start.12
  171.4 1.5 collective-permute-start.11
  173.0 9.2 %collective-permute-done.10 = bf16[4,2,208,128]{3,2,1,0:T(8,128)(2,1)S(1)} collective-permute-done((bf16[4,2,208,128]{3,2,1,0:T(8,128)(2,1)S(1)}, bf16[4,2,208,128]{3,2,1,0:T(8,128)(2,1)S(1)}, u32[]{:S(2)}, u32[]{:S(2)}) %collective-permute-start.10) | collective-permute-done | bytes 426016 | tf_op jit(solution)/shard_map/ppermute | solution.py:681
  182.2 0.1 constant_dynamic-update-slice_fusion.2
  182.3 8.6 %collective-permute-done.11 = bf16[4,2,208,128]{3,2,1,0:T(8,128)(2,1)S(1)} collective-permute-done((bf16[4,2,208,128]{3,2,1,0:T(8,128)(2,1)S(1)}, bf16[4,2,208,128]{3,2,1,0:T(8,128)(2,1)S(1)}, u32[]{:S(2)}, u32[]{:S(2)}) %collective-permute-start.11) | collective-permute-done | bytes 426016 | tf_op jit(solution)/shard_map/ppermute | solution.py:681
  190.9 0.1 constant_dynamic-update-slice_fusion.1
  190.9 0.0 collective-permute-done.12
  190.9 0.1 constant_dynamic-update-slice_fusion.own_ref
  191.0 0.1 collective-permute-start.13
  191.1 3.6 %collective-permute-done.13.other_ref = bf16[16,2,208,128]{3,2,1,0:T(8,128)(2,1)S(1)} collective-permute-done((bf16[16,2,208,128]{3,2,1,0:T(8,128)(2,1)S(1)}, bf16[16,2,208,128]{3,2,1,0:T(8,128)(2,1)S(1)}, u32[]{:S(2)}, u32[]{:S(2)}) %collective-permute-start.13) | collective-permute-done | bytes 1703968 | tf_op jit(solution)/shard_map/ppermute | solution.py:686
  194.7 0.0 copy-done
  194.7 4.2 %unpack.1 = (f32[2,256]{1,0:T(2,128)}, f32[2,256]{1,0:T(2,128)}, f32[2,1,256,384]{3,2,1,0:T(8,128)}, f32[2,1,9,128]{3,2,1,0:T(8,128)S(1)}, f32[2,1,128]{2,1,0:T(...) custom-call(s32[4]{0:T(128)S(1)} %copy-done, ...), custom_call_target="tpu_custom_call" | custom-call | tf_op jit(solution)/shard_map/unpack/pallas_call | solution.py:687
  198.9 0.6 copy.44
  (5 shorter events, 0.1 us)
Async XLA Ops:
  114.0 5.4 %copy-start.1 = (bf16[2,16,2,208,128]{4,3,2,1,0:T(8,128)(2,1)S(1)}, bf16[2,16,2,208,128]{4,3,2,1,0:T(8,128)(2,1)}, u32[]{:S(2)}) copy-start(bf16[2,16,2,208,128]{4,3,2,1,0:T(8,128)(2,1)} %get-tuple-element.33) | copy-start | bytes 10223620
  115.7 3.7 %collective-permute-start = (bf16[16,2,208,128]{3,2,1,0:T(8,128)(2,1)S(1)}, bf16[16,2,208,128]{3,2,1,0:T(8,128)(2,1)S(1)}, u32[]{:S(2)}, u32[]{:S(2)}) collective-permute-start(bf16[16,2,208,128]{3,2,1,0:T(8,128)(2,1)S(1)} %slice_bitcast_fusion), channel_id=1, source_target_pairs={{0,1},{1,0},{2,3},{3,2},{4,5},{5,4},{6,7},{7,6},{8,9},{9,8},{10,11... | collective-permute-start | bytes 5111816 | tf_op jit(solution)/shard_map/ppermute | solution.py:664
  119.9 13.4 %collective-permute-start.1 = (bf16[4,2,208,128]{3,2,1,0:T(8,128)(2,1)S(1)}, bf16[4,2,208,128]{3,2,1,0:T(8,128)(2,1)S(1)}, u32[]{:S(2)}, u32[]{:S(2)}) collective-permute-start(bf16[4,2,208,128]{3,2,1,0:T(8,128)(2,1)S(1)} %get-tuple-element.94), channel_id=1, source_target_pairs={{0,2},{2,0},{4,6},{6,4},{8,10},{10,8},{12,14},{14,12},{16,18},{18,... | collective-permute-start | bytes 1277960 | tf_op jit(solution)/shard_map/ppermute | solution.py:673
  122.7 20.8 %collective-permute-start.3 = (bf16[4,2,208,128]{3,2,1,0:T(8,128)(2,1)S(1)}, bf16[4,2,208,128]{3,2,1,0:T(8,128)(2,1)S(1)}, u32[]{:S(2)}, u32[]{:S(2)}) collective-permute-start(bf16[4,2,208,128]{3,2,1,0:T(8,128)(2,1)S(1)} %get-tuple-element.95), channel_id=1, source_target_pairs={{0,6},{2,4},{4,2},{6,0},{8,14},{10,12},{12,10},{14,8},{16,22},{18,... | collective-permute-start | bytes 1277960 | tf_op jit(solution)/shard_map/ppermute | solution.py:673
  124.1 20.6 %collective-permute-start.2 = (bf16[4,2,208,128]{3,2,1,0:T(8,128)(2,1)S(1)}, bf16[4,2,208,128]{3,2,1,0:T(8,128)(2,1)S(1)}, u32[]{:S(2)}, u32[]{:S(2)}) collective-permute-start(bf16[4,2,208,128]{3,2,1,0:T(8,128)(2,1)S(1)} %get-tuple-element.96), channel_id=1, source_target_pairs={{0,4},{2,6},{4,0},{6,2},{8,12},{10,14},{12,8},{14,10},{16,20},{18,... | collective-permute-start | bytes 1277960 | tf_op jit(solution)/shard_map/ppermute | solution.py:673
  145.0 4.9 %collective-permute-start.4 = (bf16[1,2,208,128]{3,2,1,0:T(8,128)(2,1)S(1)}, bf16[1,2,208,128]{3,2,1,0:T(8,128)(2,1)S(1)}, u32[]{:S(2)}, u32[]{:S(2)}) collective-permute-start(bf16[1,2,208,128]{3,2,1,0:T(8,128)(2,1)S(1)} %get-tuple-element.97), channel_id=1, source_target_pairs={{0,8},{2,10},{4,12},{6,14},{8,0},{10,2},{12,4},{14,6},{16,24},{18,... | collective-permute-start | bytes 319496 | tf_op jit(solution)/shard_map/ppermute | solution.py:673
  146.7 7.7 %collective-permute-start.6 = (bf16[1,2,208,128]{3,2,1,0:T(8,128)(2,1)S(1)}, bf16[1,2,208,128]{3,2,1,0:T(8,128)(2,1)S(1)}, u32[]{:S(2)}, u32[]{:S(2)}) collective-permute-start(bf16[1,2,208,128]{3,2,1,0:T(8,128)(2,1)S(1)} %get-tuple-element.98), channel_id=1, source_target_pairs={{0,24},{2,26},{4,28},{6,30},{8,16},{10,18},{12,20},{14,22},{16,8},... | collective-permute-start | bytes 319496 | tf_op jit(solution)/shard_map/ppermute | solution.py:673
  149.2 8.7 %collective-permute-start.5 = (bf16[1,2,208,128]{3,2,1,0:T(8,128)(2,1)S(1)}, bf16[1,2,208,128]{3,2,1,0:T(8,128)(2,1)S(1)}, u32[]{:S(2)}, u32[]{:S(2)}) collective-permute-start(bf16[1,2,208,128]{3,2,1,0:T(8,128)(2,1)S(1)} %get-tuple-element.99), channel_id=1, source_target_pairs={{0,16},{2,18},{4,20},{6,22},{8,24},{10,26},{12,28},{14,30},{16,0},... | collective-permute-start | bytes 319496 | tf_op jit(solution)/shard_map/ppermute | solution.py:673
  158.0 7.8 %collective-permute-start.9 = (bf16[1,2,208,128]{3,2,1,0:T(8,128)(2,1)S(1)}, bf16[1,2,208,128]{3,2,1,0:T(8,128)(2,1)S(1)}, u32[]{:S(2)}, u32[]{:S(2)}) collective-permute-start(bf16[1,2,208,128]{3,2,1,0:T(8,128)(2,1)S(1)} %get-tuple-element.93), channel_id=1, source_target_pairs={{0,24},{2,26},{4,28},{6,30},{8,16},{10,18},{12,20},{14,22},{16,8},... | collective-permute-start | bytes 319496 | tf_op jit(solution)/shard_map/ppermute | solution.py:681
  161.2 8.2 %collective-permute-start.8 = (bf16[1,2,208,128]{3,2,1,0:T(8,128)(2,1)S(1)}, bf16[1,2,208,128]{3,2,1,0:T(8,128)(2,1)S(1)}, u32[]{:S(2)}, u32[]{:S(2)}) collective-permute-start(bf16[1,2,208,128]{3,2,1,0:T(8,128)(2,1)S(1)} %get-tuple-element.93), channel_id=1, source_target_pairs={{0,16},{2,18},{4,20},{6,22},{8,24},{10,26},{12,28},{14,30},{16,0},... | collective-permute-start | bytes 319496 | tf_op jit(solution)/shard_map/ppermute | solution.py:681
  161.2 8.2 %collective-permute-start.7 = (bf16[1,2,208,128]{3,2,1,0:T(8,128)(2,1)S(1)}, bf16[1,2,208,128]{3,2,1,0:T(8,128)(2,1)S(1)}, u32[]{:S(2)}, u32[]{:S(2)}) collective-permute-start(bf16[1,2,208,128]{3,2,1,0:T(8,128)(2,1)S(1)} %get-tuple-element.93), channel_id=1, source_target_pairs={{0,8},{2,10},{4,12},{6,14},{8,0},{10,2},{12,4},{14,6},{16,24},{18,... | collective-permute-start | bytes 319496 | tf_op jit(solution)/shard_map/ppermute | solution.py:681
  169.4 25.3 %copy-start = (s32[4]{0:T(128)S(1)}, s32[4]{0:T(128)}, u32[]{:S(2)}) copy-start(s32[4]{0:T(128)} %pad_add_fusion.meta) | copy-start | bytes 52
  169.4 12.8 %collective-permute-start.10 = (bf16[4,2,208,128]{3,2,1,0:T(8,128)(2,1)S(1)}, bf16[4,2,208,128]{3,2,1,0:T(8,128)(2,1)S(1)}, u32[]{:S(2)}, u32[]{:S(2)}) collective-permute-start(bf16[4,2,208,128]{3,2,1,0:T(8,128)(2,1)S(1)} %pad_maximum_fusion), channel_id=1, source_target_pairs={{0,2},{2,0},{4,6},{6,4},{8,10},{10,8},{12,14},{14,12},{16,18},{18,... | collective-permute-start | bytes 1277960 | tf_op jit(solution)/shard_map/ppermute | solution.py:681
  171.0 20.0 %collective-permute-start.12 = (bf16[4,2,208,128]{3,2,1,0:T(8,128)(2,1)S(1)}, bf16[4,2,208,128]{3,2,1,0:T(8,128)(2,1)S(1)}, u32[]{:S(2)}, u32[]{:S(2)}) collective-permute-start(bf16[4,2,208,128]{3,2,1,0:T(8,128)(2,1)S(1)} %pad_maximum_fusion), channel_id=1, source_target_pairs={{0,6},{2,4},{4,2},{6,0},{8,14},{10,12},{12,10},{14,8},{16,22},{18,... | collective-permute-start | bytes 1277960 | tf_op jit(solution)/shard_map/ppermute | solution.py:681
  171.4 19.4 %collective-permute-start.11 = (bf16[4,2,208,128]{3,2,1,0:T(8,128)(2,1)S(1)}, bf16[4,2,208,128]{3,2,1,0:T(8,128)(2,1)S(1)}, u32[]{:S(2)}, u32[]{:S(2)}) collective-permute-start(bf16[4,2,208,128]{3,2,1,0:T(8,128)(2,1)S(1)} %pad_maximum_fusion), channel_id=1, source_target_pairs={{0,4},{2,6},{4,0},{6,2},{8,12},{10,14},{12,8},{14,10},{16,20},{18,... | collective-permute-start | bytes 1277960 | tf_op jit(solution)/shard_map/ppermute | solution.py:681
  191.0 3.7 %collective-permute-start.13 = (bf16[16,2,208,128]{3,2,1,0:T(8,128)(2,1)S(1)}, bf16[16,2,208,128]{3,2,1,0:T(8,128)(2,1)S(1)}, u32[]{:S(2)}, u32[]{:S(2)}) collective-permute-start(bf16[16,2,208,128]{3,2,1,0:T(8,128)(2,1)S(1)} %constant_dynamic-update-slice_fusion.own_ref), channel_id=1, source_target_pairs={{0,1},{1,0},{2,3},{3,2},{4,5},{5,4},{6,7},{7,6},{8,9},{9,8},{10,11... | collective-permute-start | bytes 5111816 | tf_op jit(solution)/shard_map/ppermute | solution.py:686

commit v2 on v1

--- a/solution.py
+++ b/solution.py
@@ -19,8 +19,9 @@
 SPLIT = 392
 EPSILON = 1e-05
 
-QUAD = 56
-BLOCK = 2 * QUAD
+TILE = 8
+TILES = 14
+BLOCK = TILES * TILE
 CHUNK = 2 * BLOCK
 IMG = 6 * BLOCK
 KEYS = 128
@@ -43,58 +44,35 @@
 def place_table():
     table = np.zeros((IMG, TOK_IMG), np.float32)
     for crop in range(2):
-        for quad in range(4):
-            for cell in range(49):
-                row = (quad // 2) * 7 + cell // 7
-                col = (quad % 2) * 7 + cell % 7
-                table[crop * 224 + quad * QUAD + cell, crop * 196 + row * 14 + col] = 1
+        for row in range(14):
+            for col in range(14):
+                place = crop * CHUNK + row * 16 + (col // 7) * TILE + col % 7
+                table[place, crop * 196 + row * 14 + col] = 1
     for group in range(2):
         for cell in range(108):
-            table[448 + group * BLOCK + cell, SPLIT + group * 108 + cell] = 1
+            table[2 * CHUNK + group * BLOCK + cell, SPLIT + group * 108 + cell] = 1
     return table
 
 
-def block_cells(kind):
-    cells = [None] * BLOCK
-    if kind == 2:
-        for cell in range(108):
-            cells[cell] = (cell // 36, (cell % 36) // 6, cell % 6)
-    else:
-        for half in range(2):
-            for cell in range(49):
-                row, col = cell // 7, cell % 7
-                shifted = (0, row, col + 7 * half) if kind == 0 else (0, row + 7 * half, col)
-                cells[half * QUAD + cell] = shifted
-    return cells
-
-
 def shift_tables():
-    wide = np.zeros((3, BLOCK, TAPS * KEYS), np.float32)
-    tall = np.zeros((3, TAPS * BLOCK, KEYS), np.float32)
-    for kind in range(3):
-        cells = block_cells(kind)
-        where = {cell: place for place, cell in enumerate(cells) if cell is not None}
+    wide = np.zeros((BLOCK, TAPS * KEYS), np.float32)
+    tall = np.zeros((TAPS * BLOCK, KEYS), np.float32)
+    for cell in range(108):
         for tap in range(TAPS):
-            for place, cell in enumerate(cells):
-                if cell is None:
-                    continue
-                other = where.get((cell[0], cell[1] + tap // 3 - 1, cell[2] + tap % 3 - 1))
-                if other is not None:
-                    wide[kind, place, tap * KEYS + other] = 1
-                    tall[kind, tap * BLOCK + place, other] = 1
+            row, col = (cell % 36) // 6 + tap // 3 - 1, cell % 6 + tap % 3 - 1
+            if 0 <= row < 6 and 0 <= col < 6:
+                other = 36 * (cell // 36) + 6 * row + col
+                wide[cell, tap * KEYS + other] = 1
+                tall[tap * BLOCK + cell, other] = 1
     return wide, tall
 
 
 def bias_table():
     bias = np.full((2, BLOCK, KEYS), -1e30, np.float32)
-    bias[0, :, :49] = 0
-    bias[0, :, QUAD : QUAD + 49] = 0
-    for row in range(BLOCK):
-        if row < 108:
-            first = 36 * (row // 36)
-            bias[1, row, first : first + 36] = 0
-        else:
-            bias[1, row, :108] = 0
+    bias[0, [key for key in range(BLOCK) if key % TILE < 7]] = 0
+    for query in range(KEYS):
+        first, last = (36 * (query // 36), 36 * (query // 36) + 36) if query < 108 else (0, 108)
+        bias[1, first:last, query] = 0
     return bias
 
 
@@ -133,6 +111,12 @@
 
 def fold_rows(value):
     return jnp.sum(value.reshape(value.shape[0] // 8, 8, value.shape[1]), axis=0)
+
+
+def head_rows(value, heads_ref):
+    return jnp.concatenate(
+        [value * heads_ref[head * KEYS : head * KEYS + 1, :] for head in range(GH)], axis=0
+    )
 
 
 def head_stack(value, heads_ref):
@@ -144,22 +128,65 @@
     return jnp.concatenate(rows, axis=0)
 
 
-def swap_quads(value):
+def pad_keys(value):
+    return jnp.concatenate([value, jnp.zeros((KEYS - BLOCK, value.shape[1]), value.dtype)], axis=0)
+
+
+def pipeline(stages, items):
+    results = [None] * len(items)
+    for step in range(len(items) + len(stages) - 1):
+        for place in range(len(stages)):
+            item = step - place
+            if 0 <= item < len(items):
+                results[item] = stages[place](items[item], results[item])
+    return results
+
+
+def split_tiles(value):
+    rows = value.shape[0] // 16
     return jnp.concatenate(
-        [value[:QUAD], value[2 * QUAD : 3 * QUAD], value[QUAD : 2 * QUAD], value[3 * QUAD :]], axis=0
+        [value[16 * row : 16 * row + 8] for row in range(rows)]
+        + [value[16 * row + 8 : 16 * row + 16] for row in range(rows)],
+        axis=0,
     )
 
 
-def halves(block, direction):
-    inside = lax.rem(block, 6)
-    first = block * BLOCK
-    second = first + QUAD
+def join_tiles(value):
+    half = value.shape[0] // 2
+    pieces = []
+    for row in range(half // 8):
+        pieces.append(value[8 * row : 8 * row + 8])
+        pieces.append(value[half + 8 * row : half + 8 * row + 8])
+    return jnp.concatenate(pieces, axis=0)
+
+
+def as_tiles(value):
+    return value.reshape(TILES, TILE, HW)
+
+
+def live_tiles():
+    return lax.broadcasted_iota(jnp.int32, (1, TILE, HW), 1) < TILE - 1
+
+
+def side_cells(tiles, direction):
     if direction == 1:
-        crop = (block - lax.rem(inside, 2)) * BLOCK
-        large = inside < 4
-        first = jnp.where(large, crop + QUAD * lax.rem(inside, 2), first)
-        second = jnp.where(large, crop + BLOCK + QUAD * lax.rem(inside, 2), second)
-    return pl.multiple_of(first, 8), pl.multiple_of(second, 8)
+        return pltpu.roll(tiles, 1, 1), tiles, pltpu.roll(tiles, TILE - 1, 1)
+    last = lax.broadcasted_iota(jnp.int32, (1, TILE, HW), 1) == TILE - 1
+    left, right = [], []
+    for row in range(TILES // 2):
+        near, far = tiles[2 * row : 2 * row + 1], tiles[2 * row + 1 : 2 * row + 2]
+        near_left = pltpu.roll(near, 1, 1)
+        far_right = pltpu.roll(far, TILE - 1, 1)
+        left += [near_left, pltpu.roll(jnp.where(last, near_left, far), 1, 1)]
+        right += [pltpu.roll(jnp.where(last, far_right, near), TILE - 1, 1), far_right]
+    return jnp.concatenate(left, axis=0), tiles, jnp.concatenate(right, axis=0)
+
+
+def tap_cells(tiles, direction):
+    stride = 2 if direction == 0 else 1
+    zeros = jnp.zeros((stride, TILE, HW), F32)
+    padded = [jnp.concatenate([zeros, side, zeros], axis=0) for side in side_cells(tiles, direction)]
+    return [padded[tap % 3][(tap // 3) * stride : (tap // 3) * stride + TILES] for tap in range(TAPS)]
 
 
 def tap_row(direction, tap):
@@ -193,8 +220,7 @@
     h_ref,
     normed_ref,
     qkv_ref,
-    expo_ref,
-    mixed_ref,
+    probs_ref,
     hf_ref,
     hb_ref,
     inner_ref,
@@ -222,6 +248,9 @@
     def chunk_rows(index):
         return pl.ds(pl.multiple_of(index * CHUNK, 16), CHUNK)
 
+    def chunk_tiles(index):
+        return pl.ds(index * TILES, TILES)
+
     def block_rows(index):
         return pl.ds(pl.multiple_of(index * BLOCK, 16), BLOCK)
 
@@ -242,54 +271,99 @@
             xhat, _ = norm_parts(h_ref[layer, rows, :])
             normed = xhat * g1_ref[pl.ds(layer, 1), :] + b1_ref[pl.ds(layer, 1), :]
             large = lax.rem(index, 3) < 2
-            turned = jnp.where(large, swap_quads(normed), normed)
+            turned = jnp.where(large, split_tiles(normed), normed)
             for direction, value in enumerate((normed, turned)):
                 value = value.astype(BF)
                 normed_ref[layer, direction, rows, :] = value
                 qkv_ref[layer, direction, rows, :] = dot(value, wqkv_ref[direction, layer]).astype(BF)
             return carry
 
-        lax.fori_loop(0, chunks, project, 0)
-
-        def attend(index, carry):
-            rows = block_rows(index)
-            large = lax.rem(index, 6) < 4
-            bias = bias_ref[jnp.where(large, 0, 1)]
-            for direction in range(2):
-                kind = jnp.where(large, direction, 2)
-                query = qkv_ref[layer, direction, rows, :HW]
-                keyset = qkv_ref[layer, direction, rows, HW : 2 * HW]
-                values = qkv_ref[layer, direction, rows, 2 * HW :]
-                scores = dot_nt(query, head_stack(keyset, heads_ref))
-                expo = []
-                for head in range(GH):
-                    part = scores[:, head * KEYS : (head + 1) * KEYS] + bias
-                    top = jnp.max(part, axis=-1, keepdims=True)
-                    expo.append(jnp.exp2((part - top) * EXP_SCALE).astype(BF))
-                expo = jnp.concatenate(expo, axis=1)
-                expo_ref[layer, direction, rows, :] = expo
-                both = dot(expo, jnp.concatenate([head_stack(values, heads_ref), heads_ref[...]], axis=1))
-                recip = 1.0 / both[:, HW:]
-                mixed = both[:, :HW] * recip
-                mixed_ref[layer, direction, rows, :] = mixed
-                wide_values = jnp.concatenate([values.astype(F32), jnp.zeros((KEYS - BLOCK, HW), F32)], axis=0)
-                scaled = [
-                    (wide_values * lepe_ref[direction, layer, pl.ds(tap_row(direction, tap), 1), :]).astype(BF)
-                    for tap in range(TAPS)
-                ]
-                local = dot(wide_ref[kind], jnp.concatenate(scaled, axis=0))
-                result = mixed + local + lepe_ref[direction, layer, TAPS : TAPS + 1, :]
-                first, second = halves(index, direction)
-                lanes = slice(direction * HW, (direction + 1) * HW)
-                hf_ref[pl.ds(first, QUAD), lanes] = result[:QUAD]
-                hf_ref[pl.ds(second, QUAD), lanes] = result[QUAD:]
-            return carry
-
-        lax.fori_loop(0, blocks, attend, 0)
+        lax.fori_loop(0, chunks, project, 0, unroll=2)
+
+        def tap_weight(direction, tap):
+            return lepe_ref[direction, layer, pl.ds(tap_row(direction, tap), 1), :]
+
+        def score(window, _):
+            direction, rows, _, _ = window
+            query = qkv_ref[layer, direction, rows, :HW]
+            keyset = qkv_ref[layer, direction, rows, HW : 2 * HW]
+            return dot_nt(head_rows(keyset, heads_ref), pad_keys(query))
+
+        def weigh(window, scores):
+            direction, rows, bias, _ = window
+            probs = []
+            for head in range(GH):
+                part = scores[head * BLOCK : (head + 1) * BLOCK] + bias
+                part = jnp.exp2((part - jnp.max(part, axis=0, keepdims=True)) * EXP_SCALE)
+                part = part * (1.0 / jnp.sum(part, axis=0, keepdims=True))
+                probs.append(part.astype(BF))
+                probs_ref[layer, direction, rows, head * KEYS : (head + 1) * KEYS] = probs[head]
+            return probs
+
+        def mix(window, probs):
+            direction, rows, _, _ = window
+            values = qkv_ref[layer, direction, rows, 2 * HW :]
+            side = values.T
+            mixed = [dot(side[head * HD : (head + 1) * HD], probs[head]) for head in range(GH)]
+            return jnp.concatenate(mixed, axis=0)
+
+        def finish(window, mixed):
+            direction, rows, _, block = window
+            values = qkv_ref[layer, direction, rows, 2 * HW :].astype(F32)
+            mixed = mixed.T[:BLOCK] + lepe_ref[direction, layer, TAPS : TAPS + 1, :]
+            if block is None:
+                return mixed, values
+            tiles = jnp.where(live_tiles(), as_tiles(values), 0.0)
+            result = as_tiles(mixed)
+            for tap, cells in enumerate(tap_cells(tiles, direction)):
+                result = result + cells * tap_weight(direction, tap).reshape(1, 1, HW)
+            lanes = slice(direction * HW, (direction + 1) * HW)
+            if direction == 0:
+                hf_ref[pl.ds(block * 7, 7), :, :, lanes] = result.reshape(7, 2, TILE, HW)
+            else:
+                side = lax.rem(block, 2)
+                hf_ref[pl.ds((block - side) * 7, TILES), side, :, lanes] = result
+            return None
+
+        stages = (score, weigh, mix, finish)
+
+        def attend_large(index, carry):
+            windows = []
+            for part in range(2):
+                block = 6 * (index // 2) + 2 * lax.rem(index, 2) + part
+                windows += [(direction, block_rows(block), bias_ref[0], block) for direction in range(2)]
+            pipeline(stages, windows)
+            return carry
+
+        lax.fori_loop(0, images * 2, attend_large, 0)
+
+        def attend_small(index, carry):
+            windows = []
+            for part in range(2):
+                rows = block_rows(6 * index + 4 + part)
+                windows += [(direction, rows, bias_ref[1], None) for direction in range(2)]
+            results = pipeline(stages, windows)
+            for part in range(2):
+                mixed, scaled = [], []
+                for direction in range(2):
+                    some, values = results[2 * part + direction]
+                    mixed.append(some)
+                    padded = pad_keys(values)
+                    scaled.append(
+                        jnp.concatenate(
+                            [(padded * tap_weight(direction, tap)).astype(BF) for tap in range(TAPS)], axis=0
+                        )
+                    )
+                local = dot(wide_ref[...], jnp.concatenate(scaled, axis=1))
+                result = jnp.concatenate(mixed, axis=1) + local
+                hf_ref[pl.ds((6 * index + 4 + part) * 7, 7)] = result.reshape(7, 2, TILE, D)
+            return carry
+
+        lax.fori_loop(0, images, attend_small, 0)
 
         def feed(index, carry):
             rows = chunk_rows(index)
-            heads = hf_ref[rows, :].astype(BF)
+            heads = hf_ref[chunk_tiles(index)].reshape(CHUNK, D).astype(BF)
             hb_ref[layer, rows, :] = heads
             inner = h_ref[layer, rows, :] + dot(heads, wproj_ref[layer]) + bproj_ref[pl.ds(layer, 1), :]
             inner_ref[layer, rows, :] = inner
@@ -300,12 +374,12 @@
             cdf = 0.5 + 0.5 * lax.erf(hidden * math.sqrt(0.5))
             act = (hidden * cdf).astype(BF)
             act_ref[layer, rows, :] = act
-            slope = cdf + hidden * jnp.exp(-0.5 * hidden * hidden) * (1.0 / math.sqrt(2 * math.pi))
+            slope = cdf + hidden * jnp.exp2(hidden * hidden * (-0.5 * math.log2(math.e))) * (1.0 / math.sqrt(2 * math.pi))
             slope_ref[layer, rows, :] = slope.astype(BF)
             h_ref[layer + 1, rows, :] = inner + dot(act, wfc2_ref[layer]) + bfc2_ref[pl.ds(layer, 1), :]
             return carry
 
-        lax.fori_loop(0, chunks, feed, 0)
+        lax.fori_loop(0, chunks, feed, 0, unroll=2)
         return carry
 
     lax.fori_loop(0, LAYERS, forward, 0)
@@ -341,7 +415,7 @@
             dh_ref[rows, :] = dinner
             return carry
 
-        lax.fori_loop(0, chunks, feed, 0)
+        lax.fori_loop(0, chunks, feed, 0, unroll=2)
 
         def feed_weights(index, carry):
             cols = pl.ds(pl.multiple_of(index * 256, 256), 256)
@@ -362,83 +436,128 @@
             dy = dh_ref[rows, :].astype(BF)
             dz_ref[rows, :] = dy
             acc_ref[2] += fold_rows(dy.astype(F32))
-            hf_ref[rows, :] = dot_nt(dy, wproj_ref[layer])
-            return carry
-
-        lax.fori_loop(0, chunks, project, 0)
+            hf_ref[chunk_tiles(index)] = dot_nt(dy, wproj_ref[layer]).reshape(TILES, 2, TILE, D)
+            return carry
+
+        lax.fori_loop(0, chunks, project, 0, unroll=2)
         gproj = dot_tn(hb_ref[layer], dz_ref[...]).astype(BF)
         for half in range(2):
             stage_ref[half, PROJ_AT : PROJ_AT + D, :] = gproj[:, half * HW : (half + 1) * HW]
 
-        def attend(index, carry):
-            rows = block_rows(index)
-            large = lax.rem(index, 6) < 4
-            for direction in range(2):
-                kind = jnp.where(large, direction, 2)
-                first, second = halves(index, direction)
-                lanes = slice(direction * HW, (direction + 1) * HW)
-                grad = jnp.concatenate(
-                    [hf_ref[pl.ds(first, QUAD), lanes], hf_ref[pl.ds(second, QUAD), lanes]], axis=0
-                ).astype(BF)
-                grad32 = grad.astype(F32)
-                query = qkv_ref[layer, direction, rows, :HW]
-                keyset = qkv_ref[layer, direction, rows, HW : 2 * HW]
-                values = qkv_ref[layer, direction, rows, 2 * HW :]
-                expo = expo_ref[layer, direction, rows, :]
-                recip = 1.0 / dot(expo, heads_ref[...])
-                inner = grad32 * mixed_ref[layer, direction, rows, :]
-                inner_high = inner.astype(BF)
-                inner_low = (inner - inner_high.astype(F32)).astype(BF)
-                masks = heads_ref[...]
-                dprobs = dot_nt(
-                    jnp.concatenate([grad, -inner_high, -inner_low], axis=1),
-                    jnp.concatenate([head_stack(values, heads_ref), masks, masks], axis=1),
+        def tap_weight(direction, tap):
+            return lepe_ref[direction, layer, pl.ds(tap_row(direction, tap), 1), :]
+
+        def score(window, _):
+            direction, rows, grad, _ = window
+            values = qkv_ref[layer, direction, rows, 2 * HW :]
+            return dot_nt(head_rows(values, heads_ref), pad_keys(grad))
+
+        def weigh(window, dprobs):
+            direction, rows, _, _ = window
+            dscores = []
+            for head in range(GH):
+                part = probs_ref[layer, direction, rows, head * KEYS : (head + 1) * KEYS].astype(F32)
+                dpart = dprobs[head * BLOCK : (head + 1) * BLOCK]
+                inner = jnp.sum(part * dpart, axis=0, keepdims=True)
+                dscores.append((part * (dpart - inner)).astype(BF))
+            return dscores
+
+        def mix(window, dscores):
+            direction, rows, grad, _ = window
+            query = qkv_ref[layer, direction, rows, :HW]
+            side = qkv_ref[layer, direction, rows, HW : 2 * HW].T
+            dkeys = dot(jnp.concatenate(dscores, axis=1), head_stack(query, heads_ref))
+            dvalues = dot(probs_ref[layer, direction, rows, :], head_stack(grad, heads_ref))
+            dquery = [dot(side[head * HD : (head + 1) * HD], dscores[head]) for head in range(GH)]
+            return jnp.concatenate(dquery, axis=0), dkeys, dvalues
+
+        def finish(window, results):
+            direction, rows, grad, block = window
+            dquery, dkeys, dvalues = results
+            values = qkv_ref[layer, direction, rows, 2 * HW :]
+            first = direction * 3 * HW
+            dhid_ref[rows, first : first + HW] = (dquery * SCALE).T[:BLOCK].astype(BF)
+            dhid_ref[rows, first + HW : first + 2 * HW] = (dkeys * SCALE).astype(BF)
+            if block is None:
+                return values, dvalues
+            grad_tiles = as_tiles(grad.astype(F32))
+            result = as_tiles(dvalues)
+            for tap, cells in enumerate(tap_cells(grad_tiles, direction)):
+                result = result + cells * tap_weight(direction, TAPS - 1 - tap).reshape(1, 1, HW)
+            result = jnp.where(live_tiles(), result, 0.0).reshape(BLOCK, HW)
+            dhid_ref[rows, first + 2 * HW : first + 3 * HW] = result.astype(BF)
+            tiles = jnp.where(live_tiles(), as_tiles(values.astype(F32)), 0.0)
+            for tap, cells in enumerate(tap_cells(tiles, direction)):
+                acclepe_ref[direction, tap_row(direction, tap)] += jnp.sum(grad_tiles * cells, axis=0)
+            acclepe_ref[direction, TAPS] += jnp.sum(grad_tiles, axis=0)
+            return None
+
+        stages = (score, weigh, mix, finish)
+
+        def attend_large(index, carry):
+            windows = []
+            for part in range(2):
+                block = 6 * (index // 2) + 2 * lax.rem(index, 2) + part
+                for direction in range(2):
+                    lanes = slice(direction * HW, (direction + 1) * HW)
+                    if direction == 0:
+                        tiles = hf_ref[pl.ds(block * 7, 7), :, :, lanes]
+                    else:
+                        side = lax.rem(block, 2)
+                        tiles = hf_ref[pl.ds((block - side) * 7, TILES), side, :, lanes]
+                    windows.append((direction, block_rows(block), tiles.reshape(BLOCK, HW).astype(BF), block))
+            pipeline(stages, windows)
+            return carry
+
+        lax.fori_loop(0, images * 2, attend_large, 0)
+
+        def attend_small(index, carry):
+            windows = []
+            for part in range(2):
+                block = 6 * index + 4 + part
+                tiles = hf_ref[pl.ds(block * 7, 7)].reshape(BLOCK, D)
+                for direction in range(2):
+                    grad = tiles[:, direction * HW : (direction + 1) * HW].astype(BF)
+                    windows.append((direction, block_rows(block), grad, None))
+            results = pipeline(stages, windows)
+            for part in range(2):
+                rows = windows[2 * part][1]
+                grads = [windows[2 * part + direction][2].astype(F32) for direction in range(2)]
+                scaled = []
+                for direction in range(2):
+                    padded = pad_keys(grads[direction])
+                    scaled.append(
+                        jnp.concatenate(
+                            [
+                                (padded * tap_weight(direction, TAPS - 1 - tap)).astype(BF)
+                                for tap in range(TAPS)
+                            ],
+                            axis=0,
+                        )
+                    )
+                local = dot(wide_ref[...], jnp.concatenate(scaled, axis=1))
+                shifted = dot(
+                    tall_ref[...],
+                    jnp.concatenate([pad_keys(results[2 * part + direction][0]) for direction in range(2)], axis=1),
                 )
-                dscores = (expo.astype(F32) * dprobs).astype(BF)
-                dquery = dot(dscores, head_stack(keyset, heads_ref)) * recip * SCALE
-                dkeys_all = dot_tn((query.astype(F32) * recip * SCALE).astype(BF), dscores)
-                dvalues_all = dot_tn((grad32 * recip).astype(BF), expo)
-                dkeys = jnp.concatenate(
-                    [
-                        dkeys_all[head * HD : (head + 1) * HD, head * KEYS : (head + 1) * KEYS]
-                        for head in range(GH)
-                    ],
-                    axis=0,
-                ).T[:BLOCK]
-                dvalues = jnp.concatenate(
-                    [
-                        dvalues_all[head * HD : (head + 1) * HD, head * KEYS : (head + 1) * KEYS]
-                        for head in range(GH)
-                    ],
-                    axis=0,
-                ).T[:BLOCK]
-                wide_grad = jnp.concatenate([grad32, jnp.zeros((KEYS - BLOCK, HW), F32)], axis=0)
-                scaled = [
-                    (
-                        wide_grad * lepe_ref[direction, layer, pl.ds(tap_row(direction, TAPS - 1 - tap), 1), :]
-                    ).astype(BF)
-                    for tap in range(TAPS)
-                ]
-                dvalues = dvalues + dot(wide_ref[kind], jnp.concatenate(scaled, axis=0))
-                dhid_ref[rows, direction * 3 * HW : direction * 3 * HW + HW] = dquery.astype(BF)
-                dhid_ref[rows, direction * 3 * HW + HW : direction * 3 * HW + 2 * HW] = dkeys.astype(BF)
-                dhid_ref[rows, direction * 3 * HW + 2 * HW : direction * 3 * HW + 3 * HW] = dvalues.astype(BF)
-                shifted = dot(
-                    tall_ref[kind], jnp.concatenate([values, jnp.zeros((KEYS - BLOCK, HW), BF)], axis=0)
-                )
-                for tap in range(TAPS):
-                    acclepe_ref[direction, tap_row(direction, tap)] += fold_rows(
-                        grad32 * shifted[tap * BLOCK : (tap + 1) * BLOCK]
-                    )
-                acclepe_ref[direction, TAPS] += fold_rows(grad32)
-            return carry
-
-        lax.fori_loop(0, blocks, attend, 0)
+                for direction in range(2):
+                    lanes = slice(direction * HW, (direction + 1) * HW)
+                    first = direction * 3 * HW + 2 * HW
+                    dvalues = results[2 * part + direction][1] + local[:, lanes]
+                    dhid_ref[rows, first : first + HW] = dvalues.astype(BF)
+                    for tap in range(TAPS):
+                        acclepe_ref[direction, tap_row(direction, tap)] += fold_rows(
+                            grads[direction] * shifted[tap * BLOCK : (tap + 1) * BLOCK, lanes]
+                        )
+                    acclepe_ref[direction, TAPS] += fold_rows(grads[direction])
+            return carry
+
+        lax.fori_loop(0, images, attend_small, 0)
 
         def normalize(index, carry):
             rows = chunk_rows(index)
             turned = dot_nt(dhid_ref[rows, 3 * HW : 6 * HW], wqkv_ref[1, layer])
-            turned = jnp.where(lax.rem(index, 3) < 2, swap_quads(turned), turned)
+            turned = jnp.where(lax.rem(index, 3) < 2, join_tiles(turned), turned)
             dnormed = dot_nt(dhid_ref[rows, : 3 * HW], wqkv_ref[0, layer]) + turned
             dvalue, dgain = norm_back(dnormed, h_ref[layer, rows, :], g1_ref[pl.ds(layer, 1), :])
             acc_ref[0] += fold_rows(dgain)
@@ -446,7 +565,7 @@
             dh_ref[rows, :] = dh_ref[rows, :] + dvalue
             return carry
 
-        lax.fori_loop(0, chunks, normalize, 0)
+        lax.fori_loop(0, chunks, normalize, 0, unroll=2)
         small_ref[...] = jnp.zeros_like(small_ref)
         for direction in range(2):
             gqkv = dot_tn(normed_ref[layer, direction], dhid_ref[:, direction * 3 * HW : (direction + 1) * 3 * HW]).astype(BF)
@@ -603,8 +722,7 @@
         pltpu.VMEM((LAYERS, 2, rows, D), BF),
         pltpu.VMEM((LAYERS, 2, rows, 3 * HW), BF),
         pltpu.VMEM((LAYERS, 2, rows, SPAN), BF),
-        pltpu.VMEM((LAYERS, 2, rows, HW), F32),
-        pltpu.VMEM((rows, D), F32),
+        pltpu.VMEM((rows // 16, 2, TILE, D), F32),
         pltpu.VMEM((LAYERS, rows, D), BF),
         pltpu.VMEM((LAYERS, rows, D), F32),
         pltpu.VMEM((LAYERS, rows, D), BF),

time: 200 us -> 167 us (0.83)
  Pallas kernels: 106 us -> 73 us
    pallas_call x1, Pallas kernels: 102 us -> 68.8 us  [shards(): pl.pallas_call(step_kernel, out_shape=(jax.ShapeDtypeStruct((tokens_here,...]
where the time goes in v2:
time: 167 us; the launch traced here: 166 us
  Pallas kernels  73 us (44%)
  waiting for transfers between devices  60.9 us (36%)
  starting transfers between devices  16.8 us (10%)
  blocking collectives  8.44 us (5%)
  local copies, waits for them, and re-layouts  4.11 us (2%)
  other arithmetic  2.06 us (1%)
    pallas_call x1, Pallas kernels, shards(): pl.pallas_call(step_kernel, out_shape=(jax.ShapeDtypeStruct((tokens_here,...  68.8 us
    ppermute x6, waiting for transfers between devices, shards(): lax.ppermute(pieces[step], 'dp', [(i, i ^ step * stride) for i in range(d...  29.2 us
    ppermute x6, waiting for transfers between devices, shards(): lax.ppermute(own, 'dp', [(i, i ^ step * stride) for i in range(dp)])  24.7 us
    ppermute x6, starting transfers between devices, shards(): lax.ppermute(pieces[step], 'dp', [(i, i ^ step * stride) for i in range(d...  8.5 us
    ppermute x6, starting transfers between devices, shards(): lax.ppermute(own, 'dp', [(i, i ^ step * stride) for i in range(dp)])  8.01 us
    all_gather x1, blocking collectives, shards(): wqkv_all = lax.all_gather(w_qkv.reshape(LAYERS, D, 3 * HW), 'heads', axis=0)  6.36 us
    pallas_call x1, Pallas kernels, shards(): pl.pallas_call(unpack_kernel, out_shape=(jax.ShapeDtypeStruct((LAYERS, D)...  4.21 us
    ppermute x1, waiting for transfers between devices, shards(): other = lax.ppermute(own, 'heads', swap)  3.58 us
  transfers between devices with their start and end apart: 14, of which 12 were waited for; matrix products, arithmetic and copies ran while one was open for 0% of the time, Pallas kernels for 0%

profile of v2, /device:TPU:0, one launch (start us, length us, event | category | flops | bytes accessed | tf_op | source)
XLA Modules:
  0.0 166.1 jit_solution(11818292225286291161)
XLA Ops:
  0.6 0.7 copy.46
  1.4 0.7 pad_maximum_fusion.1
  2.0 2.1 %all-gather.1 = f32[4,10,128]{2,1,0:T(8,128)} all-gather(f32[2,10,128]{2,1,0:T(8,128)S(1)} %copy.43), channel_id=3, replica_groups=mesh['dp'=16,'heads'=2] {'heads'}, dimensions={0}, use_global_device_ids=true | all-gather | bytes 30720 | tf_op jit(solution)/shard_map/all_gather | solution.py:716
  4.1 6.4 %all-gather = bf16[4,1,256,384]{3,2,1,0:T(8,128)(2,1)} all-gather(bf16[2,1,256,384]{3,2,1,0:T(8,128)(2,1)} %param.26), channel_id=2, replica_groups=mesh['dp'=16,'heads'=2] {'heads'}, dimensions={0}, use_global_device_ids=true | all-gather | bytes 1179648 | tf_op jit(solution)/shard_map/all_gather | solution.py:714
  10.5 0.7 dynamic_slice.3
  11.2 0.6 pad_add_fusion.meta
  11.8 68.8 %step.1 = (bf16[1216,256]{1,0:T(8,128)(2,1)}, f32[1216,256]{1,0:T(8,128)}, bf16[2,16,2,208,128]{4,3,2,1,0:T(8,128)(2,1)}) custom-call(s32[4]{0:T(128)} %pad_add_fusion.meta, bf16[1216,256]{1,0:T(8,128)(2,1)} %tok_ref.1, bf16[1216,256]{1,0:T(8,128)(2,1)} %cot_ref.1, f32[2,256]{1,0:T(2,128)} %g1_ref.1, f32[2,256]{1,0:T(2,128)} %b1_ref.1, ...), custom_call_target="tpu_custom_call" | custom-call | tf_op jit(solution)/shard_map/step/pallas_call | solution.py:740
  80.6 0.0 copy-start.1
  80.6 1.7 %slice_bitcast_fusion = bf16[16,2,208,128]{3,2,1,0:T(8,128)(2,1)S(1)} fusion(bf16[2,16,2,208,128]{4,3,2,1,0:T(8,128)(2,1)} %get-tuple-element.33), kind=kLoop, calls=%fused_computation.2 | loop fusion | bytes 3407872 | tf_op jit(solution)/shard_map/squeeze | solution.py:782
  82.3 0.3 collective-permute-start
  82.6 3.4 %collective-permute-done = bf16[16,2,208,128]{3,2,1,0:T(8,128)(2,1)S(1)} collective-permute-done((bf16[16,2,208,128]{3,2,1,0:T(8,128)(2,1)S(1)}, bf16[16,2,208,128]{3,2,1,0:T(8,128)(2,1)S(1)}, u32[]{:S(2)}, u32[]{:S(2)}) %collective-permute-start) | collective-permute-done | bytes 1703968 | tf_op jit(solution)/shard_map/ppermute | solution.py:782
  86.0 0.0 copy-done.1
  86.0 0.4 fusion
  86.4 0.1 fusion.1
  86.5 2.7 %collective-permute-start.1 = (bf16[4,2,208,128]{3,2,1,0:T(8,128)(2,1)S(1)}, bf16[4,2,208,128]{3,2,1,0:T(8,128)(2,1)S(1)}, u32[]{:S(2)}, u32[]{:S(2)}) collective-permute-start(bf16[4,2,208,128]{3,2,1,0:T(8,128)(2,1)S(1)} %get-tuple-element.94), channel_id=1, source_target_pairs={{0,2},{2,0},{4,6},{6,4},{8,10},{10,8},{12,14},{14,12},{16,18},{18,... | collective-permute-start | bytes 1277960 | tf_op jit(solution)/shard_map/ppermute | solution.py:791
  89.2 1.5 collective-permute-start.3
  90.7 0.0 collective-permute-start.2
  90.8 9.0 %collective-permute-done.1 = bf16[4,2,208,128]{3,2,1,0:T(8,128)(2,1)S(1)} collective-permute-done((bf16[4,2,208,128]{3,2,1,0:T(8,128)(2,1)S(1)}, bf16[4,2,208,128]{3,2,1,0:T(8,128)(2,1)S(1)}, u32[]{:S(2)}, u32[]{:S(2)}) %collective-permute-start.1) | collective-permute-done | bytes 426016 | tf_op jit(solution)/shard_map/ppermute | solution.py:791
  99.8 10.2 %collective-permute-done.3 = bf16[4,2,208,128]{3,2,1,0:T(8,128)(2,1)S(1)} collective-permute-done((bf16[4,2,208,128]{3,2,1,0:T(8,128)(2,1)S(1)}, bf16[4,2,208,128]{3,2,1,0:T(8,128)(2,1)S(1)}, u32[]{:S(2)}, u32[]{:S(2)}) %collective-permute-start.3) | collective-permute-done | bytes 426016 | tf_op jit(solution)/shard_map/ppermute | solution.py:791
  110.0 1.4 collective-permute-done.2
  111.4 0.2 add_convert_fusion
  111.6 1.6 collective-permute-start.4
  113.3 2.4 %collective-permute-start.6 = (bf16[1,2,208,128]{3,2,1,0:T(8,128)(2,1)S(1)}, bf16[1,2,208,128]{3,2,1,0:T(8,128)(2,1)S(1)}, u32[]{:S(2)}, u32[]{:S(2)}) collective-permute-start(bf16[1,2,208,128]{3,2,1,0:T(8,128)(2,1)S(1)} %get-tuple-element.98), channel_id=1, source_target_pairs={{0,24},{2,26},{4,28},{6,30},{8,16},{10,18},{12,20},{14,22},{16,8},... | collective-permute-start | bytes 319496 | tf_op jit(solution)/shard_map/ppermute | solution.py:791
  115.7 0.2 collective-permute-start.5
  115.9 0.7 collective-permute-done.4
  116.6 4.3 %collective-permute-done.6 = bf16[1,2,208,128]{3,2,1,0:T(8,128)(2,1)S(1)} collective-permute-done((bf16[1,2,208,128]{3,2,1,0:T(8,128)(2,1)S(1)}, bf16[1,2,208,128]{3,2,1,0:T(8,128)(2,1)S(1)}, u32[]{:S(2)}, u32[]{:S(2)}) %collective-permute-start.6) | collective-permute-done | bytes 106528 | tf_op jit(solution)/shard_map/ppermute | solution.py:791
  120.9 3.6 %collective-permute-done.5 = bf16[1,2,208,128]{3,2,1,0:T(8,128)(2,1)S(1)} collective-permute-done((bf16[1,2,208,128]{3,2,1,0:T(8,128)(2,1)S(1)}, bf16[1,2,208,128]{3,2,1,0:T(8,128)(2,1)S(1)}, u32[]{:S(2)}, u32[]{:S(2)}) %collective-permute-start.5) | collective-permute-done | bytes 106528 | tf_op jit(solution)/shard_map/ppermute | solution.py:791
  124.5 0.1 constant_dynamic-update-slice_fusion.6
  124.6 3.2 %collective-permute-start.9 = (bf16[1,2,208,128]{3,2,1,0:T(8,128)(2,1)S(1)}, bf16[1,2,208,128]{3,2,1,0:T(8,128)(2,1)S(1)}, u32[]{:S(2)}, u32[]{:S(2)}) collective-permute-start(bf16[1,2,208,128]{3,2,1,0:T(8,128)(2,1)S(1)} %get-tuple-element.93), channel_id=1, source_target_pairs={{0,24},{2,26},{4,28},{6,30},{8,16},{10,18},{12,20},{14,22},{16,8},... | collective-permute-start | bytes 319496 | tf_op jit(solution)/shard_map/ppermute | solution.py:799
  127.7 0.0 collective-permute-start.8
  127.7 1.3 collective-permute-start.7
  129.0 3.3 %collective-permute-done.9 = bf16[1,2,208,128]{3,2,1,0:T(8,128)(2,1)S(1)} collective-permute-done((bf16[1,2,208,128]{3,2,1,0:T(8,128)(2,1)S(1)}, bf16[1,2,208,128]{3,2,1,0:T(8,128)(2,1)S(1)}, u32[]{:S(2)}, u32[]{:S(2)}) %collective-permute-start.9) | collective-permute-done | bytes 106528 | tf_op jit(solution)/shard_map/ppermute | solution.py:799
  132.3 3.5 %collective-permute-done.8 = bf16[1,2,208,128]{3,2,1,0:T(8,128)(2,1)S(1)} collective-permute-done((bf16[1,2,208,128]{3,2,1,0:T(8,128)(2,1)S(1)}, bf16[1,2,208,128]{3,2,1,0:T(8,128)(2,1)S(1)}, u32[]{:S(2)}, u32[]{:S(2)}) %collective-permute-start.8) | collective-permute-done | bytes 106528 | tf_op jit(solution)/shard_map/ppermute | solution.py:799
  135.9 0.0 collective-permute-done.7
  135.9 0.1 pad_maximum_fusion
  135.9 0.0 copy-start
  136.0 1.6 collective-permute-start.10
  137.6 0.4 collective-permute-start.12
  138.0 1.5 collective-permute-start.11
  139.6 9.2 %collective-permute-done.10 = bf16[4,2,208,128]{3,2,1,0:T(8,128)(2,1)S(1)} collective-permute-done((bf16[4,2,208,128]{3,2,1,0:T(8,128)(2,1)S(1)}, bf16[4,2,208,128]{3,2,1,0:T(8,128)(2,1)S(1)}, u32[]{:S(2)}, u32[]{:S(2)}) %collective-permute-start.10) | collective-permute-done | bytes 426016 | tf_op jit(solution)/shard_map/ppermute | solution.py:799
  148.8 0.1 constant_dynamic-update-slice_fusion.2
  148.8 8.6 %collective-permute-done.11 = bf16[4,2,208,128]{3,2,1,0:T(8,128)(2,1)S(1)} collective-permute-done((bf16[4,2,208,128]{3,2,1,0:T(8,128)(2,1)S(1)}, bf16[4,2,208,128]{3,2,1,0:T(8,128)(2,1)S(1)}, u32[]{:S(2)}, u32[]{:S(2)}) %collective-permute-start.11) | collective-permute-done | bytes 426016 | tf_op jit(solution)/shard_map/ppermute | solution.py:799
  157.5 0.1 constant_dynamic-update-slice_fusion.1
  157.5 0.0 collective-permute-done.12
  157.5 0.1 constant_dynamic-update-slice_fusion.own_ref
  157.6 0.1 collective-permute-start.13
  157.7 3.6 %collective-permute-done.13.other_ref = bf16[16,2,208,128]{3,2,1,0:T(8,128)(2,1)S(1)} collective-permute-done((bf16[16,2,208,128]{3,2,1,0:T(8,128)(2,1)S(1)}, bf16[16,2,208,128]{3,2,1,0:T(8,128)(2,1)S(1)}, u32[]{:S(2)}, u32[]{:S(2)}) %collective-permute-start.13) | collective-permute-done | bytes 1703968 | tf_op jit(solution)/shard_map/ppermute | solution.py:804
  161.3 0.0 copy-done
  161.3 4.2 %unpack.1 = (f32[2,256]{1,0:T(2,128)}, f32[2,256]{1,0:T(2,128)}, f32[2,1,256,384]{3,2,1,0:T(8,128)}, f32[2,1,9,128]{3,2,1,0:T(8,128)S(1)}, f32[2,1,128]{2,1,0:T(...) custom-call(s32[4]{0:T(128)S(1)} %copy-done, ...), custom_call_target="tpu_custom_call" | custom-call | tf_op jit(solution)/shard_map/unpack/pallas_call | solution.py:805
  165.5 0.6 copy.44
  (5 shorter events, 0.1 us)
Async XLA Ops:
  80.6 5.4 %copy-start.1 = (bf16[2,16,2,208,128]{4,3,2,1,0:T(8,128)(2,1)S(1)}, bf16[2,16,2,208,128]{4,3,2,1,0:T(8,128)(2,1)}, u32[]{:S(2)}) copy-start(bf16[2,16,2,208,128]{4,3,2,1,0:T(8,128)(2,1)} %get-tuple-element.33) | copy-start | bytes 10223620
  82.3 3.7 %collective-permute-start = (bf16[16,2,208,128]{3,2,1,0:T(8,128)(2,1)S(1)}, bf16[16,2,208,128]{3,2,1,0:T(8,128)(2,1)S(1)}, u32[]{:S(2)}, u32[]{:S(2)}) collective-permute-start(bf16[16,2,208,128]{3,2,1,0:T(8,128)(2,1)S(1)} %slice_bitcast_fusion), channel_id=1, source_target_pairs={{0,1},{1,0},{2,3},{3,2},{4,5},{5,4},{6,7},{7,6},{8,9},{9,8},{10,11... | collective-permute-start | bytes 5111816 | tf_op jit(solution)/shard_map/ppermute | solution.py:782
  86.5 13.3 %collective-permute-start.1 = (bf16[4,2,208,128]{3,2,1,0:T(8,128)(2,1)S(1)}, bf16[4,2,208,128]{3,2,1,0:T(8,128)(2,1)S(1)}, u32[]{:S(2)}, u32[]{:S(2)}) collective-permute-start(bf16[4,2,208,128]{3,2,1,0:T(8,128)(2,1)S(1)} %get-tuple-element.94), channel_id=1, source_target_pairs={{0,2},{2,0},{4,6},{6,4},{8,10},{10,8},{12,14},{14,12},{16,18},{18,... | collective-permute-start | bytes 1277960 | tf_op jit(solution)/shard_map/ppermute | solution.py:791
  89.2 20.8 %collective-permute-start.3 = (bf16[4,2,208,128]{3,2,1,0:T(8,128)(2,1)S(1)}, bf16[4,2,208,128]{3,2,1,0:T(8,128)(2,1)S(1)}, u32[]{:S(2)}, u32[]{:S(2)}) collective-permute-start(bf16[4,2,208,128]{3,2,1,0:T(8,128)(2,1)S(1)} %get-tuple-element.95), channel_id=1, source_target_pairs={{0,6},{2,4},{4,2},{6,0},{8,14},{10,12},{12,10},{14,8},{16,22},{18,... | collective-permute-start | bytes 1277960 | tf_op jit(solution)/shard_map/ppermute | solution.py:791
  90.7 20.6 %collective-permute-start.2 = (bf16[4,2,208,128]{3,2,1,0:T(8,128)(2,1)S(1)}, bf16[4,2,208,128]{3,2,1,0:T(8,128)(2,1)S(1)}, u32[]{:S(2)}, u32[]{:S(2)}) collective-permute-start(bf16[4,2,208,128]{3,2,1,0:T(8,128)(2,1)S(1)} %get-tuple-element.96), channel_id=1, source_target_pairs={{0,4},{2,6},{4,0},{6,2},{8,12},{10,14},{12,8},{14,10},{16,20},{18,... | collective-permute-start | bytes 1277960 | tf_op jit(solution)/shard_map/ppermute | solution.py:791
  111.6 4.9 %collective-permute-start.4 = (bf16[1,2,208,128]{3,2,1,0:T(8,128)(2,1)S(1)}, bf16[1,2,208,128]{3,2,1,0:T(8,128)(2,1)S(1)}, u32[]{:S(2)}, u32[]{:S(2)}) collective-permute-start(bf16[1,2,208,128]{3,2,1,0:T(8,128)(2,1)S(1)} %get-tuple-element.97), channel_id=1, source_target_pairs={{0,8},{2,10},{4,12},{6,14},{8,0},{10,2},{12,4},{14,6},{16,24},{18,... | collective-permute-start | bytes 319496 | tf_op jit(solution)/shard_map/ppermute | solution.py:791
  113.3 7.6 %collective-permute-start.6 = (bf16[1,2,208,128]{3,2,1,0:T(8,128)(2,1)S(1)}, bf16[1,2,208,128]{3,2,1,0:T(8,128)(2,1)S(1)}, u32[]{:S(2)}, u32[]{:S(2)}) collective-permute-start(bf16[1,2,208,128]{3,2,1,0:T(8,128)(2,1)S(1)} %get-tuple-element.98), channel_id=1, source_target_pairs={{0,24},{2,26},{4,28},{6,30},{8,16},{10,18},{12,20},{14,22},{16,8},... | collective-permute-start | bytes 319496 | tf_op jit(solution)/shard_map/ppermute | solution.py:791
  115.7 8.8 %collective-permute-start.5 = (bf16[1,2,208,128]{3,2,1,0:T(8,128)(2,1)S(1)}, bf16[1,2,208,128]{3,2,1,0:T(8,128)(2,1)S(1)}, u32[]{:S(2)}, u32[]{:S(2)}) collective-permute-start(bf16[1,2,208,128]{3,2,1,0:T(8,128)(2,1)S(1)} %get-tuple-element.99), channel_id=1, source_target_pairs={{0,16},{2,18},{4,20},{6,22},{8,24},{10,26},{12,28},{14,30},{16,0},... | collective-permute-start | bytes 319496 | tf_op jit(solution)/shard_map/ppermute | solution.py:791
  124.6 7.8 %collective-permute-start.9 = (bf16[1,2,208,128]{3,2,1,0:T(8,128)(2,1)S(1)}, bf16[1,2,208,128]{3,2,1,0:T(8,128)(2,1)S(1)}, u32[]{:S(2)}, u32[]{:S(2)}) collective-permute-start(bf16[1,2,208,128]{3,2,1,0:T(8,128)(2,1)S(1)} %get-tuple-element.93), channel_id=1, source_target_pairs={{0,24},{2,26},{4,28},{6,30},{8,16},{10,18},{12,20},{14,22},{16,8},... | collective-permute-start | bytes 319496 | tf_op jit(solution)/shard_map/ppermute | solution.py:799
  127.7 8.2 %collective-permute-start.8 = (bf16[1,2,208,128]{3,2,1,0:T(8,128)(2,1)S(1)}, bf16[1,2,208,128]{3,2,1,0:T(8,128)(2,1)S(1)}, u32[]{:S(2)}, u32[]{:S(2)}) collective-permute-start(bf16[1,2,208,128]{3,2,1,0:T(8,128)(2,1)S(1)} %get-tuple-element.93), channel_id=1, source_target_pairs={{0,16},{2,18},{4,20},{6,22},{8,24},{10,26},{12,28},{14,30},{16,0},... | collective-permute-start | bytes 319496 | tf_op jit(solution)/shard_map/ppermute | solution.py:799
  127.7 8.2 %collective-permute-start.7 = (bf16[1,2,208,128]{3,2,1,0:T(8,128)(2,1)S(1)}, bf16[1,2,208,128]{3,2,1,0:T(8,128)(2,1)S(1)}, u32[]{:S(2)}, u32[]{:S(2)}) collective-permute-start(bf16[1,2,208,128]{3,2,1,0:T(8,128)(2,1)S(1)} %get-tuple-element.93), channel_id=1, source_target_pairs={{0,8},{2,10},{4,12},{6,14},{8,0},{10,2},{12,4},{14,6},{16,24},{18,... | collective-permute-start | bytes 319496 | tf_op jit(solution)/shard_map/ppermute | solution.py:799
  135.9 25.3 %copy-start = (s32[4]{0:T(128)S(1)}, s32[4]{0:T(128)}, u32[]{:S(2)}) copy-start(s32[4]{0:T(128)} %pad_add_fusion.meta) | copy-start | bytes 52
  136.0 12.8 %collective-permute-start.10 = (bf16[4,2,208,128]{3,2,1,0:T(8,128)(2,1)S(1)}, bf16[4,2,208,128]{3,2,1,0:T(8,128)(2,1)S(1)}, u32[]{:S(2)}, u32[]{:S(2)}) collective-permute-start(bf16[4,2,208,128]{3,2,1,0:T(8,128)(2,1)S(1)} %pad_maximum_fusion), channel_id=1, source_target_pairs={{0,2},{2,0},{4,6},{6,4},{8,10},{10,8},{12,14},{14,12},{16,18},{18,... | collective-permute-start | bytes 1277960 | tf_op jit(solution)/shard_map/ppermute | solution.py:799
  137.6 20.0 %collective-permute-start.12 = (bf16[4,2,208,128]{3,2,1,0:T(8,128)(2,1)S(1)}, bf16[4,2,208,128]{3,2,1,0:T(8,128)(2,1)S(1)}, u32[]{:S(2)}, u32[]{:S(2)}) collective-permute-start(bf16[4,2,208,128]{3,2,1,0:T(8,128)(2,1)S(1)} %pad_maximum_fusion), channel_id=1, source_target_pairs={{0,6},{2,4},{4,2},{6,0},{8,14},{10,12},{12,10},{14,8},{16,22},{18,... | collective-permute-start | bytes 1277960 | tf_op jit(solution)/shard_map/ppermute | solution.py:799
  138.0 19.5 %collective-permute-start.11 = (bf16[4,2,208,128]{3,2,1,0:T(8,128)(2,1)S(1)}, bf16[4,2,208,128]{3,2,1,0:T(8,128)(2,1)S(1)}, u32[]{:S(2)}, u32[]{:S(2)}) collective-permute-start(bf16[4,2,208,128]{3,2,1,0:T(8,128)(2,1)S(1)} %pad_maximum_fusion), channel_id=1, source_target_pairs={{0,4},{2,6},{4,0},{6,2},{8,12},{10,14},{12,8},{14,10},{16,20},{18,... | collective-permute-start | bytes 1277960 | tf_op jit(solution)/shard_map/ppermute | solution.py:799
  157.6 3.7 %collective-permute-start.13 = (bf16[16,2,208,128]{3,2,1,0:T(8,128)(2,1)S(1)}, bf16[16,2,208,128]{3,2,1,0:T(8,128)(2,1)S(1)}, u32[]{:S(2)}, u32[]{:S(2)}) collective-permute-start(bf16[16,2,208,128]{3,2,1,0:T(8,128)(2,1)S(1)} %constant_dynamic-update-slice_fusion.own_ref), channel_id=1, source_target_pairs={{0,1},{1,0},{2,3},{3,2},{4,5},{5,4},{6,7},{7,6},{8,9},{9,8},{10,11... | collective-permute-start | bytes 5111816 | tf_op jit(solution)/shard_map/ppermute | solution.py:804

commit v3 on v2

--- a/solution.py
+++ b/solution.py
@@ -39,6 +39,7 @@
 SMALL_AT = 3072
 SMALL = 32
 PACKED = SMALL_AT + SMALL
+ALL_PACKED = LAYERS * PACKED
 
 
 def place_table():
@@ -194,13 +195,17 @@
 
 
 def step_kernel(
-    meta,
+    counts_ref,
     tok_ref,
     cot_ref,
     g1_ref,
     b1_ref,
-    wqkv_ref,
-    lepe_ref,
+    own_wqkv_ref,
+    other_wqkv_ref,
+    own_lepe_ref,
+    other_lepe_ref,
+    own_lepeb_ref,
+    other_lepeb_ref,
     wproj_ref,
     bproj_ref,
     g2_ref,
@@ -216,7 +221,12 @@
     heads_ref,
     out_ref,
     dtok_ref,
-    packed_ref,
+    keep_first_ref,
+    keep_second_ref,
+    send_first_ref,
+    send_second_ref,
+    wqkv_ref,
+    lepe_ref,
     h_ref,
     normed_ref,
     qkv_ref,
@@ -240,10 +250,19 @@
     images = rows_all // IMG
     chunks = rows_all // CHUNK
     blocks = rows_all // BLOCK
-    parts = packed_ref.shape[1]
-    part_rows = packed_ref.shape[3]
-    core = meta[0]
-    mine = meta[1]
+    parts = keep_first_ref.shape[0]
+    first_rows = keep_first_ref.shape[1]
+    second_rows = keep_second_ref.shape[1]
+    part_rows = first_rows + second_rows
+    core = lax.axis_index("heads")
+    mine = lax.axis_index("dp")
+    for direction, (wqkv, lepe, lepeb) in (
+        (core, (own_wqkv_ref, own_lepe_ref, own_lepeb_ref)),
+        (1 - core, (other_wqkv_ref, other_lepe_ref, other_lepeb_ref)),
+    ):
+        wqkv_ref[direction] = wqkv[:, 0]
+        lepe_ref[direction, :, :TAPS] = lepe[:, 0]
+        lepe_ref[direction, :, TAPS : TAPS + 1] = lepeb[...]
 
     def chunk_rows(index):
         return pl.ds(pl.multiple_of(index * CHUNK, 16), CHUNK)
@@ -256,7 +275,7 @@
 
     def keep_of(image):
         place = lax.broadcasted_iota(jnp.int32, (IMG, 1), 0)
-        limit = meta[2 + image]
+        limit = counts_ref[core * images + image]
         group = (place - 448) // BLOCK
         inside = (place - 448) % BLOCK
         return (place < 448) | (inside < 36 * (limit - 3 * group))
@@ -394,6 +413,7 @@
 
     def backward(step, carry):
         layer = LAYERS - 1 - step
+        base = pl.multiple_of(layer * PACKED, 16)
         acc_ref[...] = jnp.zeros_like(acc_ref)
         accff_ref[...] = jnp.zeros_like(accff_ref)
         acclepe_ref[...] = jnp.zeros_like(acclepe_ref)
@@ -425,8 +445,8 @@
             for piece in range(2):
                 at = pl.multiple_of((lax.rem(index, 2) * 2 + piece) * 256, 256)
                 lanes = slice(piece * HW, (piece + 1) * HW)
-                stage_ref[half, pl.ds(FC1_AT + at, 256), :] = first[:, lanes]
-                stage_ref[half, pl.ds(FC2_AT + at, 256), :] = second[:, lanes]
+                stage_ref[half, pl.ds(base + FC1_AT + at, 256), :] = first[:, lanes]
+                stage_ref[half, pl.ds(base + FC2_AT + at, 256), :] = second[:, lanes]
             return carry
 
         lax.fori_loop(0, 4, feed_weights, 0)
@@ -442,7 +462,7 @@
         lax.fori_loop(0, chunks, project, 0, unroll=2)
         gproj = dot_tn(hb_ref[layer], dz_ref[...]).astype(BF)
         for half in range(2):
-            stage_ref[half, PROJ_AT : PROJ_AT + D, :] = gproj[:, half * HW : (half + 1) * HW]
+            stage_ref[half, pl.ds(base + PROJ_AT, D), :] = gproj[:, half * HW : (half + 1) * HW]
 
         def tap_weight(direction, tap):
             return lepe_ref[direction, layer, pl.ds(tap_row(direction, tap), 1), :]
@@ -571,7 +591,7 @@
             gqkv = dot_tn(normed_ref[layer, direction], dhid_ref[:, direction * 3 * HW : (direction + 1) * 3 * HW]).astype(BF)
             for piece in range(3):
                 at = QKV_AT + 256 * piece
-                stage_ref[direction, at : at + 256, :] = gqkv[:, piece * HW : (piece + 1) * HW]
+                stage_ref[direction, pl.ds(base + at, 256), :] = gqkv[:, piece * HW : (piece + 1) * HW]
             small_ref[direction, :10, :] = jnp.sum(acclepe_ref[direction], axis=1)
         sums = jnp.sum(acc_ref[...], axis=1)
         for piece in range(2):
@@ -579,22 +599,30 @@
         sums = jnp.sum(accff_ref[...], axis=0, keepdims=True)
         for piece in range(8):
             small_ref[1, 10 + piece : 11 + piece, :] = sums[:, piece * HW : (piece + 1) * HW]
-        stage_ref[:, SMALL_AT:PACKED, :] = small_ref[...].astype(BF)
-
-        for half in range(2):
-            slot = jnp.bitwise_xor(core, half)
-
-            def hand_out(part, carry):
-                place = digits_reversed(jnp.bitwise_xor(part, mine), parts)
-                at = pl.ds(pl.multiple_of(part * part_rows, 16), part_rows)
-                packed_ref[slot, place, layer] = stage_ref[half, at, :]
-                return carry
-
-            lax.fori_loop(0, parts, hand_out, 0)
+        stage_ref[:, pl.ds(base + SMALL_AT, SMALL), :] = small_ref[...].astype(BF)
+
         return carry
 
-    stage_ref[:, PACKED:, :] = jnp.zeros((2, stage_ref.shape[1] - PACKED, HW), BF)
+    stage_ref[:, ALL_PACKED:, :] = jnp.zeros((2, stage_ref.shape[1] - ALL_PACKED, HW), BF)
     lax.fori_loop(0, LAYERS, backward, 0)
+
+    for half in range(2):
+        for same, first_ref, second_ref in (
+            (True, keep_first_ref, keep_second_ref),
+            (False, send_first_ref, send_second_ref),
+        ):
+
+            @pl.when((core == half) == same)
+            def _():
+                def hand_out(part, carry):
+                    slot = jnp.bitwise_xor(part, mine)
+                    at = pl.multiple_of(part * part_rows, 16)
+                    first_ref[place_of(slot, parts, 0)] = stage_ref[half, pl.ds(at, first_rows), :]
+                    at = pl.multiple_of(at + first_rows, 16)
+                    second_ref[place_of(slot, parts, 1)] = stage_ref[half, pl.ds(at, second_rows), :]
+                    return carry
+
+                lax.fori_loop(0, parts, hand_out, 0)
 
     for image in range(images):
         value = dh_ref[pl.ds(image * IMG, IMG), :]
@@ -604,27 +632,27 @@
         dtok_ref[spot, :] = dot_tn(place_ref[...], high) + dot_tn(place_ref[...], low)
 
 
-def digit_sizes(parts):
-    sizes = []
-    while parts > 1:
-        size = 4 if parts % 4 == 0 else 2
-        sizes.append(size)
-        parts //= size
-    return sizes
-
-
-def digits_reversed(index, parts):
+def digits_of(parts, which):
+    digits, stride = [], 1
+    while stride < parts:
+        size = 4 if parts // stride % 4 == 0 else 2
+        digits.append((size, stride))
+        stride *= size
+    return digits[which:] + digits[:which]
+
+
+def place_of(index, parts, which):
     place = 0
-    for size in digit_sizes(parts):
-        place = place * size + lax.rem(index, size)
-        index = index // size
+    for size, stride in digits_of(parts, which):
+        place = place * size + lax.rem(index // stride, size)
     return place
 
 
 def unpack_kernel(
-    meta,
-    own_ref,
-    other_ref,
+    own_first_ref,
+    own_second_ref,
+    other_first_ref,
+    other_second_ref,
     g1_ref,
     b1_ref,
     gqkv_ref,
@@ -640,43 +668,49 @@
     gbfc2_ref,
     stage_ref,
 ):
-    parts = own_ref.shape[0]
-    part_rows = own_ref.shape[2]
-    core = meta[0]
-    mine = meta[1]
-
+    parts = own_first_ref.shape[0]
+    first_rows = own_first_ref.shape[1]
+    second_rows = own_second_ref.shape[1]
+    core = lax.axis_index("heads")
+    mine = lax.axis_index("dp")
+
+    def collect(part, carry):
+        slot = jnp.bitwise_xor(part, mine)
+        at = pl.multiple_of(part * (first_rows + second_rows), 16)
+        first = place_of(slot, parts, 0)
+        second = place_of(slot, parts, 1)
+        stage_ref[core, pl.ds(at, first_rows), :] = own_first_ref[first]
+        stage_ref[1 - core, pl.ds(at, first_rows), :] = other_first_ref[first]
+        at = pl.multiple_of(at + first_rows, 16)
+        stage_ref[core, pl.ds(at, second_rows), :] = own_second_ref[second]
+        stage_ref[1 - core, pl.ds(at, second_rows), :] = other_second_ref[second]
+        return carry
+
+    lax.fori_loop(0, parts, collect, 0)
     for layer in range(LAYERS):
-
-        def collect(part, carry):
-            place = digits_reversed(jnp.bitwise_xor(part, mine), parts)
-            at = pl.ds(pl.multiple_of(part * part_rows, 16), part_rows)
-            stage_ref[core, at, :] = own_ref[place, layer]
-            stage_ref[1 - core, at, :] = other_ref[place, layer]
-            return carry
-
-        lax.fori_loop(0, parts, collect, 0)
+        base = layer * PACKED
         for half in range(2):
             for piece in range(4):
                 lanes = slice(half * 512 + piece * HW, half * 512 + (piece + 1) * HW)
-                at = FC1_AT + 256 * piece
+                at = base + FC1_AT + 256 * piece
                 gfc1_ref[layer, :, lanes] = stage_ref[half, at : at + 256, :].astype(F32)
-                at = FC2_AT + 256 * piece
+                at = base + FC2_AT + 256 * piece
                 gfc2_ref[layer, lanes, :] = stage_ref[half, at : at + 256, :].astype(F32).T
             gproj_ref[layer, :, half * HW : (half + 1) * HW] = stage_ref[
-                half, PROJ_AT : PROJ_AT + 256, :
+                half, base + PROJ_AT : base + PROJ_AT + 256, :
             ].astype(F32)
         for piece in range(3):
-            at = QKV_AT + 256 * piece
+            at = base + QKV_AT + 256 * piece
             gqkv_ref[layer, 0, :, piece * HW : (piece + 1) * HW] = stage_ref[core, at : at + 256, :].astype(F32)
-        small = stage_ref[core, SMALL_AT:PACKED, :].astype(F32)
+        small = stage_ref[core, base + SMALL_AT : base + PACKED, :].astype(F32)
         glepe_ref[layer, 0] = small[:TAPS]
         glepeb_ref[layer] = small[TAPS : TAPS + 1]
-        small = stage_ref[0, SMALL_AT:PACKED, :].astype(F32)
+        small = stage_ref[0, base + SMALL_AT : base + PACKED, :].astype(F32)
         for place, ref in enumerate((g1_ref, b1_ref, gbproj_ref, g2_ref, b2_ref, gbfc2_ref)):
             for piece in range(2):
                 row = 10 + 6 * piece + place
                 ref[layer : layer + 1, piece * HW : (piece + 1) * HW] = small[row : row + 1]
-        small = stage_ref[1, SMALL_AT:PACKED, :].astype(F32)
+        small = stage_ref[1, base + SMALL_AT : base + PACKED, :].astype(F32)
         for piece in range(8):
             gbfc1_ref[layer : layer + 1, piece * HW : (piece + 1) * HW] = small[10 + piece : 11 + piece]
 
@@ -707,17 +741,19 @@
     tokens_here = tokens.shape[0]
     images = tokens_here // TOK_IMG
     rows = images * IMG
-    core = lax.axis_index("heads")
-    mine = lax.axis_index("dp")
-    own_counts = lax.dynamic_slice(counts, (core * images,), (images,))
-    meta = jnp.concatenate([jnp.stack([core, mine]).astype(jnp.int32), own_counts])
-    wqkv_all = lax.all_gather(w_qkv.reshape(LAYERS, D, 3 * HW), "heads", axis=0)
-    lepe = jnp.concatenate([lepe_w[:, 0], lepe_b], axis=1)
-    lepe_all = lax.all_gather(lepe, "heads", axis=0)
-    part_rows = -(-PACKED // (16 * dp)) * 16
+    swap = [(0, 1), (1, 0)]
+
+    def across(value):
+        return lax.ppermute(value, "heads", swap)
+
+    part_rows = -(-ALL_PACKED // (16 * dp)) * 16
+    second_rows = (part_rows + 24) // 48 * 16
+    first_rows = part_rows - second_rows
     wide, tall = shift_tables()
     table = place_table()
     scratch = [
+        pltpu.VMEM((2, LAYERS, D, 3 * HW), BF),
+        pltpu.VMEM((2, LAYERS, 16, HW), F32),
         pltpu.VMEM((LAYERS + 1, rows, D), F32),
         pltpu.VMEM((LAYERS, 2, rows, D), BF),
         pltpu.VMEM((LAYERS, 2, rows, 3 * HW), BF),
@@ -737,26 +773,30 @@
         pltpu.VMEM((2, SMALL, HW), F32),
         pltpu.VMEM((2, part_rows * dp, HW), BF),
     ]
-    result, grad, packed = pl.pallas_call(
+    result, grad, *packed = pl.pallas_call(
         step_kernel,
         out_shape=(
             jax.ShapeDtypeStruct((tokens_here, D), BF),
             jax.ShapeDtypeStruct((tokens_here, D), F32),
-            jax.ShapeDtypeStruct((2, dp, LAYERS, part_rows, HW), BF),
+            *[jax.ShapeDtypeStruct((dp, some, HW), BF) for some in (first_rows, second_rows) * 2],
         ),
-        in_specs=[SMEM] + [VMEM] * 19,
-        out_specs=(VMEM,) * 3,
+        in_specs=[SMEM] + [VMEM] * 23,
+        out_specs=(VMEM,) * 6,
         scratch_shapes=scratch,
         compiler_params=pltpu.CompilerParams(vmem_limit_bytes=60 * 1024 * 1024),
         name="step",
     )(
-        meta,
+        counts,
         tokens,
         cotangent,
         ln1_gain,
         ln1_bias,
-        wqkv_all,
-        lepe_all,
+        w_qkv,
+        across(w_qkv),
+        lepe_w,
+        across(lepe_w),
+        lepe_b,
+        across(lepe_b),
         w_proj,
         b_proj,
         ln2_gain,
@@ -778,30 +818,35 @@
             total = total + item.astype(F32)
         return total.astype(BF)
 
-    swap = [(0, 1), (1, 0)]
-    own = add(packed[0], lax.ppermute(packed[1], "heads", swap))
-    digits = []
-    stride = 1
-    for size in digit_sizes(dp):
-        digits.append((size, stride))
-        stride *= size
-    for size, stride in digits:
-        pieces = own.reshape((size, own.shape[0] // size) + own.shape[1:])
-        arrived = [
-            lax.ppermute(pieces[step], "dp", [(i, i ^ (step * stride)) for i in range(dp)])
-            for step in range(1, size)
-        ]
-        own = add(pieces[0], *arrived)
-    for size, stride in reversed(digits):
-        own = jnp.concatenate(
-            [own]
-            + [
-                lax.ppermute(own, "dp", [(i, i ^ (step * stride)) for i in range(dp)])
-                for step in range(1, size)
-            ],
-            axis=0,
-        )
-    other = lax.ppermute(own, "heads", swap)
+    own = [add(packed[place], across(packed[2 + place])) for place in range(2)]
+    orders = [digits_of(dp, place) for place in range(2)]
+
+    def exchange(step, pieces_of):
+        sent = []
+        for place in (1, 0):
+            size, stride = orders[place][step]
+            pieces = pieces_of(place, size)
+            for hop in range(size - 1, 0, -1):
+                pairs = [(device, device ^ (hop * stride)) for device in range(dp)]
+                sent.append((place, hop, lax.ppermute(pieces[hop], "dp", pairs)))
+        arrived = lax.optimization_barrier(tuple(item[2] for item in sent))
+        got = [{}, {}]
+        for (place, hop, _), value in zip(sent, arrived):
+            got[place][hop] = value
+        return [[got[place][hop] for hop in sorted(got[place])] for place in range(2)]
+
+    for step in range(len(orders[0])):
+
+        def cut(place, size):
+            value = own[place]
+            return value.reshape((size, value.shape[0] // size) + value.shape[1:])
+
+        arrived = exchange(step, cut)
+        own = [add(cut(place, orders[place][step][0])[0], *arrived[place]) for place in range(2)]
+    for step in reversed(range(len(orders[0]))):
+        arrived = exchange(step, lambda place, size: [own[place]] * size)
+        own = [jnp.concatenate([own[place]] + arrived[place], axis=0) for place in range(2)]
+    other = [across(value) for value in own]
     grads = pl.pallas_call(
         unpack_kernel,
         out_shape=(
@@ -819,12 +864,12 @@
             jax.ShapeDtypeStruct((LAYERS, FF, D), F32),
             jax.ShapeDtypeStruct((LAYERS, D), F32),
         ),
-        in_specs=[SMEM] + [VMEM] * 2,
+        in_specs=[VMEM] * 4,
         out_specs=(VMEM,) * 13,
         scratch_shapes=[pltpu.VMEM((2, part_rows * dp, HW), BF)],
         compiler_params=pltpu.CompilerParams(vmem_limit_bytes=48 * 1024 * 1024),
         name="unpack",
-    )(meta, own, other)
+    )(*own, *other)
     return (result, grad) + tuple(grads)
 
 

time: 167 us -> 147 us (0.88)
  waiting for transfers between devices: 60.9 us -> 24.4 us
  starting transfers between devices: 16.8 us -> 45.6 us
  blocking collectives: 8.44 us -> 0 us
  Pallas kernels: 73 us -> 70.9 us
    ppermute x14 -> x31, waiting for transfers between devices: 60.9 us -> 24.4 us  [the longest x24 17.3 us: exchange(): sent.append((place, hop, lax.ppermute(pieces[hop], 'dp', pairs)))]
    ppermute x14 -> x31, starting transfers between devices: 16.8 us -> 45.6 us  [the longest x24 43.4 us: exchange(): sent.append((place, hop, lax.ppermute(pieces[hop], 'dp', pairs)))]
    all_gather x2 -> x0, blocking collectives: 8.44 us -> none  [the longest x1 6.36 us: shards(): wqkv_all = lax.all_gather(w_qkv.reshape(LAYERS, D, 3 * HW), 'heads', axis=0)]
    squeeze x1 -> x0, local copies, waits for them, and re-layouts: 1.72 us -> none  [shards(): own = add(packed[0], lax.ppermute(packed[1], 'heads', swap))]
  transfers between devices with their start and end apart: 14 -> 31, of which waited for: 12 -> 11; matrix products, arithmetic and copies ran while one was open for 0% -> 1% of each run, Pallas kernels for 0% -> 0%
where the time goes in v3:
time: 147 us
  Pallas kernels  70.9 us (48%)
  starting transfers between devices  45.6 us (31%)
  waiting for transfers between devices  24.4 us (17%)
  local copies, waits for them, and re-layouts  2.99 us (2%)
  other arithmetic  1.85 us (1%)
    pallas_call x1, Pallas kernels, shards(): pl.pallas_call(step_kernel, out_shape=(jax.ShapeDtypeStruct((tokens_here,...  67.6 us
    ppermute x24, starting transfers between devices, exchange(): sent.append((place, hop, lax.ppermute(pieces[hop], 'dp', pairs)))  43.4 us
    ppermute x24, waiting for transfers between devices, exchange(): sent.append((place, hop, lax.ppermute(pieces[hop], 'dp', pairs)))  17.3 us
    ppermute x7, waiting for transfers between devices, across(): return lax.ppermute(value, 'heads', swap)  7.06 us
    pallas_call x1, Pallas kernels, shards(): pl.pallas_call(unpack_kernel, out_shape=(jax.ShapeDtypeStruct((LAYERS, D)...  3.29 us
  transfers between devices with their start and end apart: 31, of which 11 were waited for; matrix products, arithmetic and copies ran while one was open for 1% of the time, Pallas kernels for 0%

profile of v3, /device:TPU:0, one launch (start us, length us, event | category | flops | bytes accessed | tf_op | source)
XLA Modules:
  0.0 146.6 jit_solution(12831404962459400657)
XLA Ops:
  0.6 0.5 collective-permute-start
  1.2 0.7 copy.37.own_lepe_ref
  1.9 0.1 collective-permute-start.1
  1.9 0.5 collective-permute-start.2
  2.4 1.0 collective-permute-done.2.other_lepeb_ref
  3.4 0.0 collective-permute-done.1.other_lepe_ref
  3.4 0.0 collective-permute-done.other_wqkv_ref
  3.4 0.5 copy-done.4
  4.0 0.0 copy-done.3
  4.0 0.7 copy-done.1
  4.7 67.6 %step.1 = (bf16[1216,256]{1,0:T(8,128)(2,1)}, f32[1216,256]{1,0:T(8,128)}, bf16[16,272,128]{2,1,0:T(8,128)(2,1)}, bf16[16,128,128]{2,1,0:T(8,128)(2,1)}, bf16[16...) custom-call(s32[4]{0:T(128)} %counts_ref.1, bf16[1216,256]{1,0:T(8,128)(2,1)} %tok_ref.1, ...), custom_call_target="tpu_custom_call" | custom-call | tf_op jit(solution)/shard_map/step/pallas_call | solution.py:776
  72.4 0.0 copy-start
  72.4 0.4 collective-permute-start.3
  72.8 0.2 collective-permute-start.4
  73.0 3.2 %collective-permute-done.4 = bf16[16,128,128]{2,1,0:T(8,128)(2,1)S(1)} collective-permute-done((bf16[16,128,128]{2,1,0:T(8,128)(2,1)}, bf16[16,128,128]{2,1,0:T(8,128)(2,1)S(1)}, u32[]{:S(2)}, u32[]{:S(2)}) %collective-permute-start.4) | collective-permute-done | bytes 524320 | tf_op jit(solution)/shard_map/ppermute | solution.py:747
  76.2 1.2 add_convert_fusion.1
  77.4 0.0 collective-permute-done.3
  77.4 0.3 add_convert_fusion
  77.7 0.1 fusion
  77.7 2.9 %collective-permute-start.10 = (bf16[4,272,128]{2,1,0:T(8,128)(2,1)S(1)}, bf16[4,272,128]{2,1,0:T(8,128)(2,1)S(1)}, u32[]{:S(2)}, u32[]{:S(2)}) collective-permute-start(bf16[4,272,128]{2,1,0:T(8,128)(2,1)S(1)} %get-tuple-element.120), channel_id=1, source_target_pairs={{0,2},{2,0},{4,6},{6,4},{8,10},{10,8},{12,14},{14,12},{16,18},{18,... | collective-permute-start | bytes 835592 | tf_op jit(solution)/shard_map/ppermute | solution.py:831
  80.6 1.5 %collective-permute-start.9 = (bf16[4,272,128]{2,1,0:T(8,128)(2,1)S(1)}, bf16[4,272,128]{2,1,0:T(8,128)(2,1)S(1)}, u32[]{:S(2)}, u32[]{:S(2)}) collective-permute-start(bf16[4,272,128]{2,1,0:T(8,128)(2,1)S(1)} %get-tuple-element.121), channel_id=1, source_target_pairs={{0,4},{2,6},{4,0},{6,2},{8,12},{10,14},{12,8},{14,10},{16,20},{18,... | collective-permute-start | bytes 835592 | tf_op jit(solution)/shard_map/ppermute | solution.py:831
  82.1 0.0 collective-permute-start.8
  82.2 2.1 %collective-permute-start.7 = (bf16[4,128,128]{2,1,0:T(8,128)(2,1)S(1)}, bf16[4,128,128]{2,1,0:T(8,128)(2,1)S(1)}, u32[]{:S(2)}, u32[]{:S(2)}) collective-permute-start(bf16[4,128,128]{2,1,0:T(8,128)(2,1)S(1)} %get-tuple-element.123), channel_id=1, source_target_pairs={{0,8},{2,10},{4,12},{6,14},{8,0},{10,2},{12,4},{14,6},{16,24},{18,... | collective-permute-start | bytes 393224 | tf_op jit(solution)/shard_map/ppermute | solution.py:831
  84.3 2.6 %collective-permute-start.6 = (bf16[4,128,128]{2,1,0:T(8,128)(2,1)S(1)}, bf16[4,128,128]{2,1,0:T(8,128)(2,1)S(1)}, u32[]{:S(2)}, u32[]{:S(2)}) collective-permute-start(bf16[4,128,128]{2,1,0:T(8,128)(2,1)S(1)} %get-tuple-element.124), channel_id=1, source_target_pairs={{0,16},{2,18},{4,20},{6,22},{8,24},{10,26},{12,28},{14,30},{16,0},... | collective-permute-start | bytes 393224 | tf_op jit(solution)/shard_map/ppermute | solution.py:831
  86.9 1.7 %collective-permute-done.7 = bf16[4,128,128]{2,1,0:T(8,128)(2,1)S(1)} collective-permute-done((bf16[4,128,128]{2,1,0:T(8,128)(2,1)S(1)}, bf16[4,128,128]{2,1,0:T(8,128)(2,1)S(1)}, u32[]{:S(2)}, u32[]{:S(2)}) %collective-permute-start.7) | collective-permute-done | bytes 131104 | tf_op jit(solution)/shard_map/ppermute | solution.py:831
  88.6 4.1 %collective-permute-start.5 = (bf16[4,128,128]{2,1,0:T(8,128)(2,1)S(1)}, bf16[4,128,128]{2,1,0:T(8,128)(2,1)S(1)}, u32[]{:S(2)}, u32[]{:S(2)}) collective-permute-start(bf16[4,128,128]{2,1,0:T(8,128)(2,1)S(1)} %get-tuple-element.125), channel_id=1, source_target_pairs={{0,24},{2,26},{4,28},{6,30},{8,16},{10,18},{12,20},{14,22},{16,8},... | collective-permute-start | bytes 393224 | tf_op jit(solution)/shard_map/ppermute | solution.py:831
  92.7 3.5 %collective-permute-done.6 = bf16[4,128,128]{2,1,0:T(8,128)(2,1)S(1)} collective-permute-done((bf16[4,128,128]{2,1,0:T(8,128)(2,1)S(1)}, bf16[4,128,128]{2,1,0:T(8,128)(2,1)S(1)}, u32[]{:S(2)}, u32[]{:S(2)}) %collective-permute-start.6) | collective-permute-done | bytes 131104 | tf_op jit(solution)/shard_map/ppermute | solution.py:831
  96.2 0.0 collective-permute-done.5
  96.2 0.0 collective-permute-done.9
  96.3 0.0 collective-permute-done.8
  96.3 0.2 add_convert_fusion.2
  96.5 2.5 %collective-permute-start.16 = (bf16[1,272,128]{2,1,0:T(8,128)(2,1)S(1)}, bf16[1,272,128]{2,1,0:T(8,128)(2,1)S(1)}, u32[]{:S(2)}, u32[]{:S(2)}) collective-permute-start(bf16[1,272,128]{2,1,0:T(8,128)(2,1)S(1)} %get-tuple-element.126), channel_id=1, source_target_pairs={{0,8},{2,10},{4,12},{6,14},{8,0},{10,2},{12,4},{14,6},{16,24},{18,... | collective-permute-start | bytes 208904 | tf_op jit(solution)/shard_map/ppermute | solution.py:831
  99.0 1.5 %collective-permute-start.15 = (bf16[1,272,128]{2,1,0:T(8,128)(2,1)S(1)}, bf16[1,272,128]{2,1,0:T(8,128)(2,1)S(1)}, u32[]{:S(2)}, u32[]{:S(2)}) collective-permute-start(bf16[1,272,128]{2,1,0:T(8,128)(2,1)S(1)} %get-tuple-element.127), channel_id=1, source_target_pairs={{0,16},{2,18},{4,20},{6,22},{8,24},{10,26},{12,28},{14,30},{16,0},... | collective-permute-start | bytes 208904 | tf_op jit(solution)/shard_map/ppermute | solution.py:831
  100.5 1.0 collective-permute-start.14
  101.4 0.1 add_convert_fusion.3
  101.5 1.6 %collective-permute-start.13 = (bf16[1,128,128]{2,1,0:T(8,128)(2,1)S(1)}, bf16[1,128,128]{2,1,0:T(8,128)(2,1)S(1)}, u32[]{:S(2)}, u32[]{:S(2)}) collective-permute-start(bf16[1,128,128]{2,1,0:T(8,128)(2,1)S(1)} %get-tuple-element.129), channel_id=1, source_target_pairs={{0,2},{2,0},{4,6},{6,4},{8,10},{10,8},{12,14},{14,12},{16,18},{18,... | collective-permute-start | bytes 98312 | tf_op jit(solution)/shard_map/ppermute | solution.py:831
  103.1 1.5 %collective-permute-start.12 = (bf16[1,128,128]{2,1,0:T(8,128)(2,1)S(1)}, bf16[1,128,128]{2,1,0:T(8,128)(2,1)S(1)}, u32[]{:S(2)}, u32[]{:S(2)}) collective-permute-start(bf16[1,128,128]{2,1,0:T(8,128)(2,1)S(1)} %get-tuple-element.130), channel_id=1, source_target_pairs={{0,4},{2,6},{4,0},{6,2},{8,12},{10,14},{12,8},{14,10},{16,20},{18,... | collective-permute-start | bytes 98312 | tf_op jit(solution)/shard_map/ppermute | solution.py:831
  104.6 0.9 collective-permute-done.13
  105.5 2.4 %collective-permute-start.11 = (bf16[1,128,128]{2,1,0:T(8,128)(2,1)S(1)}, bf16[1,128,128]{2,1,0:T(8,128)(2,1)S(1)}, u32[]{:S(2)}, u32[]{:S(2)}) collective-permute-start(bf16[1,128,128]{2,1,0:T(8,128)(2,1)S(1)} %get-tuple-element.131), channel_id=1, source_target_pairs={{0,6},{2,4},{4,2},{6,0},{8,14},{10,12},{12,10},{14,8},{16,22},{18,... | collective-permute-start | bytes 98312 | tf_op jit(solution)/shard_map/ppermute | solution.py:831
  108.0 0.0 collective-permute-done.12
  108.0 2.4 %collective-permute-done.11 = bf16[1,128,128]{2,1,0:T(8,128)(2,1)S(1)} collective-permute-done((bf16[1,128,128]{2,1,0:T(8,128)(2,1)S(1)}, bf16[1,128,128]{2,1,0:T(8,128)(2,1)S(1)}, u32[]{:S(2)}, u32[]{:S(2)}) %collective-permute-start.11) | collective-permute-done | bytes 32800 | tf_op jit(solution)/shard_map/ppermute | solution.py:831
  110.4 1.1 collective-permute-start.22
  111.5 2.7 %collective-permute-start.21 = (bf16[1,272,128]{2,1,0:T(8,128)(2,1)S(1)}, bf16[1,272,128]{2,1,0:T(8,128)(2,1)S(1)}, u32[]{:S(2)}, u32[]{:S(2)}) collective-permute-start(bf16[1,272,128]{2,1,0:T(8,128)(2,1)S(1)} %get-tuple-element.119), channel_id=1, source_target_pairs={{0,16},{2,18},{4,20},{6,22},{8,24},{10,26},{12,28},{14,30},{16,0},... | collective-permute-start | bytes 208904 | tf_op jit(solution)/shard_map/ppermute | solution.py:831
  114.2 0.6 collective-permute-start.20
  114.9 1.6 %collective-permute-start.19 = (bf16[1,128,128]{2,1,0:T(8,128)(2,1)S(1)}, bf16[1,128,128]{2,1,0:T(8,128)(2,1)S(1)}, u32[]{:S(2)}, u32[]{:S(2)}) collective-permute-start(bf16[1,128,128]{2,1,0:T(8,128)(2,1)S(1)} %get-tuple-element.117), channel_id=1, source_target_pairs={{0,2},{2,0},{4,6},{6,4},{8,10},{10,8},{12,14},{14,12},{16,18},{18,... | collective-permute-start | bytes 98312 | tf_op jit(solution)/shard_map/ppermute | solution.py:831
  116.4 1.5 %collective-permute-start.18 = (bf16[1,128,128]{2,1,0:T(8,128)(2,1)S(1)}, bf16[1,128,128]{2,1,0:T(8,128)(2,1)S(1)}, u32[]{:S(2)}, u32[]{:S(2)}) collective-permute-start(bf16[1,128,128]{2,1,0:T(8,128)(2,1)S(1)} %get-tuple-element.117), channel_id=1, source_target_pairs={{0,4},{2,6},{4,0},{6,2},{8,12},{10,14},{12,8},{14,10},{16,20},{18,... | collective-permute-start | bytes 98312 | tf_op jit(solution)/shard_map/ppermute | solution.py:831
  118.0 0.9 collective-permute-done.19
  118.9 2.4 %collective-permute-start.17 = (bf16[1,128,128]{2,1,0:T(8,128)(2,1)S(1)}, bf16[1,128,128]{2,1,0:T(8,128)(2,1)S(1)}, u32[]{:S(2)}, u32[]{:S(2)}) collective-permute-start(bf16[1,128,128]{2,1,0:T(8,128)(2,1)S(1)} %get-tuple-element.117), channel_id=1, source_target_pairs={{0,6},{2,4},{4,2},{6,0},{8,14},{10,12},{12,10},{14,8},{16,22},{18,... | collective-permute-start | bytes 98312 | tf_op jit(solution)/shard_map/ppermute | solution.py:831
  121.3 2.7 %collective-permute-done.17 = bf16[1,128,128]{2,1,0:T(8,128)(2,1)S(1)} collective-permute-done((bf16[1,128,128]{2,1,0:T(8,128)(2,1)S(1)}, bf16[1,128,128]{2,1,0:T(8,128)(2,1)S(1)}, u32[]{:S(2)}, u32[]{:S(2)}) %collective-permute-start.17) | collective-permute-done | bytes 32800 | tf_op jit(solution)/shard_map/ppermute | solution.py:831
  124.0 0.2 collective-permute-start.25
  124.2 3.8 %collective-permute-start.24 = (bf16[4,128,128]{2,1,0:T(8,128)(2,1)S(1)}, bf16[4,128,128]{2,1,0:T(8,128)(2,1)S(1)}, u32[]{:S(2)}, u32[]{:S(2)}) collective-permute-start(bf16[4,128,128]{2,1,0:T(8,128)(2,1)S(1)} %pad_maximum_fusion.1), channel_id=1, source_target_pairs={{0,16},{2,18},{4,20},{6,22},{8,24},{10,26},{12,28},{14,30},{16,0},... | collective-permute-start | bytes 393224 | tf_op jit(solution)/shard_map/ppermute | solution.py:831
  128.0 1.5 %collective-permute-start.28 = (bf16[4,272,128]{2,1,0:T(8,128)(2,1)S(1)}, bf16[4,272,128]{2,1,0:T(8,128)(2,1)S(1)}, u32[]{:S(2)}, u32[]{:S(2)}) collective-permute-start(bf16[4,272,128]{2,1,0:T(8,128)(2,1)S(1)} %pad_maximum_fusion), channel_id=1, source_target_pairs={{0,2},{2,0},{4,6},{6,4},{8,10},{10,8},{12,14},{14,12},{16,18},{18,... | collective-permute-start | bytes 835592 | tf_op jit(solution)/shard_map/ppermute | solution.py:831
  129.5 1.3 collective-permute-start.27
  130.7 0.8 collective-permute-start.26
  131.5 0.0 collective-permute-done.25
  131.6 2.2 %collective-permute-start.23 = (bf16[4,128,128]{2,1,0:T(8,128)(2,1)S(1)}, bf16[4,128,128]{2,1,0:T(8,128)(2,1)S(1)}, u32[]{:S(2)}, u32[]{:S(2)}) collective-permute-start(bf16[4,128,128]{2,1,0:T(8,128)(2,1)S(1)} %pad_maximum_fusion.1), channel_id=1, source_target_pairs={{0,24},{2,26},{4,28},{6,30},{8,16},{10,18},{12,20},{14,22},{16,8},... | collective-permute-start | bytes 393224 | tf_op jit(solution)/shard_map/ppermute | solution.py:831
  133.8 4.6 %collective-permute-done.23 = bf16[4,128,128]{2,1,0:T(8,128)(2,1)S(1)} collective-permute-done((bf16[4,128,128]{2,1,0:T(8,128)(2,1)S(1)}, bf16[4,128,128]{2,1,0:T(8,128)(2,1)S(1)}, u32[]{:S(2)}, u32[]{:S(2)}) %collective-permute-start.23) | collective-permute-done | bytes 131104 | tf_op jit(solution)/shard_map/ppermute | solution.py:831
  138.4 0.6 collective-permute-done.27
  139.0 0.0 collective-permute-done.26
  139.1 0.1 collective-permute-start.29
  139.3 0.5 collective-permute-start.30
  139.9 2.8 %collective-permute-done.30.other_second_ref = bf16[16,128,128]{2,1,0:T(8,128)(2,1)S(1)} collective-permute-done((bf16[16,128,128]{2,1,0:T(8,128)(2,1)S(1)}, bf16[16,128,128]{2,1,0:T(8,128)(2,1)S(1)}, u32[]{:S(2)}, u32[]{:S(2)}) %collective-permute-start.30) | collective-permute-done | bytes 524320 | tf_op jit(solution)/shard_map/ppermute | solution.py:747
  142.7 3.3 %unpack.1 = (f32[2,256]{1,0:T(2,128)}, f32[2,256]{1,0:T(2,128)}, f32[2,1,256,384]{3,2,1,0:T(8,128)}, f32[2,1,9,128]{3,2,1,0:T(8,128)S(1)}, f32[2,1,128]{2,1,0:T(...) custom-call(bf16[16,272,128]{2,1,0:T(8,128)(2,1)S(1)} %constant_dyna, ...), custom_call_target="tpu_custom_call" | custom-call | tf_op jit(solution)/shard_map/unpack/pallas_call | solution.py:850
  146.0 0.6 copy.38
  (36 shorter events, 0.5 us)
Async XLA Ops:
  0.6 2.8 %collective-permute-start = (bf16[2,1,256,384]{3,2,1,0:T(8,128)(2,1)}, bf16[2,1,256,384]{3,2,1,0:T(8,128)(2,1)S(1)}, u32[]{:S(2)}, u32[]{:S(2)}) collective-permute-start(bf16[2,1,256,384]{3,2,1,0:T(8,128)(2,1)} %own_wqkv_ref.1), channel_id=1, source_target_pairs={{0,1},{1,0},{2,3},{3,2},{4,5},{5,4},{6,7},{7,6},{8,9},{9,8},{10,11... | collective-permute-start | bytes 1179656 | tf_op jit(solution)/shard_map/ppermute | solution.py:747
  1.9 1.6 %copy-start.2 = (f32[2,1,9,128]{3,2,1,0:T(8,128)}, f32[2,1,9,128]{3,2,1,0:T(8,128)S(1)}, u32[]{:S(2)}) copy-start(f32[2,1,9,128]{3,2,1,0:T(8,128)S(1)} %copy.37.own_lepe_ref) | copy-start | bytes 27652
  1.9 1.5 %collective-permute-start.1 = (f32[2,1,9,128]{3,2,1,0:T(8,128)S(1)}, f32[2,1,9,128]{3,2,1,0:T(8,128)S(1)}, u32[]{:S(2)}, u32[]{:S(2)}) collective-permute-start(f32[2,1,9,128]{3,2,1,0:T(8,128)S(1)} %copy.37.own_lepe_ref), channel_id=1, source_target_pairs={{0,1},{1,0},{2,3},{3,2},{4,5},{5,4},{6,7},{7,6},{8,9},{9,8},{10,11... | collective-permute-start | bytes 27656 | tf_op jit(solution)/shard_map/ppermute | solution.py:747
  1.9 1.5 %collective-permute-start.2 = (f32[2,1,128]{2,1,0:T(1,128)}, f32[2,1,128]{2,1,0:T(1,128)S(1)}, u32[]{:S(2)}, u32[]{:S(2)}) collective-permute-start(f32[2,1,128]{2,1,0:T(1,128)} %own_lepeb_ref.1), channel_id=1, source_target_pairs={{0,1},{1,0},{2,3},{3,2},{4,5},{5,4},{6,7},{7,6},{8,9},{9,8},{10,11... | collective-permute-start | bytes 3080 | tf_op jit(solution)/shard_map/ppermute | solution.py:747
  3.4 0.6 copy-start.4
  3.4 0.6 copy-start.3
  4.0 0.7 copy-start.1
  72.4 5.0 %copy-start = (bf16[16,272,128]{2,1,0:T(8,128)(2,1)S(1)}, bf16[16,272,128]{2,1,0:T(8,128)(2,1)}, u32[]{:S(2)}) copy-start(bf16[16,272,128]{2,1,0:T(8,128)(2,1)} %get-tuple-element.60) | copy-start | bytes 3342340
  72.4 5.0 %collective-permute-start.3 = (bf16[16,272,128]{2,1,0:T(8,128)(2,1)}, bf16[16,272,128]{2,1,0:T(8,128)(2,1)S(1)}, u32[]{:S(2)}, u32[]{:S(2)}) collective-permute-start(bf16[16,272,128]{2,1,0:T(8,128)(2,1)} %get-tuple-element.61), channel_id=1, source_target_pairs={{0,1},{1,0},{2,3},{3,2},{4,5},{5,4},{6,7},{7,6},{8,9},{9,8},{10,11... | collective-permute-start | bytes 3342344 | tf_op jit(solution)/shard_map/ppermute | solution.py:747
  72.8 3.4 %collective-permute-start.4 = (bf16[16,128,128]{2,1,0:T(8,128)(2,1)}, bf16[16,128,128]{2,1,0:T(8,128)(2,1)S(1)}, u32[]{:S(2)}, u32[]{:S(2)}) collective-permute-start(bf16[16,128,128]{2,1,0:T(8,128)(2,1)} %get-tuple-element.63), channel_id=1, source_target_pairs={{0,1},{1,0},{2,3},{3,2},{4,5},{5,4},{6,7},{7,6},{8,9},{9,8},{10,11... | collective-permute-start | bytes 1572872 | tf_op jit(solution)/shard_map/ppermute | solution.py:747
  77.7 18.5 %collective-permute-start.10 = (bf16[4,272,128]{2,1,0:T(8,128)(2,1)S(1)}, bf16[4,272,128]{2,1,0:T(8,128)(2,1)S(1)}, u32[]{:S(2)}, u32[]{:S(2)}) collective-permute-start(bf16[4,272,128]{2,1,0:T(8,128)(2,1)S(1)} %get-tuple-element.120), channel_id=1, source_target_pairs={{0,2},{2,0},{4,6},{6,4},{8,10},{10,8},{12,14},{14,12},{16,18},{18,... | collective-permute-start | bytes 835592 | tf_op jit(solution)/shard_map/ppermute | solution.py:831
  80.6 15.6 %collective-permute-start.9 = (bf16[4,272,128]{2,1,0:T(8,128)(2,1)S(1)}, bf16[4,272,128]{2,1,0:T(8,128)(2,1)S(1)}, u32[]{:S(2)}, u32[]{:S(2)}) collective-permute-start(bf16[4,272,128]{2,1,0:T(8,128)(2,1)S(1)} %get-tuple-element.121), channel_id=1, source_target_pairs={{0,4},{2,6},{4,0},{6,2},{8,12},{10,14},{12,8},{14,10},{16,20},{18,... | collective-permute-start | bytes 835592 | tf_op jit(solution)/shard_map/ppermute | solution.py:831
  82.1 14.1 %collective-permute-start.8 = (bf16[4,272,128]{2,1,0:T(8,128)(2,1)S(1)}, bf16[4,272,128]{2,1,0:T(8,128)(2,1)S(1)}, u32[]{:S(2)}, u32[]{:S(2)}) collective-permute-start(bf16[4,272,128]{2,1,0:T(8,128)(2,1)S(1)} %get-tuple-element.122), channel_id=1, source_target_pairs={{0,6},{2,4},{4,2},{6,0},{8,14},{10,12},{12,10},{14,8},{16,22},{18,... | collective-permute-start | bytes 835592 | tf_op jit(solution)/shard_map/ppermute | solution.py:831
  82.2 6.4 %collective-permute-start.7 = (bf16[4,128,128]{2,1,0:T(8,128)(2,1)S(1)}, bf16[4,128,128]{2,1,0:T(8,128)(2,1)S(1)}, u32[]{:S(2)}, u32[]{:S(2)}) collective-permute-start(bf16[4,128,128]{2,1,0:T(8,128)(2,1)S(1)} %get-tuple-element.123), channel_id=1, source_target_pairs={{0,8},{2,10},{4,12},{6,14},{8,0},{10,2},{12,4},{14,6},{16,24},{18,... | collective-permute-start | bytes 393224 | tf_op jit(solution)/shard_map/ppermute | solution.py:831
  84.3 11.9 %collective-permute-start.6 = (bf16[4,128,128]{2,1,0:T(8,128)(2,1)S(1)}, bf16[4,128,128]{2,1,0:T(8,128)(2,1)S(1)}, u32[]{:S(2)}, u32[]{:S(2)}) collective-permute-start(bf16[4,128,128]{2,1,0:T(8,128)(2,1)S(1)} %get-tuple-element.124), channel_id=1, source_target_pairs={{0,16},{2,18},{4,20},{6,22},{8,24},{10,26},{12,28},{14,30},{16,0},... | collective-permute-start | bytes 393224 | tf_op jit(solution)/shard_map/ppermute | solution.py:831
  88.6 7.6 %collective-permute-start.5 = (bf16[4,128,128]{2,1,0:T(8,128)(2,1)S(1)}, bf16[4,128,128]{2,1,0:T(8,128)(2,1)S(1)}, u32[]{:S(2)}, u32[]{:S(2)}) collective-permute-start(bf16[4,128,128]{2,1,0:T(8,128)(2,1)S(1)} %get-tuple-element.125), channel_id=1, source_target_pairs={{0,24},{2,26},{4,28},{6,30},{8,16},{10,18},{12,20},{14,22},{16,8},... | collective-permute-start | bytes 393224 | tf_op jit(solution)/shard_map/ppermute | solution.py:831
  96.5 13.9 %collective-permute-start.16 = (bf16[1,272,128]{2,1,0:T(8,128)(2,1)S(1)}, bf16[1,272,128]{2,1,0:T(8,128)(2,1)S(1)}, u32[]{:S(2)}, u32[]{:S(2)}) collective-permute-start(bf16[1,272,128]{2,1,0:T(8,128)(2,1)S(1)} %get-tuple-element.126), channel_id=1, source_target_pairs={{0,8},{2,10},{4,12},{6,14},{8,0},{10,2},{12,4},{14,6},{16,24},{18,... | collective-permute-start | bytes 208904 | tf_op jit(solution)/shard_map/ppermute | solution.py:831
  99.0 11.4 %collective-permute-start.15 = (bf16[1,272,128]{2,1,0:T(8,128)(2,1)S(1)}, bf16[1,272,128]{2,1,0:T(8,128)(2,1)S(1)}, u32[]{:S(2)}, u32[]{:S(2)}) collective-permute-start(bf16[1,272,128]{2,1,0:T(8,128)(2,1)S(1)} %get-tuple-element.127), channel_id=1, source_target_pairs={{0,16},{2,18},{4,20},{6,22},{8,24},{10,26},{12,28},{14,30},{16,0},... | collective-permute-start | bytes 208904 | tf_op jit(solution)/shard_map/ppermute | solution.py:831
  100.5 9.9 %collective-permute-start.14 = (bf16[1,272,128]{2,1,0:T(8,128)(2,1)S(1)}, bf16[1,272,128]{2,1,0:T(8,128)(2,1)S(1)}, u32[]{:S(2)}, u32[]{:S(2)}) collective-permute-start(bf16[1,272,128]{2,1,0:T(8,128)(2,1)S(1)} %get-tuple-element.128), channel_id=1, source_target_pairs={{0,24},{2,26},{4,28},{6,30},{8,16},{10,18},{12,20},{14,22},{16,8},... | collective-permute-start | bytes 208904 | tf_op jit(solution)/shard_map/ppermute | solution.py:831
  101.5 4.0 %collective-permute-start.13 = (bf16[1,128,128]{2,1,0:T(8,128)(2,1)S(1)}, bf16[1,128,128]{2,1,0:T(8,128)(2,1)S(1)}, u32[]{:S(2)}, u32[]{:S(2)}) collective-permute-start(bf16[1,128,128]{2,1,0:T(8,128)(2,1)S(1)} %get-tuple-element.129), channel_id=1, source_target_pairs={{0,2},{2,0},{4,6},{6,4},{8,10},{10,8},{12,14},{14,12},{16,18},{18,... | collective-permute-start | bytes 98312 | tf_op jit(solution)/shard_map/ppermute | solution.py:831
  103.1 4.9 %collective-permute-start.12 = (bf16[1,128,128]{2,1,0:T(8,128)(2,1)S(1)}, bf16[1,128,128]{2,1,0:T(8,128)(2,1)S(1)}, u32[]{:S(2)}, u32[]{:S(2)}) collective-permute-start(bf16[1,128,128]{2,1,0:T(8,128)(2,1)S(1)} %get-tuple-element.130), channel_id=1, source_target_pairs={{0,4},{2,6},{4,0},{6,2},{8,12},{10,14},{12,8},{14,10},{16,20},{18,... | collective-permute-start | bytes 98312 | tf_op jit(solution)/shard_map/ppermute | solution.py:831
  105.5 4.8 %collective-permute-start.11 = (bf16[1,128,128]{2,1,0:T(8,128)(2,1)S(1)}, bf16[1,128,128]{2,1,0:T(8,128)(2,1)S(1)}, u32[]{:S(2)}, u32[]{:S(2)}) collective-permute-start(bf16[1,128,128]{2,1,0:T(8,128)(2,1)S(1)} %get-tuple-element.131), channel_id=1, source_target_pairs={{0,6},{2,4},{4,2},{6,0},{8,14},{10,12},{12,10},{14,8},{16,22},{18,... | collective-permute-start | bytes 98312 | tf_op jit(solution)/shard_map/ppermute | solution.py:831
  110.4 13.6 %collective-permute-start.22 = (bf16[1,272,128]{2,1,0:T(8,128)(2,1)S(1)}, bf16[1,272,128]{2,1,0:T(8,128)(2,1)S(1)}, u32[]{:S(2)}, u32[]{:S(2)}) collective-permute-start(bf16[1,272,128]{2,1,0:T(8,128)(2,1)S(1)} %get-tuple-element.119), channel_id=1, source_target_pairs={{0,8},{2,10},{4,12},{6,14},{8,0},{10,2},{12,4},{14,6},{16,24},{18,... | collective-permute-start | bytes 208904 | tf_op jit(solution)/shard_map/ppermute | solution.py:831
  111.5 12.5 %collective-permute-start.21 = (bf16[1,272,128]{2,1,0:T(8,128)(2,1)S(1)}, bf16[1,272,128]{2,1,0:T(8,128)(2,1)S(1)}, u32[]{:S(2)}, u32[]{:S(2)}) collective-permute-start(bf16[1,272,128]{2,1,0:T(8,128)(2,1)S(1)} %get-tuple-element.119), channel_id=1, source_target_pairs={{0,16},{2,18},{4,20},{6,22},{8,24},{10,26},{12,28},{14,30},{16,0},... | collective-permute-start | bytes 208904 | tf_op jit(solution)/shard_map/ppermute | solution.py:831
  114.2 9.8 %collective-permute-start.20 = (bf16[1,272,128]{2,1,0:T(8,128)(2,1)S(1)}, bf16[1,272,128]{2,1,0:T(8,128)(2,1)S(1)}, u32[]{:S(2)}, u32[]{:S(2)}) collective-permute-start(bf16[1,272,128]{2,1,0:T(8,128)(2,1)S(1)} %get-tuple-element.119), channel_id=1, source_target_pairs={{0,24},{2,26},{4,28},{6,30},{8,16},{10,18},{12,20},{14,22},{16,8},... | collective-permute-start | bytes 208904 | tf_op jit(solution)/shard_map/ppermute | solution.py:831
  114.9 4.0 %collective-permute-start.19 = (bf16[1,128,128]{2,1,0:T(8,128)(2,1)S(1)}, bf16[1,128,128]{2,1,0:T(8,128)(2,1)S(1)}, u32[]{:S(2)}, u32[]{:S(2)}) collective-permute-start(bf16[1,128,128]{2,1,0:T(8,128)(2,1)S(1)} %get-tuple-element.117), channel_id=1, source_target_pairs={{0,2},{2,0},{4,6},{6,4},{8,10},{10,8},{12,14},{14,12},{16,18},{18,... | collective-permute-start | bytes 98312 | tf_op jit(solution)/shard_map/ppermute | solution.py:831
  116.4 4.9 %collective-permute-start.18 = (bf16[1,128,128]{2,1,0:T(8,128)(2,1)S(1)}, bf16[1,128,128]{2,1,0:T(8,128)(2,1)S(1)}, u32[]{:S(2)}, u32[]{:S(2)}) collective-permute-start(bf16[1,128,128]{2,1,0:T(8,128)(2,1)S(1)} %get-tuple-element.117), channel_id=1, source_target_pairs={{0,4},{2,6},{4,0},{6,2},{8,12},{10,14},{12,8},{14,10},{16,20},{18,... | collective-permute-start | bytes 98312 | tf_op jit(solution)/shard_map/ppermute | solution.py:831
  118.9 5.1 %collective-permute-start.17 = (bf16[1,128,128]{2,1,0:T(8,128)(2,1)S(1)}, bf16[1,128,128]{2,1,0:T(8,128)(2,1)S(1)}, u32[]{:S(2)}, u32[]{:S(2)}) collective-permute-start(bf16[1,128,128]{2,1,0:T(8,128)(2,1)S(1)} %get-tuple-element.117), channel_id=1, source_target_pairs={{0,6},{2,4},{4,2},{6,0},{8,14},{10,12},{12,10},{14,8},{16,22},{18,... | collective-permute-start | bytes 98312 | tf_op jit(solution)/shard_map/ppermute | solution.py:831
  124.0 7.5 %collective-permute-start.25 = (bf16[4,128,128]{2,1,0:T(8,128)(2,1)S(1)}, bf16[4,128,128]{2,1,0:T(8,128)(2,1)S(1)}, u32[]{:S(2)}, u32[]{:S(2)}) collective-permute-start(bf16[4,128,128]{2,1,0:T(8,128)(2,1)S(1)} %pad_maximum_fusion.1), channel_id=1, source_target_pairs={{0,8},{2,10},{4,12},{6,14},{8,0},{10,2},{12,4},{14,6},{16,24},{18,... | collective-permute-start | bytes 393224 | tf_op jit(solution)/shard_map/ppermute | solution.py:831
  124.2 9.6 %collective-permute-start.24 = (bf16[4,128,128]{2,1,0:T(8,128)(2,1)S(1)}, bf16[4,128,128]{2,1,0:T(8,128)(2,1)S(1)}, u32[]{:S(2)}, u32[]{:S(2)}) collective-permute-start(bf16[4,128,128]{2,1,0:T(8,128)(2,1)S(1)} %pad_maximum_fusion.1), channel_id=1, source_target_pairs={{0,16},{2,18},{4,20},{6,22},{8,24},{10,26},{12,28},{14,30},{16,0},... | collective-permute-start | bytes 393224 | tf_op jit(solution)/shard_map/ppermute | solution.py:831
  128.0 10.4 %collective-permute-start.28 = (bf16[4,272,128]{2,1,0:T(8,128)(2,1)S(1)}, bf16[4,272,128]{2,1,0:T(8,128)(2,1)S(1)}, u32[]{:S(2)}, u32[]{:S(2)}) collective-permute-start(bf16[4,272,128]{2,1,0:T(8,128)(2,1)S(1)} %pad_maximum_fusion), channel_id=1, source_target_pairs={{0,2},{2,0},{4,6},{6,4},{8,10},{10,8},{12,14},{14,12},{16,18},{18,... | collective-permute-start | bytes 835592 | tf_op jit(solution)/shard_map/ppermute | solution.py:831
  129.5 9.5 %collective-permute-start.27 = (bf16[4,272,128]{2,1,0:T(8,128)(2,1)S(1)}, bf16[4,272,128]{2,1,0:T(8,128)(2,1)S(1)}, u32[]{:S(2)}, u32[]{:S(2)}) collective-permute-start(bf16[4,272,128]{2,1,0:T(8,128)(2,1)S(1)} %pad_maximum_fusion), channel_id=1, source_target_pairs={{0,4},{2,6},{4,0},{6,2},{8,12},{10,14},{12,8},{14,10},{16,20},{18,... | collective-permute-start | bytes 835592 | tf_op jit(solution)/shard_map/ppermute | solution.py:831
  130.7 8.3 %collective-permute-start.26 = (bf16[4,272,128]{2,1,0:T(8,128)(2,1)S(1)}, bf16[4,272,128]{2,1,0:T(8,128)(2,1)S(1)}, u32[]{:S(2)}, u32[]{:S(2)}) collective-permute-start(bf16[4,272,128]{2,1,0:T(8,128)(2,1)S(1)} %pad_maximum_fusion), channel_id=1, source_target_pairs={{0,6},{2,4},{4,2},{6,0},{8,14},{10,12},{12,10},{14,8},{16,22},{18,... | collective-permute-start | bytes 835592 | tf_op jit(solution)/shard_map/ppermute | solution.py:831
  131.6 6.8 %collective-permute-start.23 = (bf16[4,128,128]{2,1,0:T(8,128)(2,1)S(1)}, bf16[4,128,128]{2,1,0:T(8,128)(2,1)S(1)}, u32[]{:S(2)}, u32[]{:S(2)}) collective-permute-start(bf16[4,128,128]{2,1,0:T(8,128)(2,1)S(1)} %pad_maximum_fusion.1), channel_id=1, source_target_pairs={{0,24},{2,26},{4,28},{6,30},{8,16},{10,18},{12,20},{14,22},{16,8},... | collective-permute-start | bytes 393224 | tf_op jit(solution)/shard_map/ppermute | solution.py:831
  139.1 3.6 %collective-permute-start.29 = (bf16[16,272,128]{2,1,0:T(8,128)(2,1)S(1)}, bf16[16,272,128]{2,1,0:T(8,128)(2,1)S(1)}, u32[]{:S(2)}, u32[]{:S(2)}) collective-permute-start(bf16[16,272,128]{2,1,0:T(8,128)(2,1)S(1)} %constant_dynamic-update-slice_fusion.own_first_ref), channel_id=1, source_target_pairs={{0,1},{1,0},{2,3},{3,2},{4,5},{5,4},{6,7},{7,6},{8,9},{9,8},{10,11... | collective-permute-start | bytes 3342344 | tf_op jit(solution)/shard_map/ppermute | solution.py:747
  139.3 3.4 %collective-permute-start.30 = (bf16[16,128,128]{2,1,0:T(8,128)(2,1)S(1)}, bf16[16,128,128]{2,1,0:T(8,128)(2,1)S(1)}, u32[]{:S(2)}, u32[]{:S(2)}) collective-permute-start(bf16[16,128,128]{2,1,0:T(8,128)(2,1)S(1)} %constant_dynamic-update-slice_fusion.7.own_second_ref), channel_id=1, source_target_pairs={{0,1},{1,0},{2,3},{3,2},{4,5},{5,4},{6,7},{7,6},{8,9},{9,8},{10,11... | collective-permute-start | bytes 1572872 | tf_op jit(solution)/shard_map/ppermute | solution.py:747

commit v4 on v3

v4 whole, which is shorter than its diff:
```python
import functools
import math

import jax
import jax.numpy as jnp
import numpy as np
from jax import lax
from jax.experimental import pallas as pl
from jax.experimental.pallas import tpu as pltpu
from jax.sharding import PartitionSpec as P

D = 256
FF = 1024
HD = 32
GH = 4
HW = 128
LAYERS = 2
TOK_IMG = 608
SPLIT = 392
EPSILON = 1e-05

TILE = 8
TILES = 14
BLOCK = TILES * TILE
CHUNK = 2 * BLOCK
IMG = 6 * BLOCK
KEYS = 128
SPAN = GH * KEYS
TAPS = 9
SCALE = HD**-0.5
EXP_SCALE = SCALE * math.log2(math.e)
BF = jnp.bfloat16
F32 = jnp.float32

FC1_AT = 0
FC2_AT = 1024
PROJ_AT = 2048
QKV_AT = 2304
SMALL_AT = 3072
SMALL = 32
PACKED = SMALL_AT + SMALL
ALL_PACKED = LAYERS * PACKED


def place_table():
    table = np.zeros((IMG, TOK_IMG), np.float32)
    for crop in range(2):
        for row in range(14):
            for col in range(14):
                place = crop * CHUNK + row * 16 + (col // 7) * TILE + col % 7
                table[place, crop * 196 + row * 14 + col] = 1
    for group in range(2):
        for cell in range(108):
            table[2 * CHUNK + group * BLOCK + cell, SPLIT + group * 108 + cell] = 1
    return table


def window_cells(kind):
    cells = [None] * BLOCK
    if kind == 2:
        for place in range(108):
            cells[place] = (place // 36, place % 36 // 6, place % 6)
    else:
        for place in range(BLOCK):
            tile, col = divmod(place, TILE)
            if col < 7:
                cells[place] = (0, tile // 2, 7 * (tile % 2) + col) if kind == 0 else (0, tile, col)
    return cells


def shift_tables():
    wide = np.zeros((3, BLOCK, TAPS * KEYS), np.float32)
    tall = np.zeros((TAPS * BLOCK, KEYS), np.float32)
    for kind in range(3):
        cells = window_cells(kind)
        spots = {cell: place for place, cell in enumerate(cells) if cell is not None}
        for place, cell in enumerate(cells):
            for tap in range(TAPS):
                other = cell and spots.get((cell[0], cell[1] + tap // 3 - 1, cell[2] + tap % 3 - 1))
                if other is not None:
                    wide[kind, place, tap * KEYS + other] = 1
                    if kind == 2:
                        tall[tap * BLOCK + place, other] = 1
    return wide, tall


def bias_table():
    bias = np.full((2, BLOCK, KEYS), -1e30, np.float32)
    bias[0, [key for key in range(BLOCK) if key % TILE < 7]] = 0
    for query in range(KEYS):
        first, last = (36 * (query // 36), 36 * (query // 36) + 36) if query < 108 else (0, 108)
        bias[1, first:last, query] = 0
    return bias


def head_table():
    table = np.zeros((SPAN, HW), np.float32)
    for head in range(GH):
        table[head * KEYS : (head + 1) * KEYS, head * HD : (head + 1) * HD] = 1
    return table


def dot(left, right):
    return lax.dot_general(left, right, (((1,), (0,)), ((), ())), preferred_element_type=F32)


def dot_nt(left, right):
    return lax.dot_general(left, right, (((1,), (1,)), ((), ())), preferred_element_type=F32)


def dot_tn(left, right):
    return lax.dot_general(left, right, (((0,), (0,)), ((), ())), preferred_element_type=F32)


def norm_parts(value):
    center = value - jnp.mean(value, axis=-1, keepdims=True)
    scale = lax.rsqrt(jnp.mean(center * center, axis=-1, keepdims=True) + EPSILON)
    return center * scale, scale


def norm_back(dout, value, gain):
    xhat, scale = norm_parts(value)
    grown = dout * gain
    mean = jnp.mean(grown, axis=-1, keepdims=True)
    cross = jnp.mean(grown * xhat, axis=-1, keepdims=True)
    return scale * (grown - mean - xhat * cross), dout * xhat


def fold_rows(value):
    return jnp.sum(value.reshape(value.shape[0] // 8, 8, value.shape[1]), axis=0)


def head_rows(value, heads_ref):
    return jnp.concatenate(
        [value * heads_ref[head * KEYS : head * KEYS + 1, :] for head in range(GH)], axis=0
    )


def head_stack(value, heads_ref):
    rows = []
    pad = jnp.zeros((KEYS - BLOCK, HW), BF)
    for head in range(GH):
        rows.append(value * heads_ref[head * KEYS : head * KEYS + 1, :])
        rows.append(pad)
    return jnp.concatenate(rows, axis=0)


def pad_keys(value):
    return jnp.concatenate([value, jnp.zeros((KEYS - BLOCK, value.shape[1]), value.dtype)], axis=0)


def pipeline(stages, items, fillers=()):
    results = [None] * len(items)
    fillers = list(fillers)
    for step in range(len(items) + len(stages) - 1):
        if fillers:
            fillers.pop(0)()
        for place in range(len(stages)):
            item = step - place
            if 0 <= item < len(items):
                results[item] = stages[place](items[item], results[item])
    return results


def split_tiles(value):
    rows = value.shape[0] // 16
    return jnp.concatenate(
        [value[16 * row : 16 * row + 8] for row in range(rows)]
        + [value[16 * row + 8 : 16 * row + 16] for row in range(rows)],
        axis=0,
    )


def join_tiles(value):
    half = value.shape[0] // 2
    pieces = []
    for row in range(half // 8):
        pieces.append(value[8 * row : 8 * row + 8])
        pieces.append(value[half + 8 * row : half + 8 * row + 8])
    return jnp.concatenate(pieces, axis=0)


def as_tiles(value):
    return value.reshape(TILES, TILE, HW)


def live_tiles():
    return lax.broadcasted_iota(jnp.int32, (1, TILE, HW), 1) < TILE - 1


def side_cells(tiles, direction):
    if direction == 1:
        return pltpu.roll(tiles, 1, 1), tiles, pltpu.roll(tiles, TILE - 1, 1)
    last = lax.broadcasted_iota(jnp.int32, (1, TILE, HW), 1) == TILE - 1
    left, right = [], []
    for row in range(TILES // 2):
        near, far = tiles[2 * row : 2 * row + 1], tiles[2 * row + 1 : 2 * row + 2]
        near_left = pltpu.roll(near, 1, 1)
        far_right = pltpu.roll(far, TILE - 1, 1)
        left += [near_left, pltpu.roll(jnp.where(last, near_left, far), 1, 1)]
        right += [pltpu.roll(jnp.where(last, far_right, near), TILE - 1, 1), far_right]
    return jnp.concatenate(left, axis=0), tiles, jnp.concatenate(right, axis=0)


def tap_cells(tiles, direction):
    stride = 2 if direction == 0 else 1
    zeros = jnp.zeros((stride, TILE, HW), F32)
    padded = [jnp.concatenate([zeros, side, zeros], axis=0) for side in side_cells(tiles, direction)]
    return [padded[tap % 3][(tap // 3) * stride : (tap // 3) * stride + TILES] for tap in range(TAPS)]


def tap_row(direction, tap):
    return tap if direction == 0 else 3 * (tap % 3) + tap // 3


def compact(ref, image, value):
    first = image * TOK_IMG
    for tile in range(2 * 2 * TILES):
        ref[first + 7 * tile : first + 7 * tile + 7, :] = value[TILE * tile : TILE * tile + 7]
    for group in range(2):
        at = first + SPLIT + 108 * group
        row = 2 * CHUNK + BLOCK * group
        ref[at : at + 108, :] = value[row : row + 108]


def step_kernel(
    counts_ref,
    tok_ref,
    cot_from,
    g1_ref,
    b1_ref,
    own_wqkv_from,
    other_wqkv_from,
    own_lepe_ref,
    other_lepe_ref,
    own_lepeb_ref,
    other_lepeb_ref,
    wproj_from,
    bproj_ref,
    g2_ref,
    b2_ref,
    wfc1_from,
    bfc1_ref,
    wfc2_from,
    bfc2_ref,
    place_ref,
    wide_from,
    tall_from,
    bias_ref,
    heads_ref,
    out_ref,
    dtok_ref,
    keep_ref,
    send_ref,
    cot_ref,
    wproj_ref,
    wfc1_ref,
    half_wfc2_ref,
    wide_ref,
    tall_ref,
    fetched,
    handed,
    wqkv_ref,
    lepe_ref,
    h_ref,
    normed_ref,
    qkv_ref,
    probs_ref,
    hf_ref,
    hb_ref,
    inner_ref,
    normed2_ref,
    act_ref,
    slope_ref,
    dz_ref,
    dy_ref,
    dhid_ref,
    dqkv_ref,
    acc_ref,
    bfc1_sum_ref,
    accproj_ref,
    accqkv_ref,
    acclepe_ref,
    small_ref,
    stage_ref,
):
    rows_all = h_ref.shape[1]
    images = rows_all // IMG
    chunks = rows_all // CHUNK
    blocks = rows_all // BLOCK
    parts = keep_ref.shape[0]
    part_rows = keep_ref.shape[1]
    core = lax.axis_index("heads")
    mine = lax.axis_index("dp")
    moves = (
        (own_wqkv_from.at[:, 0], wqkv_ref.at[core]),
        (other_wqkv_from.at[:, 0], wqkv_ref.at[1 - core]),
        (wproj_from, wproj_ref),
        (wfc1_from, wfc1_ref),
        (wfc2_from, half_wfc2_ref),
        (wide_from, wide_ref),
        (cot_from, cot_ref),
        (tall_from, tall_ref),
    )
    fetches = [pltpu.make_async_copy(*move, fetched.at[place]) for place, move in enumerate(moves)]
    for fetch in fetches:
        fetch.start()
    for direction, (lepe, lepeb) in (
        (core, (own_lepe_ref, own_lepeb_ref)),
        (1 - core, (other_lepe_ref, other_lepeb_ref)),
    ):
        lepe_ref[direction, :, :TAPS] = lepe[:, :, 0]
        lepe_ref[direction, :, TAPS : TAPS + 1] = lepeb[...]

    def chunk_rows(index):
        return pl.ds(index * CHUNK, CHUNK)

    def chunk_tiles(index):
        return pl.ds(index * TILES, TILES)

    def wide_rows(index):
        return pl.ds(index * 2 * CHUNK, 2 * CHUNK)

    def wide_tiles(index):
        return pl.ds(index * 2 * TILES, 2 * TILES)

    def block_rows(index):
        return pl.ds(index * BLOCK, BLOCK)

    def is_small(block):
        return block % 6 >= 4

    def keep_of(image):
        place = lax.broadcasted_iota(jnp.int32, (IMG, 1), 0)
        limit = counts_ref[core * images + image]
        group = (place - 448) // BLOCK
        inside = (place - 448) % BLOCK
        return (place < 448) | (inside < 36 * (limit - 3 * group))

    for image in range(images):
        spot = pl.ds(image * TOK_IMG, TOK_IMG)
        h_ref[0, pl.ds(image * IMG, IMG), :] = dot(place_ref[...], tok_ref[spot, :])

    for fetch in fetches[:6]:
        fetch.wait()
    half_wfc2_ref[...] = half_wfc2_ref[...] * jnp.asarray(0.5, BF)

    def forward(layer, carry):
        gain1, bias1 = g1_ref[pl.ds(layer, 1), :], b1_ref[pl.ds(layer, 1), :]

        def normalize(index, _):
            rows = chunk_rows(index)
            xhat, _ = norm_parts(h_ref[layer, rows, :])
            normed = xhat * gain1 + bias1
            turned = split_tiles(normed) if index % 3 < 2 else normed
            return normed.astype(BF), turned.astype(BF)

        def project(index, values):
            rows = chunk_rows(index)
            for direction, value in enumerate(values):
                normed_ref[layer, direction, rows, :] = value
                qkv_ref[layer, direction, rows, :] = dot(value, wqkv_ref[direction, layer]).astype(BF)

        pipeline((normalize, project), range(chunks))

        def tap_weight(direction, tap):
            return lepe_ref[direction, layer, pl.ds(tap_row(direction, tap), 1), :]

        def score(window, _):
            direction, block = window
            rows = block_rows(block)
            query = qkv_ref[layer, direction, rows, :HW]
            keyset = qkv_ref[layer, direction, rows, HW : 2 * HW]
            return dot_nt(head_rows(keyset, heads_ref), pad_keys(query))

        def weigh(window, scores):
            direction, block = window
            rows = block_rows(block)
            bias = bias_ref[int(is_small(block))]
            probs = []
            for head in range(GH):
                part = scores[head * BLOCK : (head + 1) * BLOCK] + bias
                part = jnp.exp2((part - jnp.max(part, axis=0, keepdims=True)) * EXP_SCALE)
                part = part * (1.0 / jnp.sum(part, axis=0, keepdims=True))
                probs.append(part.astype(BF))
                probs_ref[layer, direction, rows, head * KEYS : (head + 1) * KEYS] = probs[head]
            return probs

        def mix(window, probs):
            direction, block = window
            rows = block_rows(block)
            values = qkv_ref[layer, direction, rows, 2 * HW :]
            side = values.T
            mixed = [dot(side[head * HD : (head + 1) * HD], probs[head]) for head in range(GH)]
            return jnp.concatenate(mixed, axis=0)

        def finish(window, mixed):
            direction, block = window
            lanes = slice(direction * HW, (direction + 1) * HW)
            result = mixed.T[:BLOCK] + lepe_ref[direction, layer, TAPS : TAPS + 1, :] + local[window]
            if direction == 0 or is_small(block):
                hf_ref[block * 7 : block * 7 + 7, :, :, lanes] = result.reshape(7, 2, TILE, HW)
            else:
                side = block % 2
                rows = slice((block - side) * 7, (block - side) * 7 + TILES)
                hf_ref[rows, side, :, lanes] = as_tiles(result)

        local = {}

        def filter_pair(kind, windows):
            scaled = []
            for direction, block in windows:
                values = qkv_ref[layer, direction, block_rows(block), 2 * HW :]
                scaled.append(
                    jnp.concatenate(
                        [pad_keys(values * tap_weight(direction, tap).astype(BF)) for tap in range(TAPS)], axis=0
                    )
                )
            both = dot(wide_ref[kind], jnp.concatenate(scaled, axis=1))
            for place, window in enumerate(windows):
                local[window] = both[:, place * HW : (place + 1) * HW]

        windows, fillers = [], []
        for block in range(blocks):
            windows += [(direction, block) for direction in range(2)]
            if is_small(block):
                fillers.append(functools.partial(filter_pair, 2, windows[-2:]))
            elif block % 2 == 1:
                for direction in range(2):
                    pair = [(direction, block - 1), (direction, block)]
                    fillers.append(functools.partial(filter_pair, direction, pair))
        pipeline((score, weigh, mix, finish), windows, fillers)

        gain2, bias2 = g2_ref[pl.ds(layer, 1), :], b2_ref[pl.ds(layer, 1), :]

        def join(index, _):
            rows = chunk_rows(index)
            heads = hf_ref[chunk_tiles(index)].reshape(CHUNK, D).astype(BF)
            hb_ref[layer, rows, :] = heads
            inner = h_ref[layer, rows, :] + dot(heads, wproj_ref[layer]) + bproj_ref[pl.ds(layer, 1), :]
            inner_ref[layer, rows, :] = inner
            return inner

        def widen(index, inner):
            xhat, _ = norm_parts(inner)
            normed2 = (xhat * gain2 + bias2).astype(BF)
            normed2_ref[layer, chunk_rows(index), :] = normed2
            return dot(normed2, wfc1_ref[layer])

        def narrow(index, hidden):
            rows = chunk_rows(index)
            hidden = hidden + bfc1_ref[pl.ds(layer, 1), :]
            cdf = 1.0 + lax.erf(hidden * math.sqrt(0.5))
            act = (hidden * cdf).astype(BF)
            act_ref[layer, rows, :] = act
            bell = jnp.exp2(hidden * hidden * (-0.5 * math.log2(math.e)))
            slope_ref[layer, rows, :] = (cdf + hidden * bell * math.sqrt(2 / math.pi)).astype(BF)
            return dot(act, half_wfc2_ref[layer])

        def close(index, branch):
            rows = chunk_rows(index)
            h_ref[layer + 1, rows, :] = inner_ref[layer, rows, :] + branch + bfc2_ref[pl.ds(layer, 1), :]

        pipeline((join, widen, narrow, close), range(chunks))
        return carry

    lax.fori_loop(0, LAYERS, forward, 0)
    for fetch in fetches[6:]:
        fetch.wait()

    for image in range(images):
        spot = pl.ds(image * TOK_IMG, TOK_IMG)
        wide = pl.ds(image * IMG, IMG)
        keep = keep_of(image)
        compact(dtok_ref, image, jnp.where(keep, h_ref[LAYERS, wide, :], 0.0))
        h_ref[LAYERS, wide, :] = jnp.where(keep, dot(place_ref[...], cot_ref[spot, :]), 0.0)
    out_ref[...] = dtok_ref[...].astype(BF)

    def backward(step, carry):
        layer = LAYERS - 1 - step
        base = pl.multiple_of(layer * PACKED, 16)
        acc_ref[...] = jnp.zeros_like(acc_ref)
        acclepe_ref[...] = jnp.zeros_like(acclepe_ref)

        accproj_ref[...] = jnp.zeros_like(accproj_ref)
        bfc1_sum_ref[...] = jnp.zeros_like(bfc1_sum_ref)
        gain2 = g2_ref[pl.ds(layer, 1), :]

        def pair_rows(index):
            return pl.ds((index - 1) * CHUNK, 2 * CHUNK)

        def widen(index, _):
            rows = wide_rows(index)
            dz = h_ref[LAYERS, rows, :].astype(BF)
            dz_ref[rows, :] = dz
            acc_ref[5] += fold_rows(dz.astype(F32))
            return dot_nt(dz, half_wfc2_ref[layer])

        def narrow(index, dact):
            rows = wide_rows(index)
            dhid = dact * slope_ref[layer, rows, :].astype(F32)
            bfc1_sum_ref[...] += fold_rows(dhid)
            dhid = dhid.astype(BF)
            dhid_ref[rows, :] = dhid
            return dot_nt(dhid, wfc1_ref[layer])

        def close(index, dnormed):
            rows = wide_rows(index)
            dvalue, dgain = norm_back(dnormed, inner_ref[layer, rows, :], gain2)
            acc_ref[3] += fold_rows(dgain)
            acc_ref[4] += fold_rows(dnormed)
            dinner = h_ref[LAYERS, rows, :] + dvalue
            h_ref[LAYERS, rows, :] = dinner
            dy = dinner.astype(BF)
            dy_ref[rows, :] = dy
            acc_ref[2] += fold_rows(dy.astype(F32))
            return dot_nt(dy, wproj_ref[layer])

        def project(index, dheads):
            hf_ref[wide_tiles(index)] = dheads.reshape(2 * TILES, 2, TILE, D)
            rows = wide_rows(index)
            accproj_ref[...] += dot_tn(hb_ref[layer, rows, :], dy_ref[rows, :])

        pipeline((widen, narrow, close, project), range(chunks // 2))
        for half in range(2):
            stage_ref[half, pl.ds(base + PROJ_AT, D), :] = accproj_ref[:, half * HW : (half + 1) * HW].astype(BF)

        def tap_weight(direction, tap):
            return lepe_ref[direction, layer, pl.ds(tap_row(direction, tap), 1), :]

        def grad_of(direction, block):
            lanes = slice(direction * HW, (direction + 1) * HW)
            if direction == 0 or is_small(block):
                tiles = hf_ref[block * 7 : block * 7 + 7, :, :, lanes]
            else:
                side = block % 2
                tiles = hf_ref[(block - side) * 7 : (block - side) * 7 + TILES, side, :, lanes]
            return tiles.reshape(BLOCK, HW).astype(BF)

        def score(window, _):
            direction, block = window
            rows = block_rows(block)
            grad = grad_of(direction, block)
            values = qkv_ref[layer, direction, rows, 2 * HW :]
            return dot_nt(head_rows(values, heads_ref), pad_keys(grad))

        def weigh(window, dprobs):
            direction, block = window
            rows = block_rows(block)
            dscores = []
            for head in range(GH):
                part = probs_ref[layer, direction, rows, head * KEYS : (head + 1) * KEYS].astype(F32)
                dpart = dprobs[head * BLOCK : (head + 1) * BLOCK]
                inner = jnp.sum(part * dpart, axis=0, keepdims=True)
                dscores.append((part * (dpart - inner)).astype(BF))
            return dscores

        def mix(window, dscores):
            direction, block = window
            rows = block_rows(block)
            grad = grad_of(direction, block)
            query = qkv_ref[layer, direction, rows, :HW]
            side = qkv_ref[layer, direction, rows, HW : 2 * HW].T
            dkeys = dot(jnp.concatenate(dscores, axis=1), head_stack(query, heads_ref))
            dvalues = dot(probs_ref[layer, direction, rows, :], head_stack(grad, heads_ref))
            dquery = [dot(side[head * HD : (head + 1) * HD], dscores[head]) for head in range(GH)]
            return jnp.concatenate(dquery, axis=0), dkeys, dvalues

        def finish(window, results):
            direction, block = window
            rows = block_rows(block)
            grad = grad_of(direction, block)
            lanes = slice(direction * HW, (direction + 1) * HW)
            dquery, dkeys, dvalues = results
            values = qkv_ref[layer, direction, rows, 2 * HW :]
            first = direction * 3 * HW
            dqkv_ref[rows, first : first + HW] = (dquery * SCALE).T[:BLOCK].astype(BF)
            dqkv_ref[rows, first + HW : first + 2 * HW] = (dkeys * SCALE).astype(BF)
            if is_small(block):
                dvalues = dvalues + local[block][:, lanes]
                dqkv_ref[rows, first + 2 * HW : first + 3 * HW] = dvalues.astype(BF)
                return None
            grad_tiles = as_tiles(grad.astype(F32))
            result = as_tiles(dvalues)
            for tap, cells in enumerate(tap_cells(grad_tiles, direction)):
                result = result + cells * tap_weight(direction, TAPS - 1 - tap).reshape(1, 1, HW)
            result = jnp.where(live_tiles(), result, 0.0).reshape(BLOCK, HW)
            dqkv_ref[rows, first + 2 * HW : first + 3 * HW] = result.astype(BF)
            tiles = jnp.where(live_tiles(), as_tiles(values.astype(F32)), 0.0)
            for tap, cells in enumerate(tap_cells(tiles, direction)):
                acclepe_ref[direction, tap_row(direction, tap)] += jnp.sum(grad_tiles * cells, axis=0)
            acclepe_ref[direction, TAPS] += jnp.sum(grad_tiles, axis=0)
            return None

        half_rows = rows_all // 2
        spans = [pl.ds(part * half_rows, half_rows) for part in range(2)]
        sides = {}

        def feed_weights(index):
            width = FF // (2 * images)
            cols = pl.ds(index * width, width)
            partial = []

            def first(part):
                rows = spans[part]
                if (0, part) not in sides:
                    sides[0, part] = normed2_ref[layer, rows, :].T
                partial.append(dot(sides[0, part], dhid_ref[rows, cols]))

            def second(part):
                rows = spans[part]
                if (1, part) not in sides:
                    sides[1, part] = dz_ref[rows, :].T
                partial.append(dot(sides[1, part], act_ref[layer, rows, cols]))

            def store(at):
                total = partial[0] + partial[1]
                if at == FC2_AT:
                    total = total * 0.5
                for piece in range(width // HW):
                    column = index * (width // HW) + piece
                    place = pl.multiple_of(base + at + column % 4 * 256, 16)
                    value = total[:, piece * HW : (piece + 1) * HW].astype(BF)
                    stage_ref[column // 4, pl.ds(place, 256), :] = value
                partial.clear()

            return [
                lambda: first(0),
                lambda: (first(1), store(FC1_AT)),
                lambda: second(0),
                lambda: (second(1), store(FC2_AT)),
            ]

        local = {}

        def filter_small(block):
            scaled = []
            for direction in range(2):
                padded = pad_keys(grad_of(direction, block).astype(F32))
                scaled.append(
                    jnp.concatenate(
                        [(padded * tap_weight(direction, TAPS - 1 - tap)).astype(BF) for tap in range(TAPS)], axis=0
                    )
                )
            local[block] = dot(wide_ref[2], jnp.concatenate(scaled, axis=1))

        def shift_small(block):
            values = [pad_keys(qkv_ref[layer, direction, block_rows(block), 2 * HW :]) for direction in range(2)]
            shifted = dot(tall_ref[...], jnp.concatenate(values, axis=1))
            for direction in range(2):
                lanes = slice(direction * HW, (direction + 1) * HW)
                grad = grad_of(direction, block).astype(F32)
                for tap in range(TAPS):
                    acclepe_ref[direction, tap_row(direction, tap)] += fold_rows(
                        grad * shifted[tap * BLOCK : (tap + 1) * BLOCK, lanes]
                    )
                acclepe_ref[direction, TAPS] += fold_rows(grad)

        order = [block for block in range(blocks) if not is_small(block)]
        order += [block for block in range(blocks) if is_small(block)]
        windows = [(direction, block) for block in order for direction in range(2)]
        fillers = [filler for index in range(2 * images) for filler in feed_weights(index)]
        for block in order:
            if is_small(block):
                fillers += [functools.partial(filter_small, block), functools.partial(shift_small, block)]
        pipeline((score, weigh, mix, finish), windows, fillers)

        accqkv_ref[...] = jnp.zeros_like(accqkv_ref)
        gain1 = g1_ref[pl.ds(layer, 1), :]

        def collect(index, _):
            rows = chunk_rows(index)
            return [
                dot_nt(dqkv_ref[rows, direction * 3 * HW : (direction + 1) * 3 * HW], wqkv_ref[direction, layer])
                for direction in range(2)
            ]

        def weigh_inputs(index, dnormed):
            if index % 2 == 1:
                rows = pair_rows(index)
                for direction in range(2):
                    accqkv_ref[direction] += dot(
                        normed_ref[layer, direction, rows, :].T,
                        dqkv_ref[rows, direction * 3 * HW : (direction + 1) * 3 * HW],
                    )
            return dnormed

        def spread(index, dnormed):
            rows = chunk_rows(index)
            straight, turned = dnormed
            dnormed = straight + (join_tiles(turned) if index % 3 < 2 else turned)
            dvalue, dgain = norm_back(dnormed, h_ref[layer, rows, :], gain1)
            acc_ref[0] += fold_rows(dgain)
            acc_ref[1] += fold_rows(dnormed)
            h_ref[LAYERS, rows, :] = h_ref[LAYERS, rows, :] + dvalue

        pipeline((collect, weigh_inputs, spread), range(chunks))
        small_ref[...] = jnp.zeros_like(small_ref)
        for direction in range(2):
            for piece in range(3):
                at = QKV_AT + 256 * piece
                stage_ref[direction, pl.ds(base + at, 256), :] = accqkv_ref[
                    direction, :, piece * HW : (piece + 1) * HW
                ].astype(BF)
            small_ref[direction, :10, :] = jnp.sum(acclepe_ref[direction], axis=1)
        sums = jnp.sum(acc_ref[...], axis=1)
        for piece in range(2):
            small_ref[0, 10 + 6 * piece : 16 + 6 * piece, :] = sums[:, piece * HW : (piece + 1) * HW]
        sums = jnp.sum(bfc1_sum_ref[...], axis=0, keepdims=True)
        for piece in range(8):
            small_ref[1, 10 + piece : 11 + piece, :] = sums[:, piece * HW : (piece + 1) * HW]
        stage_ref[:, pl.ds(base + SMALL_AT, SMALL), :] = small_ref[...].astype(BF)

        return carry

    stage_ref[:, ALL_PACKED:, :] = jnp.zeros((2, stage_ref.shape[1] - ALL_PACKED, HW), BF)
    lax.fori_loop(0, LAYERS, backward, 0)

    copies = []
    for slot, target in enumerate((keep_ref, send_ref)):
        half = jnp.bitwise_xor(core, slot)
        first = jnp.where(half == 0, place_of(mine, parts, 0), place_of(mine, parts, 1))
        for part in range(parts):
            change = jnp.where(half == 0, place_of(part, parts, 0), place_of(part, parts, 1))
            source = stage_ref.at[half, pl.ds(part * part_rows, part_rows), :]
            place = target.at[jnp.bitwise_xor(first, change)]
            copies.append(pltpu.make_async_copy(source, place, handed.at[slot, part]))
    for copy in copies:
        copy.start()
    for image in range(images):
        compact(dtok_ref, image, h_ref[LAYERS, pl.ds(image * IMG, IMG), :])
    for copy in copies:
        copy.wait()


def digits_of(parts, core):
    digits, stride = [], 1
    while stride < parts:
        size = 4 if parts // stride % 4 == 0 else 2
        digits.append((size, stride))
        stride *= size
    if len({size for size, _ in digits}) == 1 and core == 1:
        digits = digits[1:] + digits[:1]
    return digits


def place_of(index, parts, core):
    place = 0
    for size, stride in digits_of(parts, core):
        place = place * size + index // stride % size
    return place


def unpack_kernel(
    own_ref,
    other_ref,
    g1_ref,
    b1_ref,
    gqkv_ref,
    glepe_ref,
    glepeb_ref,
    gproj_ref,
    gbproj_ref,
    g2_ref,
    b2_ref,
    gfc1_ref,
    gbfc1_ref,
    gfc2_ref,
    gbfc2_ref,
    stage_ref,
):
    parts = own_ref.shape[0]
    part_rows = own_ref.shape[1]
    core = lax.axis_index("heads")
    mine = lax.axis_index("dp")
    for slot, ref in enumerate((own_ref, other_ref)):
        half = jnp.bitwise_xor(core, slot)
        first = jnp.where(half == 0, place_of(mine, parts, 0), place_of(mine, parts, 1))
        for part in range(parts):
            change = jnp.where(half == 0, place_of(part, parts, 0), place_of(part, parts, 1))
            stage_ref[half, part * part_rows : (part + 1) * part_rows, :] = ref[jnp.bitwise_xor(first, change)]

    for layer in range(LAYERS):
        base = layer * PACKED
        for half in range(2):
            for piece in range(4):
                lanes = slice(half * 512 + piece * HW, half * 512 + (piece + 1) * HW)
                at = base + FC1_AT + 256 * piece
                gfc1_ref[layer, :, lanes] = stage_ref[half, at : at + 256, :].astype(F32)
                at = base + FC2_AT + 256 * piece
                gfc2_ref[layer, lanes, :] = stage_ref[half, at : at + 256, :].astype(F32).T
            gproj_ref[layer, :, half * HW : (half + 1) * HW] = stage_ref[
                half, base + PROJ_AT : base + PROJ_AT + 256, :
            ].astype(F32)
        for piece in range(3):
            at = base + QKV_AT + 256 * piece
            gqkv_ref[layer, 0, :, piece * HW : (piece + 1) * HW] = stage_ref[core, at : at + 256, :].astype(F32)
        small = stage_ref[core, base + SMALL_AT : base + PACKED, :].astype(F32)
        glepe_ref[layer, :, 0] = small[:TAPS]
        glepeb_ref[layer] = small[TAPS : TAPS + 1]
        small = stage_ref[0, base + SMALL_AT : base + PACKED, :].astype(F32)
        for place, ref in enumerate((g1_ref, b1_ref, gbproj_ref, g2_ref, b2_ref, gbfc2_ref)):
            for piece in range(2):
                row = 10 + 6 * piece + place
                ref[layer : layer + 1, piece * HW : (piece + 1) * HW] = small[row : row + 1]
        small = stage_ref[1, base + SMALL_AT : base + PACKED, :].astype(F32)
        for piece in range(8):
            gbfc1_ref[layer : layer + 1, piece * HW : (piece + 1) * HW] = small[10 + piece : 11 + piece]


SMEM = pl.BlockSpec(memory_space=pltpu.SMEM)
VMEM = pl.BlockSpec(memory_space=pltpu.VMEM)
ANY = pl.BlockSpec(memory_space=pl.ANY)


def shards(
    dp,
    tokens,
    cotangent,
    counts,
    ln1_gain,
    ln1_bias,
    w_qkv,
    lepe_w,
    lepe_b,
    w_proj,
    b_proj,
    ln2_gain,
    ln2_bias,
    w_fc1,
    b_fc1,
    w_fc2,
    b_fc2,
):
    tokens_here = tokens.shape[0]
    images = tokens_here // TOK_IMG
    rows = images * IMG
    swap = [(0, 1), (1, 0)]

    def across(value):
        return lax.ppermute(value, "heads", swap)

    part_rows = -(-ALL_PACKED // (16 * dp)) * 16
    wide, tall = shift_tables()
    table = place_table()
    scratch = [
        pltpu.VMEM((tokens_here, D), BF),
        pltpu.VMEM((LAYERS, D, D), BF),
        pltpu.VMEM((LAYERS, D, FF), BF),
        pltpu.VMEM((LAYERS, FF, D), BF),
        pltpu.VMEM((3, BLOCK, TAPS * KEYS), BF),
        pltpu.VMEM((TAPS * BLOCK, KEYS), BF),
        pltpu.SemaphoreType.DMA((8,)),
        pltpu.SemaphoreType.DMA((2, dp)),
        pltpu.VMEM((2, LAYERS, D, 3 * HW), BF),
        pltpu.VMEM((2, LAYERS, 16, HW), F32),
        pltpu.VMEM((LAYERS + 1, rows, D), F32),
        pltpu.VMEM((LAYERS, 2, rows, D), BF),
        pltpu.VMEM((LAYERS, 2, rows, 3 * HW), BF),
        pltpu.VMEM((LAYERS, 2, rows, SPAN), BF),
        pltpu.VMEM((rows // 16, 2, TILE, D), F32),
        pltpu.VMEM((LAYERS, rows, D), BF),
        pltpu.VMEM((LAYERS, rows, D), F32),
        pltpu.VMEM((LAYERS, rows, D), BF),
        pltpu.VMEM((LAYERS, rows, FF), BF),
        pltpu.VMEM((LAYERS, rows, FF), BF),
        pltpu.VMEM((rows, D), BF),
        pltpu.VMEM((rows, D), BF),
        pltpu.VMEM((rows, FF), BF),
        pltpu.VMEM((rows, 6 * HW), BF),
        pltpu.VMEM((6, 8, D), F32),
        pltpu.VMEM((8, FF), F32),
        pltpu.VMEM((D, D), F32),
        pltpu.VMEM((2, D, 3 * HW), F32),
        pltpu.VMEM((2, TAPS + 1, 8, HW), F32),
        pltpu.VMEM((2, SMALL, HW), F32),
        pltpu.VMEM((2, part_rows * dp, HW), BF),
    ]
    result, grad, keep, send = pl.pallas_call(
        step_kernel,
        out_shape=(
            jax.ShapeDtypeStruct((tokens_here, D), BF),
            jax.ShapeDtypeStruct((tokens_here, D), F32),
            jax.ShapeDtypeStruct((dp, part_rows, HW), BF),
            jax.ShapeDtypeStruct((dp, part_rows, HW), BF),
        ),
        in_specs=[SMEM, VMEM, ANY, VMEM, VMEM, ANY, ANY] + [VMEM] * 4 + [ANY] + [VMEM] * 3 + [ANY, VMEM, ANY, VMEM, VMEM, ANY, ANY, VMEM, VMEM],
        out_specs=(VMEM, VMEM, ANY, ANY),
        scratch_shapes=scratch,
        compiler_params=pltpu.CompilerParams(vmem_limit_bytes=60 * 1024 * 1024),
        name="step",
    )(
        counts,
        tokens,
        cotangent,
        ln1_gain,
        ln1_bias,
        w_qkv,
        across(w_qkv),
        lepe_w.swapaxes(1, 2),
        across(lepe_w.swapaxes(1, 2)),
        lepe_b,
        across(lepe_b),
        w_proj,
        b_proj,
        ln2_gain,
        ln2_bias,
        w_fc1,
        b_fc1,
        w_fc2,
        b_fc2,
        jnp.asarray(table, BF),
        jnp.asarray(wide, BF),
        jnp.asarray(tall, BF),
        jnp.asarray(bias_table()),
        jnp.asarray(head_table(), BF),
    )

    def add(first, *rest):
        total = first.astype(F32)
        for item in rest:
            total = total + item.astype(F32)
        return total.astype(BF)

    own = add(keep, across(send))
    orders = [digits_of(dp, core) for core in range(2)]

    def exchange(step, pieces):
        arrived = []
        for hop in range(len(pieces) - 1, 0, -1):
            pairs = []
            for chip in range(dp):
                for core in range(2):
                    partner = chip ^ (hop * orders[core][step][1])
                    pairs.append((2 * chip + core, 2 * partner + core))
            arrived.append(lax.ppermute(pieces[hop], ("dp", "heads"), pairs))
        return lax.optimization_barrier(tuple(arrived))[::-1]

    for step, (size, _) in enumerate(orders[0]):
        pieces = own.reshape((size, own.shape[0] // size) + own.shape[1:])
        own = add(pieces[0], *exchange(step, pieces))
    for step, (size, _) in reversed(list(enumerate(orders[0]))):
        own = jnp.concatenate((own,) + tuple(exchange(step, [own] * size)), axis=0)
    other = across(own)
    grads = list(pl.pallas_call(
        unpack_kernel,
        out_shape=(
            jax.ShapeDtypeStruct((LAYERS, D), F32),
            jax.ShapeDtypeStruct((LAYERS, D), F32),
            jax.ShapeDtypeStruct((LAYERS, 1, D, 3 * HW), F32),
            jax.ShapeDtypeStruct((LAYERS, TAPS, 1, HW), F32),
            jax.ShapeDtypeStruct((LAYERS, 1, HW), F32),
            jax.ShapeDtypeStruct((LAYERS, D, D), F32),
            jax.ShapeDtypeStruct((LAYERS, D), F32),
            jax.ShapeDtypeStruct((LAYERS, D), F32),
            jax.ShapeDtypeStruct((LAYERS, D), F32),
            jax.ShapeDtypeStruct((LAYERS, D, FF), F32),
            jax.ShapeDtypeStruct((LAYERS, FF), F32),
            jax.ShapeDtypeStruct((LAYERS, FF, D), F32),
            jax.ShapeDtypeStruct((LAYERS, D), F32),
        ),
        in_specs=[VMEM] * 2,
        out_specs=(VMEM,) * 13,
        scratch_shapes=[pltpu.VMEM((2, part_rows * dp, HW), BF)],
        compiler_params=pltpu.CompilerParams(vmem_limit_bytes=48 * 1024 * 1024),
        name="unpack",
    )(own, other))
    grads[3] = grads[3].swapaxes(1, 2)
    return (result, grad) + tuple(grads)


def solution(mesh):
    spread = P(("dp", "heads"), None)
    group = (P(None, "heads", None, None), P(None, "heads", None, None), P(None, "heads", None))
    in_specs = (spread, spread, P("dp"), P(), P()) + group + (P(),) * 8
    out_specs = (spread, spread, P(), P()) + group + (P(),) * 8
    return jax.shard_map(
        functools.partial(shards, mesh.shape["dp"]),
        mesh=mesh,
        in_specs=in_specs,
        out_specs=out_specs,
        check_vma=False,
    )
```

time: 147 us -> 125 us (0.85)
  the two profiles are of different devices: /device:TPU:0 before, /device:TPU:9 now
where the time goes in v4:
time: 125 us
  waiting for transfers between devices  56.3 us (45%)
  Pallas kernels  51 us (41%)
  starting transfers between devices  12.6 us (10%)
  other arithmetic  2.3 us (2%)
  local copies, waits for them, and re-layouts  1.65 us (1%)
    ppermute x12, waiting for transfers between devices, exchange(): arrived.append(lax.ppermute(pieces[hop], ('dp', 'heads'), pairs))  48.4 us
    pallas_call x1, Pallas kernels, shards(): pl.pallas_call(step_kernel, out_shape=(jax.ShapeDtypeStruct((tokens_here,...  48 us
    ppermute x12, starting transfers between devices, exchange(): arrived.append(lax.ppermute(pieces[hop], ('dp', 'heads'), pairs))  10.8 us
    ppermute x5, waiting for transfers between devices, across(): return lax.ppermute(value, 'heads', swap)  7.9 us
    pallas_call x1, Pallas kernels, shards(): pl.pallas_call(unpack_kernel, out_shape=(jax.ShapeDtypeStruct((LAYERS, D)...  3 us
  transfers between devices with their start and end apart: 17, of which 15 were waited for; matrix products, arithmetic and copies ran while one was open for 0% of the time, Pallas kernels for 0%

profile of v4, /device:TPU:9, one launch (start us, length us, event | category | flops | bytes accessed | tf_op | source)
XLA Modules:
  0.0 124.8 jit_solution(8862653853157112424)
XLA Ops:
  0.6 0.7 collective-permute-start
  1.4 0.1 collective-permute-start.1
  1.5 0.4 collective-permute-start.2
  1.9 1.1 collective-permute-done.2.other_lepeb_ref
  3.0 0.0 copy-start.2
  3.0 0.0 collective-permute-done.1.other_lepe_ref
  3.0 0.0 copy-start.1
  3.0 0.0 collective-permute-done.other_wqkv_from
  3.0 0.5 copy-done.2
  3.5 0.0 copy-done.1
  3.6 0.0 copy-start
  3.6 0.7 copy-done
  4.3 48.0 %step.1 = (bf16[1216,256]{1,0:T(8,128)(2,1)}, f32[1216,256]{1,0:T(8,128)}, bf16[16,400,128]{2,1,0:T(8,128)(2,1)}, bf16[16,400,128]{2,1,0:T(8,128)(2,1)}) custom-call(s32[4]{0:T(128)} %counts_ref.1, bf16[1216,256]{1,0:T(8,128)(2,1)} %tok_ref.1, bf16[1216,256]{1,0:T(8,128)(2,1)} %cot_from.1, f32[2,256]{1,0:T(2,128)} %g1_ref.1, f32[2,256]{1,0:T(2,128)} %b1_ref.1, ...), custom_call_target="tpu_custom_call" | custom-call | tf_op jit(solution)/shard_map/step/pallas_call | solution.py:879
  52.4 0.4 collective-permute-start.3
  52.8 3.3 %collective-permute-done.3 = bf16[16,400,128]{2,1,0:T(8,128)(2,1)S(1)} collective-permute-done((bf16[16,400,128]{2,1,0:T(8,128)(2,1)}, bf16[16,400,128]{2,1,0:T(8,128)(2,1)S(1)}, u32[]{:S(2)}, u32[]{:S(2)}) %collective-permute-start.3) | collective-permute-done | bytes 1638432 | tf_op jit(solution)/shard_map/ppermute | solution.py:841
  56.1 2.0 %add_convert_fusion = bf16[16,400,128]{2,1,0:T(8,128)(2,1)S(1)} fusion(bf16[16,400,128]{2,1,0:T(8,128)(2,1)S(1)} %collective-permute-done.3, bf16[16,400,128]{2,1,0:T(8,128)(2,1)} %get-tuple-element.46), kind=kLoop, calls=%fused_computation | loop fusion | flops 3276800 | bytes 4915200 | tf_op jit(solution)/shard_map/convert_element_type | solution.py:923
  58.1 0.1 fusion
  58.2 0.1 collective-permute-start.6
  58.3 2.5 %collective-permute-start.5 = (bf16[4,400,128]{2,1,0:T(8,128)(2,1)S(1)}, bf16[4,400,128]{2,1,0:T(8,128)(2,1)S(1)}, u32[]{:S(2)}, u32[]{:S(2)}) collective-permute-start(bf16[4,400,128]{2,1,0:T(8,128)(2,1)S(1)} %get-tuple-element.76), channel_id=1, source_target_pairs={{0,4},{1,17},{2,6},{3,19},{4,0},{5,21},{6,2},{7,23},{8,12},{9,25},... | collective-permute-start | bytes 1228808 | tf_op jit(solution)/shard_map/ppermute | solution.py:936
  60.8 0.2 collective-permute-start.4
  60.9 6.5 %collective-permute-done.6 = bf16[4,400,128]{2,1,0:T(8,128)(2,1)S(1)} collective-permute-done((bf16[4,400,128]{2,1,0:T(8,128)(2,1)S(1)}, bf16[4,400,128]{2,1,0:T(8,128)(2,1)S(1)}, u32[]{:S(2)}, u32[]{:S(2)}) %collective-permute-start.6) | collective-permute-done | bytes 409632 | tf_op jit(solution)/shard_map/ppermute | solution.py:936
  67.4 7.0 %collective-permute-done.5 = bf16[4,400,128]{2,1,0:T(8,128)(2,1)S(1)} collective-permute-done((bf16[4,400,128]{2,1,0:T(8,128)(2,1)S(1)}, bf16[4,400,128]{2,1,0:T(8,128)(2,1)S(1)}, u32[]{:S(2)}, u32[]{:S(2)}) %collective-permute-start.5) | collective-permute-done | bytes 409632 | tf_op jit(solution)/shard_map/ppermute | solution.py:936
  74.5 9.6 %collective-permute-done.4 = bf16[4,400,128]{2,1,0:T(8,128)(2,1)S(1)} collective-permute-done((bf16[4,400,128]{2,1,0:T(8,128)(2,1)S(1)}, bf16[4,400,128]{2,1,0:T(8,128)(2,1)S(1)}, u32[]{:S(2)}, u32[]{:S(2)}) %collective-permute-start.4) | collective-permute-done | bytes 409632 | tf_op jit(solution)/shard_map/ppermute | solution.py:936
  84.1 0.2 add_convert_fusion.1
  84.3 1.1 collective-permute-start.9
  85.4 1.2 collective-permute-start.8
  86.6 0.4 collective-permute-start.7
  87.0 1.2 collective-permute-done.9
  88.2 0.7 collective-permute-done.8
  88.9 2.1 %collective-permute-done.7 = bf16[1,400,128]{2,1,0:T(8,128)(2,1)S(1)} collective-permute-done((bf16[1,400,128]{2,1,0:T(8,128)(2,1)S(1)}, bf16[1,400,128]{2,1,0:T(8,128)(2,1)S(1)}, u32[]{:S(2)}, u32[]{:S(2)}) %collective-permute-start.7) | collective-permute-done | bytes 102432 | tf_op jit(solution)/shard_map/ppermute | solution.py:936
  91.0 0.1 constant_dynamic-update-slice_fusion.6
  91.1 0.7 collective-permute-start.12
  91.8 0.3 collective-permute-start.11
  92.2 1.7 %collective-permute-start.10 = (bf16[1,400,128]{2,1,0:T(8,128)(2,1)S(1)}, bf16[1,400,128]{2,1,0:T(8,128)(2,1)S(1)}, u32[]{:S(2)}, u32[]{:S(2)}) collective-permute-start(bf16[1,400,128]{2,1,0:T(8,128)(2,1)S(1)} %get-tuple-element.74), channel_id=1, source_target_pairs={{0,24},{1,7},{2,26},{3,5},{4,28},{5,3},{6,30},{7,1},{8,16},{9,15},... | collective-permute-start | bytes 307208 | tf_op jit(solution)/shard_map/ppermute | solution.py:936
  93.8 0.9 collective-permute-done.12
  94.7 0.7 collective-permute-done.11
  95.3 1.2 collective-permute-done.10
  96.6 0.1 pad_maximum_fusion
  96.6 0.1 collective-permute-start.15
  96.7 2.2 %collective-permute-start.14 = (bf16[4,400,128]{2,1,0:T(8,128)(2,1)S(1)}, bf16[4,400,128]{2,1,0:T(8,128)(2,1)S(1)}, u32[]{:S(2)}, u32[]{:S(2)}) collective-permute-start(bf16[4,400,128]{2,1,0:T(8,128)(2,1)S(1)} %pad_maximum_fusion), channel_id=1, source_target_pairs={{0,4},{1,17},{2,6},{3,19},{4,0},{5,21},{6,2},{7,23},{8,12},{9,25},... | collective-permute-start | bytes 1228808 | tf_op jit(solution)/shard_map/ppermute | solution.py:936
  98.9 0.5 collective-permute-start.13
  99.4 6.2 %collective-permute-done.15 = bf16[4,400,128]{2,1,0:T(8,128)(2,1)S(1)} collective-permute-done((bf16[4,400,128]{2,1,0:T(8,128)(2,1)S(1)}, bf16[4,400,128]{2,1,0:T(8,128)(2,1)S(1)}, u32[]{:S(2)}, u32[]{:S(2)}) %collective-permute-start.15) | collective-permute-done | bytes 409632 | tf_op jit(solution)/shard_map/ppermute | solution.py:936
  105.6 7.0 %collective-permute-done.14 = bf16[4,400,128]{2,1,0:T(8,128)(2,1)S(1)} collective-permute-done((bf16[4,400,128]{2,1,0:T(8,128)(2,1)S(1)}, bf16[4,400,128]{2,1,0:T(8,128)(2,1)S(1)}, u32[]{:S(2)}, u32[]{:S(2)}) %collective-permute-start.14) | collective-permute-done | bytes 409632 | tf_op jit(solution)/shard_map/ppermute | solution.py:936
  112.6 5.3 %collective-permute-done.13 = bf16[4,400,128]{2,1,0:T(8,128)(2,1)S(1)} collective-permute-done((bf16[4,400,128]{2,1,0:T(8,128)(2,1)S(1)}, bf16[4,400,128]{2,1,0:T(8,128)(2,1)S(1)}, u32[]{:S(2)}, u32[]{:S(2)}) %collective-permute-start.13) | collective-permute-done | bytes 409632 | tf_op jit(solution)/shard_map/ppermute | solution.py:936
  117.9 0.1 constant_dynamic-update-slice_fusion.2
  117.9 0.1 constant_dynamic-update-slice_fusion.1
  118.0 0.1 constant_dynamic-update-slice_fusion.own_ref
  118.1 0.1 collective-permute-start.16
  118.2 3.5 %collective-permute-done.16.other_ref = bf16[16,400,128]{2,1,0:T(8,128)(2,1)S(1)} collective-permute-done((bf16[16,400,128]{2,1,0:T(8,128)(2,1)S(1)}, bf16[16,400,128]{2,1,0:T(8,128)(2,1)S(1)}, u32[]{:S(2)}, u32[]{:S(2)}) %collective-permute-start.16) | collective-permute-done | bytes 1638432 | tf_op jit(solution)/shard_map/ppermute | solution.py:841
  121.6 3.0 %unpack.1 = (f32[2,256]{1,0:T(2,128)}, f32[2,256]{1,0:T(2,128)}, f32[2,1,256,384]{3,2,1,0:T(8,128)}, f32[2,9,1,128]{3,2,1,0:T(1,128)}, f32[2,1,128]{2,1,0:T(1,12...) custom-call(bf16[16,400,128]{2,1,0:T(8,128)(2,1)S(1)} %constant_dyna, ...), custom_call_target="tpu_custom_call" | custom-call | tf_op jit(solution)/shard_map/unpack/pallas_call | solution.py:945
  (4 shorter events, 0.1 us)
Async XLA Ops:
  0.6 2.3 %collective-permute-start = (bf16[2,1,256,384]{3,2,1,0:T(8,128)(2,1)}, bf16[2,1,256,384]{3,2,1,0:T(8,128)(2,1)S(1)}, u32[]{:S(2)}, u32[]{:S(2)}) collective-permute-start(bf16[2,1,256,384]{3,2,1,0:T(8,128)(2,1)} %own_wqkv_from.1), channel_id=1, source_target_pairs={{0,1},{1,0},{2,3},{3,2},{4,5},{5,4},{6,7},{7,6},{8,9},{9,8},{10,11... | collective-permute-start | bytes 1179656 | tf_op jit(solution)/shard_map/ppermute | solution.py:841
  1.4 1.6 %collective-permute-start.1 = (f32[2,9,1,128]{3,2,1,0:T(1,128)}, f32[2,9,1,128]{3,2,1,0:T(1,128)S(1)}, u32[]{:S(2)}, u32[]{:S(2)}) collective-permute-start(f32[2,9,1,128]{3,2,1,0:T(1,128)} %bitcast.2), channel_id=1, source_target_pairs={{0,1},{1,0},{2,3},{3,2},{4,5},{5,4},{6,7},{7,6},{8,9},{9,8},{10,11... | collective-permute-start | bytes 27656 | tf_op jit(solution)/shard_map/ppermute | solution.py:841
  1.5 1.5 %collective-permute-start.2 = (f32[2,1,128]{2,1,0:T(1,128)}, f32[2,1,128]{2,1,0:T(1,128)S(1)}, u32[]{:S(2)}, u32[]{:S(2)}) collective-permute-start(f32[2,1,128]{2,1,0:T(1,128)} %own_lepeb_ref.1), channel_id=1, source_target_pairs={{0,1},{1,0},{2,3},{3,2},{4,5},{5,4},{6,7},{7,6},{8,9},{9,8},{10,11... | collective-permute-start | bytes 3080 | tf_op jit(solution)/shard_map/ppermute | solution.py:841
  3.0 0.6 copy-start.2
  3.0 0.6 copy-start.1
  3.6 0.7 copy-start
  52.4 3.8 %collective-permute-start.3 = (bf16[16,400,128]{2,1,0:T(8,128)(2,1)}, bf16[16,400,128]{2,1,0:T(8,128)(2,1)S(1)}, u32[]{:S(2)}, u32[]{:S(2)}) collective-permute-start(bf16[16,400,128]{2,1,0:T(8,128)(2,1)} %get-tuple-element.47), channel_id=1, source_target_pairs={{0,1},{1,0},{2,3},{3,2},{4,5},{5,4},{6,7},{7,6},{8,9},{9,8},{10,11... | collective-permute-start | bytes 4915208 | tf_op jit(solution)/shard_map/ppermute | solution.py:841
  58.2 9.2 %collective-permute-start.6 = (bf16[4,400,128]{2,1,0:T(8,128)(2,1)S(1)}, bf16[4,400,128]{2,1,0:T(8,128)(2,1)S(1)}, u32[]{:S(2)}, u32[]{:S(2)}) collective-permute-start(bf16[4,400,128]{2,1,0:T(8,128)(2,1)S(1)} %get-tuple-element.75), channel_id=1, source_target_pairs={{0,2},{1,9},{2,0},{3,11},{4,6},{5,13},{6,4},{7,15},{8,10},{9,1},{1... | collective-permute-start | bytes 1228808 | tf_op jit(solution)/shard_map/ppermute | solution.py:936
  58.3 16.2 %collective-permute-start.5 = (bf16[4,400,128]{2,1,0:T(8,128)(2,1)S(1)}, bf16[4,400,128]{2,1,0:T(8,128)(2,1)S(1)}, u32[]{:S(2)}, u32[]{:S(2)}) collective-permute-start(bf16[4,400,128]{2,1,0:T(8,128)(2,1)S(1)} %get-tuple-element.76), channel_id=1, source_target_pairs={{0,4},{1,17},{2,6},{3,19},{4,0},{5,21},{6,2},{7,23},{8,12},{9,25},... | collective-permute-start | bytes 1228808 | tf_op jit(solution)/shard_map/ppermute | solution.py:936
  60.8 23.3 %collective-permute-start.4 = (bf16[4,400,128]{2,1,0:T(8,128)(2,1)S(1)}, bf16[4,400,128]{2,1,0:T(8,128)(2,1)S(1)}, u32[]{:S(2)}, u32[]{:S(2)}) collective-permute-start(bf16[4,400,128]{2,1,0:T(8,128)(2,1)S(1)} %get-tuple-element.77), channel_id=1, source_target_pairs={{0,6},{1,25},{2,4},{3,27},{4,2},{5,29},{6,0},{7,31},{8,14},{9,17},... | collective-permute-start | bytes 1228808 | tf_op jit(solution)/shard_map/ppermute | solution.py:936
  84.3 3.9 %collective-permute-start.9 = (bf16[1,400,128]{2,1,0:T(8,128)(2,1)S(1)}, bf16[1,400,128]{2,1,0:T(8,128)(2,1)S(1)}, u32[]{:S(2)}, u32[]{:S(2)}) collective-permute-start(bf16[1,400,128]{2,1,0:T(8,128)(2,1)S(1)} %get-tuple-element.78), channel_id=1, source_target_pairs={{0,8},{1,3},{2,10},{3,1},{4,12},{5,7},{6,14},{7,5},{8,0},{9,11},{1... | collective-permute-start | bytes 307208 | tf_op jit(solution)/shard_map/ppermute | solution.py:936
  85.4 3.5 %collective-permute-start.8 = (bf16[1,400,128]{2,1,0:T(8,128)(2,1)S(1)}, bf16[1,400,128]{2,1,0:T(8,128)(2,1)S(1)}, u32[]{:S(2)}, u32[]{:S(2)}) collective-permute-start(bf16[1,400,128]{2,1,0:T(8,128)(2,1)S(1)} %get-tuple-element.79), channel_id=1, source_target_pairs={{0,16},{1,5},{2,18},{3,7},{4,20},{5,1},{6,22},{7,3},{8,24},{9,13},... | collective-permute-start | bytes 307208 | tf_op jit(solution)/shard_map/ppermute | solution.py:936
  86.6 4.4 %collective-permute-start.7 = (bf16[1,400,128]{2,1,0:T(8,128)(2,1)S(1)}, bf16[1,400,128]{2,1,0:T(8,128)(2,1)S(1)}, u32[]{:S(2)}, u32[]{:S(2)}) collective-permute-start(bf16[1,400,128]{2,1,0:T(8,128)(2,1)S(1)} %get-tuple-element.80), channel_id=1, source_target_pairs={{0,24},{1,7},{2,26},{3,5},{4,28},{5,3},{6,30},{7,1},{8,16},{9,15},... | collective-permute-start | bytes 307208 | tf_op jit(solution)/shard_map/ppermute | solution.py:936
  91.1 3.6 %collective-permute-start.12 = (bf16[1,400,128]{2,1,0:T(8,128)(2,1)S(1)}, bf16[1,400,128]{2,1,0:T(8,128)(2,1)S(1)}, u32[]{:S(2)}, u32[]{:S(2)}) collective-permute-start(bf16[1,400,128]{2,1,0:T(8,128)(2,1)S(1)} %get-tuple-element.74), channel_id=1, source_target_pairs={{0,8},{1,3},{2,10},{3,1},{4,12},{5,7},{6,14},{7,5},{8,0},{9,11},{1... | collective-permute-start | bytes 307208 | tf_op jit(solution)/shard_map/ppermute | solution.py:936
  91.8 3.5 %collective-permute-start.11 = (bf16[1,400,128]{2,1,0:T(8,128)(2,1)S(1)}, bf16[1,400,128]{2,1,0:T(8,128)(2,1)S(1)}, u32[]{:S(2)}, u32[]{:S(2)}) collective-permute-start(bf16[1,400,128]{2,1,0:T(8,128)(2,1)S(1)} %get-tuple-element.74), channel_id=1, source_target_pairs={{0,16},{1,5},{2,18},{3,7},{4,20},{5,1},{6,22},{7,3},{8,24},{9,13},... | collective-permute-start | bytes 307208 | tf_op jit(solution)/shard_map/ppermute | solution.py:936
  92.2 4.4 %collective-permute-start.10 = (bf16[1,400,128]{2,1,0:T(8,128)(2,1)S(1)}, bf16[1,400,128]{2,1,0:T(8,128)(2,1)S(1)}, u32[]{:S(2)}, u32[]{:S(2)}) collective-permute-start(bf16[1,400,128]{2,1,0:T(8,128)(2,1)S(1)} %get-tuple-element.74), channel_id=1, source_target_pairs={{0,24},{1,7},{2,26},{3,5},{4,28},{5,3},{6,30},{7,1},{8,16},{9,15},... | collective-permute-start | bytes 307208 | tf_op jit(solution)/shard_map/ppermute | solution.py:936
  96.6 9.0 %collective-permute-start.15 = (bf16[4,400,128]{2,1,0:T(8,128)(2,1)S(1)}, bf16[4,400,128]{2,1,0:T(8,128)(2,1)S(1)}, u32[]{:S(2)}, u32[]{:S(2)}) collective-permute-start(bf16[4,400,128]{2,1,0:T(8,128)(2,1)S(1)} %pad_maximum_fusion), channel_id=1, source_target_pairs={{0,2},{1,9},{2,0},{3,11},{4,6},{5,13},{6,4},{7,15},{8,10},{9,1},{1... | collective-permute-start | bytes 1228808 | tf_op jit(solution)/shard_map/ppermute | solution.py:936
  96.7 15.9 %collective-permute-start.14 = (bf16[4,400,128]{2,1,0:T(8,128)(2,1)S(1)}, bf16[4,400,128]{2,1,0:T(8,128)(2,1)S(1)}, u32[]{:S(2)}, u32[]{:S(2)}) collective-permute-start(bf16[4,400,128]{2,1,0:T(8,128)(2,1)S(1)} %pad_maximum_fusion), channel_id=1, source_target_pairs={{0,4},{1,17},{2,6},{3,19},{4,0},{5,21},{6,2},{7,23},{8,12},{9,25},... | collective-permute-start | bytes 1228808 | tf_op jit(solution)/shard_map/ppermute | solution.py:936
  98.9 19.0 %collective-permute-start.13 = (bf16[4,400,128]{2,1,0:T(8,128)(2,1)S(1)}, bf16[4,400,128]{2,1,0:T(8,128)(2,1)S(1)}, u32[]{:S(2)}, u32[]{:S(2)}) collective-permute-start(bf16[4,400,128]{2,1,0:T(8,128)(2,1)S(1)} %pad_maximum_fusion), channel_id=1, source_target_pairs={{0,6},{1,25},{2,4},{3,27},{4,2},{5,29},{6,0},{7,31},{8,14},{9,17},... | collective-permute-start | bytes 1228808 | tf_op jit(solution)/shard_map/ppermute | solution.py:936
  118.1 3.6 %collective-permute-start.16 = (bf16[16,400,128]{2,1,0:T(8,128)(2,1)S(1)}, bf16[16,400,128]{2,1,0:T(8,128)(2,1)S(1)}, u32[]{:S(2)}, u32[]{:S(2)}) collective-permute-start(bf16[16,400,128]{2,1,0:T(8,128)(2,1)S(1)} %constant_dynamic-update-slice_fusion.own_ref), channel_id=1, source_target_pairs={{0,1},{1,0},{2,3},{3,2},{4,5},{5,4},{6,7},{7,6},{8,9},{9,8},{10,11... | collective-permute-start | bytes 4915208 | tf_op jit(solution)/shard_map/ppermute | solution.py:841

commit v5 on v4

--- a/solution.py
+++ b/solution.py
@@ -224,6 +224,7 @@
 
 
 def step_kernel(
+    pieces,
     counts_ref,
     tok_ref,
     cot_from,
@@ -248,10 +249,15 @@
     tall_from,
     bias_ref,
     heads_ref,
+    out_to,
+    dtok_to,
+    *rest,
+):
+    keep_refs, send_refs, rest = rest[:pieces], rest[pieces : 2 * pieces], rest[2 * pieces :]
+    (
     out_ref,
     dtok_ref,
-    keep_ref,
-    send_ref,
+    written,
     cot_ref,
     wproj_ref,
     wfc1_ref,
@@ -283,13 +289,13 @@
     acclepe_ref,
     small_ref,
     stage_ref,
-):
+    ) = rest
     rows_all = h_ref.shape[1]
     images = rows_all // IMG
     chunks = rows_all // CHUNK
     blocks = rows_all // BLOCK
-    parts = keep_ref.shape[0]
-    part_rows = keep_ref.shape[1]
+    parts = pieces * keep_refs[0].shape[0]
+    part_rows = keep_refs[0].shape[1]
     core = lax.axis_index("heads")
     mine = lax.axis_index("dp")
     moves = (
@@ -475,6 +481,8 @@
         compact(dtok_ref, image, jnp.where(keep, h_ref[LAYERS, wide, :], 0.0))
         h_ref[LAYERS, wide, :] = jnp.where(keep, dot(place_ref[...], cot_ref[spot, :]), 0.0)
     out_ref[...] = dtok_ref[...].astype(BF)
+    out_copy = pltpu.make_async_copy(out_ref, out_to, written.at[0])
+    out_copy.start()
 
     def backward(step, carry):
         layer = LAYERS - 1 - step
@@ -717,20 +725,23 @@
     lax.fori_loop(0, LAYERS, backward, 0)
 
     copies = []
-    for slot, target in enumerate((keep_ref, send_ref)):
+    for slot, targets in enumerate((keep_refs, send_refs)):
         half = jnp.bitwise_xor(core, slot)
-        first = jnp.where(half == 0, place_of(mine, parts, 0), place_of(mine, parts, 1))
-        for part in range(parts):
-            change = jnp.where(half == 0, place_of(part, parts, 0), place_of(part, parts, 1))
-            source = stage_ref.at[half, pl.ds(part * part_rows, part_rows), :]
-            place = target.at[jnp.bitwise_xor(first, change)]
-            copies.append(pltpu.make_async_copy(source, place, handed.at[slot, part]))
+        for place in range(parts):
+            part = jnp.bitwise_xor(part_at(place, parts, half), mine)
+            source = stage_ref.at[half, pl.ds(pl.multiple_of(part * part_rows, 16), part_rows), :]
+            target = targets[place * pieces // parts].at[place % (parts // pieces)]
+            copies.append(pltpu.make_async_copy(source, target, handed.at[slot, place]))
     for copy in copies:
         copy.start()
     for image in range(images):
         compact(dtok_ref, image, h_ref[LAYERS, pl.ds(image * IMG, IMG), :])
+    dtok_copy = pltpu.make_async_copy(dtok_ref, dtok_to, written.at[1])
+    dtok_copy.start()
+    out_copy.wait()
     for copy in copies:
         copy.wait()
+    dtok_copy.wait()
 
 
 def digits_of(parts, core):
@@ -744,16 +755,23 @@
     return digits
 
 
-def place_of(index, parts, core):
-    place = 0
-    for size, stride in digits_of(parts, core):
-        place = place * size + index // stride % size
-    return place
+def part_at(place, parts, core):
+    found = []
+    for which in range(2):
+        index, left = 0, place
+        for size, stride in reversed(digits_of(parts, which)):
+            index += left % size * stride
+            left //= size
+        found.append(index)
+    return jnp.where(core == 0, found[0], found[1])
 
 
 def unpack_kernel(
-    own_ref,
-    other_ref,
+    pieces,
+    *refs,
+):
+    own_refs, other_refs, refs = refs[:pieces], refs[pieces : 2 * pieces], refs[2 * pieces :]
+    (
     g1_ref,
     b1_ref,
     gqkv_ref,
@@ -768,17 +786,17 @@
     gfc2_ref,
     gbfc2_ref,
     stage_ref,
-):
-    parts = own_ref.shape[0]
-    part_rows = own_ref.shape[1]
+    ) = refs
+    parts = pieces * own_refs[0].shape[0]
+    part_rows = own_refs[0].shape[1]
     core = lax.axis_index("heads")
     mine = lax.axis_index("dp")
-    for slot, ref in enumerate((own_ref, other_ref)):
+    for slot, sources in enumerate((own_refs, other_refs)):
         half = jnp.bitwise_xor(core, slot)
-        first = jnp.where(half == 0, place_of(mine, parts, 0), place_of(mine, parts, 1))
-        for part in range(parts):
-            change = jnp.where(half == 0, place_of(part, parts, 0), place_of(part, parts, 1))
-            stage_ref[half, part * part_rows : (part + 1) * part_rows, :] = ref[jnp.bitwise_xor(first, change)]
+        for place in range(parts):
+            part = jnp.bitwise_xor(part_at(place, parts, 0), mine)
+            at = pl.ds(pl.multiple_of(part * part_rows, 16), part_rows)
+            stage_ref[half, at, :] = sources[place * pieces // parts][place % (parts // pieces)]
 
     for layer in range(LAYERS):
         base = layer * PACKED
@@ -844,6 +862,9 @@
     wide, tall = shift_tables()
     table = place_table()
     scratch = [
+        pltpu.VMEM((tokens_here, D), BF),
+        pltpu.VMEM((tokens_here, D), F32),
+        pltpu.SemaphoreType.DMA((2,)),
         pltpu.VMEM((tokens_here, D), BF),
         pltpu.VMEM((LAYERS, D, D), BF),
         pltpu.VMEM((LAYERS, D, FF), BF),
@@ -876,16 +897,17 @@
         pltpu.VMEM((2, SMALL, HW), F32),
         pltpu.VMEM((2, part_rows * dp, HW), BF),
     ]
-    result, grad, keep, send = pl.pallas_call(
-        step_kernel,
+    pieces = digits_of(dp, 0)[0][0]
+    piece = jax.ShapeDtypeStruct((dp // pieces, part_rows, HW), BF)
+    result, grad, *packed = pl.pallas_call(
+        functools.partial(step_kernel, pieces),
         out_shape=(
             jax.ShapeDtypeStruct((tokens_here, D), BF),
             jax.ShapeDtypeStruct((tokens_here, D), F32),
-            jax.ShapeDtypeStruct((dp, part_rows, HW), BF),
-            jax.ShapeDtypeStruct((dp, part_rows, HW), BF),
-        ),
+        )
+        + (piece,) * (2 * pieces),
         in_specs=[SMEM, VMEM, ANY, VMEM, VMEM, ANY, ANY] + [VMEM] * 4 + [ANY] + [VMEM] * 3 + [ANY, VMEM, ANY, VMEM, VMEM, ANY, ANY, VMEM, VMEM],
-        out_specs=(VMEM, VMEM, ANY, ANY),
+        out_specs=(ANY,) * (2 + 2 * pieces),
         scratch_shapes=scratch,
         compiler_params=pltpu.CompilerParams(vmem_limit_bytes=60 * 1024 * 1024),
         name="step",
@@ -922,28 +944,37 @@
             total = total + item.astype(F32)
         return total.astype(BF)
 
-    own = add(keep, across(send))
+    keep, send = packed[:pieces], packed[pieces:]
     orders = [digits_of(dp, core) for core in range(2)]
 
-    def exchange(step, pieces):
-        arrived = []
-        for hop in range(len(pieces) - 1, 0, -1):
-            pairs = []
-            for chip in range(dp):
-                for core in range(2):
-                    partner = chip ^ (hop * orders[core][step][1])
-                    pairs.append((2 * chip + core, 2 * partner + core))
-            arrived.append(lax.ppermute(pieces[hop], ("dp", "heads"), pairs))
-        return lax.optimization_barrier(tuple(arrived))[::-1]
-
-    for step, (size, _) in enumerate(orders[0]):
-        pieces = own.reshape((size, own.shape[0] // size) + own.shape[1:])
-        own = add(pieces[0], *exchange(step, pieces))
-    for step, (size, _) in reversed(list(enumerate(orders[0]))):
-        own = jnp.concatenate((own,) + tuple(exchange(step, [own] * size)), axis=0)
-    other = across(own)
+    def hop_pairs(orders, step, hop):
+        pairs = []
+        for chip in range(dp):
+            for core in range(2):
+                pairs.append((2 * chip + core, 2 * (chip ^ (hop * orders[core][step][1])) + core))
+        return pairs
+
+    def exchange(step, values, orders=orders):
+        arrived = [
+            lax.ppermute(values[hop], ("dp", "heads"), hop_pairs(orders, step, hop)) for hop in range(len(values) - 1, 0, -1)
+        ]
+        return arrived[::-1]
+
+    received = [across(send[hop]) for hop in range(pieces - 1, -1, -1)][::-1]
+    sums = [None] + [add(keep[hop], received[hop]) for hop in range(1, pieces)]
+    arrived = lax.optimization_barrier(tuple(exchange(0, sums)))
+    own = add(keep[0], received[0], *arrived)
+    for step in range(1, len(orders[0])):
+        size = orders[0][step][0]
+        cuts = own.reshape((size, own.shape[0] // size) + own.shape[1:])
+        own = add(cuts[0], *lax.optimization_barrier(tuple(exchange(step, cuts))))
+    for step in range(len(orders[0]) - 1, 0, -1):
+        arrived = lax.optimization_barrier(tuple(exchange(step, [own] * orders[0][step][0], orders[:1] * 2)))
+        own = jnp.concatenate((own,) + tuple(arrived), axis=0)
+    whole = [own] + exchange(0, [own] * pieces, orders[:1] * 2)
+    others = [across(value) for value in whole]
     grads = list(pl.pallas_call(
-        unpack_kernel,
+        functools.partial(unpack_kernel, pieces),
         out_shape=(
             jax.ShapeDtypeStruct((LAYERS, D), F32),
             jax.ShapeDtypeStruct((LAYERS, D), F32),
@@ -959,12 +990,12 @@
             jax.ShapeDtypeStruct((LAYERS, FF, D), F32),
             jax.ShapeDtypeStruct((LAYERS, D), F32),
         ),
-        in_specs=[VMEM] * 2,
+        in_specs=[VMEM] * (2 * pieces),
         out_specs=(VMEM,) * 13,
         scratch_shapes=[pltpu.VMEM((2, part_rows * dp, HW), BF)],
         compiler_params=pltpu.CompilerParams(vmem_limit_bytes=48 * 1024 * 1024),
         name="unpack",
-    )(own, other))
+    )(*whole, *others))
     grads[3] = grads[3].swapaxes(1, 2)
     return (result, grad) + tuple(grads)
 

time: 125 us -> 119 us (0.952)
  the two profiles are of different devices: /device:TPU:9 before, /device:TPU:0 now
where the time goes in v5:
time: 119 us
  Pallas kernels  50.4 us (42%)
  starting transfers between devices  33.7 us (28%)
  waiting for transfers between devices  29.7 us (25%)
  other arithmetic  2.71 us (2%)
  local copies, waits for them, and re-layouts  1.37 us (1%)
    pallas_call x1, Pallas kernels, shards(): pl.pallas_call(functools.partial(step_kernel, pieces), out_shape=(jax.Sha...  47.3 us
    ppermute x12, waiting for transfers between devices, exchange(): lax.ppermute(values[hop], ('dp', 'heads'), hop_pairs(orders, step, hop))  25.7 us
    ppermute x12, starting transfers between devices, exchange(): lax.ppermute(values[hop], ('dp', 'heads'), hop_pairs(orders, step, hop))  17 us
    ppermute x11, starting transfers between devices, across(): return lax.ppermute(value, 'heads', swap)  16.6 us
    ppermute x11, waiting for transfers between devices, across(): return lax.ppermute(value, 'heads', swap)  3.97 us
    pallas_call x1, Pallas kernels, shards(): pl.pallas_call(functools.partial(unpack_kernel, pieces), out_shape=(jax.S...  3.01 us
    convert_element_type x5, other arithmetic, add(): return total.astype(BF)  2.66 us
  transfers between devices with their start and end apart: 23, of which 12 were waited for; matrix products, arithmetic and copies ran while one was open for 2% of the time, Pallas kernels for 0%

profile of v5, /device:TPU:0, one launch (start us, length us, event | category | flops | bytes accessed | tf_op | source)
XLA Modules:
  0.0 118.8 jit_solution(17040479580952158682)
XLA Ops:
  0.6 0.5 collective-permute-start
  1.2 0.1 collective-permute-start.1
  1.2 0.4 collective-permute-start.2
  1.7 1.1 collective-permute-done.2.other_lepeb_ref
  2.7 0.0 copy-start.4
  2.7 0.0 collective-permute-done.1.other_lepe_ref
  2.8 0.0 collective-permute-done.other_wqkv_from
  2.8 0.5 copy-done.4
  3.3 0.0 copy-done.3
  3.3 0.7 copy-done.2
  4.1 47.3 %step.1 = (bf16[1216,256]{1,0:T(8,128)(2,1)}, f32[1216,256]{1,0:T(8,128)}, bf16[4,400,128]{2,1,0:T(8,128)(2,1)}, bf16[4,400,128]{2,1,0:T(8,128)(2,1)}, bf16[4,40...) custom-call(s32[4]{0:T(128)} %counts_ref.1, ...), custom_call_target="tpu_custom_call" | custom-call | tf_op jit(solution)/shard_map/step/pallas_call | solution.py:902
  51.4 0.0 copy-start.1
  51.5 0.0 copy-start.5
  51.5 0.0 copy-start
  51.5 0.4 collective-permute-start.4
  51.9 0.1 collective-permute-start.6
  52.1 0.4 collective-permute-start.8
  52.4 1.1 collective-permute-done.4
  53.5 1.1 add_convert_fusion.3
  54.6 2.9 %collective-permute-start.5 = (bf16[4,400,128]{2,1,0:T(8,128)(2,1)S(1)}, bf16[4,400,128]{2,1,0:T(8,128)(2,1)S(1)}, u32[]{:S(2)}, u32[]{:S(2)}) collective-permute-start(bf16[4,400,128]{2,1,0:T(8,128)(2,1)S(1)} %add_convert_fusion.3), channel_id=1, source_target_pairs={{0,2},{1,9},{2,0},{3,11},{4,6},{5,13},{6,4},{7,15},{8,10},{9,1},{1... | collective-permute-start | bytes 1228808 | tf_op jit(solution)/shard_map/ppermute | solution.py:959
  57.5 0.0 collective-permute-done.6
  57.5 1.1 add_convert_fusion.2
  58.7 1.6 %collective-permute-start.7 = (bf16[4,400,128]{2,1,0:T(8,128)(2,1)S(1)}, bf16[4,400,128]{2,1,0:T(8,128)(2,1)S(1)}, u32[]{:S(2)}, u32[]{:S(2)}) collective-permute-start(bf16[4,400,128]{2,1,0:T(8,128)(2,1)S(1)} %add_convert_fusion.2), channel_id=1, source_target_pairs={{0,4},{1,17},{2,6},{3,19},{4,0},{5,21},{6,2},{7,23},{8,12},{9,25},... | collective-permute-start | bytes 1228808 | tf_op jit(solution)/shard_map/ppermute | solution.py:959
  60.2 0.0 collective-permute-done.8
  60.2 0.0 copy-done.1
  60.2 0.1 add_convert_fusion.1
  60.4 0.1 collective-permute-start.9
  60.4 0.0 copy-done.5
  60.5 0.8 collective-permute-start.3
  61.2 2.2 %collective-permute-done.5 = bf16[4,400,128]{2,1,0:T(8,128)(2,1)S(1)} collective-permute-done((bf16[4,400,128]{2,1,0:T(8,128)(2,1)S(1)}, bf16[4,400,128]{2,1,0:T(8,128)(2,1)S(1)}, u32[]{:S(2)}, u32[]{:S(2)}) %collective-permute-start.5) | collective-permute-done | bytes 409632 | tf_op jit(solution)/shard_map/ppermute | solution.py:959
  63.5 7.6 %collective-permute-done.7 = bf16[4,400,128]{2,1,0:T(8,128)(2,1)S(1)} collective-permute-done((bf16[4,400,128]{2,1,0:T(8,128)(2,1)S(1)}, bf16[4,400,128]{2,1,0:T(8,128)(2,1)S(1)}, u32[]{:S(2)}, u32[]{:S(2)}) %collective-permute-start.7) | collective-permute-done | bytes 409632 | tf_op jit(solution)/shard_map/ppermute | solution.py:959
  71.1 0.0 collective-permute-done.9
  71.1 0.0 collective-permute-done.3
  71.1 0.0 copy-done
  71.1 0.3 add_convert_fusion
  71.4 3.7 %collective-permute-start.12 = (bf16[1,400,128]{2,1,0:T(8,128)(2,1)S(1)}, bf16[1,400,128]{2,1,0:T(8,128)(2,1)S(1)}, u32[]{:S(2)}, u32[]{:S(2)}) collective-permute-start(bf16[1,400,128]{2,1,0:T(8,128)(2,1)S(1)} %get-tuple-element.79), channel_id=1, source_target_pairs={{0,24},{1,7},{2,26},{3,5},{4,28},{5,3},{6,30},{7,1},{8,16},{9,15},... | collective-permute-start | bytes 307208 | tf_op jit(solution)/shard_map/ppermute | solution.py:959
  75.0 0.0 collective-permute-start.11
  75.1 0.8 collective-permute-start.10
  75.8 2.2 %collective-permute-done.12 = bf16[1,400,128]{2,1,0:T(8,128)(2,1)S(1)} collective-permute-done((bf16[1,400,128]{2,1,0:T(8,128)(2,1)S(1)}, bf16[1,400,128]{2,1,0:T(8,128)(2,1)S(1)}, u32[]{:S(2)}, u32[]{:S(2)}) %collective-permute-start.12) | collective-permute-done | bytes 102432 | tf_op jit(solution)/shard_map/ppermute | solution.py:959
  78.0 4.7 %collective-permute-done.11 = bf16[1,400,128]{2,1,0:T(8,128)(2,1)S(1)} collective-permute-done((bf16[1,400,128]{2,1,0:T(8,128)(2,1)S(1)}, bf16[1,400,128]{2,1,0:T(8,128)(2,1)S(1)}, u32[]{:S(2)}, u32[]{:S(2)}) %collective-permute-start.11) | collective-permute-done | bytes 102432 | tf_op jit(solution)/shard_map/ppermute | solution.py:959
  82.7 0.0 collective-permute-done.10
  82.7 0.1 add_convert_fusion.4
  82.7 2.5 %collective-permute-start.15 = (bf16[1,400,128]{2,1,0:T(8,128)(2,1)S(1)}, bf16[1,400,128]{2,1,0:T(8,128)(2,1)S(1)}, u32[]{:S(2)}, u32[]{:S(2)}) collective-permute-start(bf16[1,400,128]{2,1,0:T(8,128)(2,1)S(1)} %add_convert_fusion.4), channel_id=1, source_target_pairs={{0,24},{1,25},{2,26},{3,27},{4,28},{5,29},{6,30},{7,31},{8,16},{9,... | collective-permute-start | bytes 307208 | tf_op jit(solution)/shard_map/ppermute | solution.py:959
  85.3 0.0 collective-permute-start.14
  85.3 1.9 %collective-permute-start.13 = (bf16[1,400,128]{2,1,0:T(8,128)(2,1)S(1)}, bf16[1,400,128]{2,1,0:T(8,128)(2,1)S(1)}, u32[]{:S(2)}, u32[]{:S(2)}) collective-permute-start(bf16[1,400,128]{2,1,0:T(8,128)(2,1)S(1)} %add_convert_fusion.4), channel_id=1, source_target_pairs={{0,8},{1,9},{2,10},{3,11},{4,12},{5,13},{6,14},{7,15},{8,0},{9,1},... | collective-permute-start | bytes 307208 | tf_op jit(solution)/shard_map/ppermute | solution.py:959
  87.2 2.1 %collective-permute-done.15 = bf16[1,400,128]{2,1,0:T(8,128)(2,1)S(1)} collective-permute-done((bf16[1,400,128]{2,1,0:T(8,128)(2,1)S(1)}, bf16[1,400,128]{2,1,0:T(8,128)(2,1)S(1)}, u32[]{:S(2)}, u32[]{:S(2)}) %collective-permute-start.15) | collective-permute-done | bytes 102432 | tf_op jit(solution)/shard_map/ppermute | solution.py:959
  89.3 2.1 %collective-permute-done.14 = bf16[1,400,128]{2,1,0:T(8,128)(2,1)S(1)} collective-permute-done((bf16[1,400,128]{2,1,0:T(8,128)(2,1)S(1)}, bf16[1,400,128]{2,1,0:T(8,128)(2,1)S(1)}, u32[]{:S(2)}, u32[]{:S(2)}) %collective-permute-start.14) | collective-permute-done | bytes 102432 | tf_op jit(solution)/shard_map/ppermute | solution.py:959
  91.5 0.0 collective-permute-done.13
  91.5 0.1 pad_maximum_fusion.refs_0_
  91.5 1.6 %collective-permute-start.18 = (bf16[4,400,128]{2,1,0:T(8,128)(2,1)S(1)}, bf16[4,400,128]{2,1,0:T(8,128)(2,1)S(1)}, u32[]{:S(2)}, u32[]{:S(2)}) collective-permute-start(bf16[4,400,128]{2,1,0:T(8,128)(2,1)S(1)} %pad_maximum_fusion.refs_0_), channel_id=1, source_target_pairs={{0,6},{1,7},{2,4},{3,5},{4,2},{5,3},{6,0},{7,1},{8,14},{9,15},{10,... | collective-permute-start | bytes 1228808 | tf_op jit(solution)/shard_map/ppermute | solution.py:959
  93.1 0.6 collective-permute-start.17
  93.7 1.4 %collective-permute-start.16 = (bf16[4,400,128]{2,1,0:T(8,128)(2,1)S(1)}, bf16[4,400,128]{2,1,0:T(8,128)(2,1)S(1)}, u32[]{:S(2)}, u32[]{:S(2)}) collective-permute-start(bf16[4,400,128]{2,1,0:T(8,128)(2,1)S(1)} %pad_maximum_fusion.refs_0_), channel_id=1, source_target_pairs={{0,2},{1,3},{2,0},{3,1},{4,6},{5,7},{6,4},{7,5},{8,10},{9,11},{10,... | collective-permute-start | bytes 1228808 | tf_op jit(solution)/shard_map/ppermute | solution.py:959
  95.1 4.8 %collective-permute-start.19 = (bf16[4,400,128]{2,1,0:T(8,128)(2,1)S(1)}, bf16[4,400,128]{2,1,0:T(8,128)(2,1)S(1)}, u32[]{:S(2)}, u32[]{:S(2)}) collective-permute-start(bf16[4,400,128]{2,1,0:T(8,128)(2,1)S(1)} %pad_maximum_fusion.refs_0_), channel_id=1, source_target_pairs={{0,1},{1,0},{2,3},{3,2},{4,5},{5,4},{6,7},{7,6},{8,9},{9,8},{10,11... | collective-permute-start | bytes 1228808 | tf_op jit(solution)/shard_map/ppermute | solution.py:859
  99.9 0.7 collective-permute-done.18.refs_3_
  100.5 8.6 %collective-permute-start.22 = (bf16[4,400,128]{2,1,0:T(8,128)(2,1)S(1)}, bf16[4,400,128]{2,1,0:T(8,128)(2,1)S(1)}, u32[]{:S(2)}, u32[]{:S(2)}) collective-permute-start(bf16[4,400,128]{2,1,0:T(8,128)(2,1)S(1)} %collective-permute-done.18.refs_3_), channel_id=1, source_target_pairs={{0,1},{1,0},{2,3},{3,2},{4,5},{5,4},{6,7},{7,6},{8,9},{9,8},{10,11... | collective-permute-start | bytes 1228808 | tf_op jit(solution)/shard_map/ppermute | solution.py:859
  109.1 4.2 %collective-permute-done.17.refs_2_ = bf16[4,400,128]{2,1,0:T(8,128)(2,1)S(1)} collective-permute-done((bf16[4,400,128]{2,1,0:T(8,128)(2,1)S(1)}, bf16[4,400,128]{2,1,0:T(8,128)(2,1)S(1)}, u32[]{:S(2)}, u32[]{:S(2)}) %collective-permute-start.17) | collective-permute-done | bytes 409632 | tf_op jit(solution)/shard_map/ppermute | solution.py:959
  113.3 0.2 collective-permute-start.21
  113.4 0.0 collective-permute-done.16.refs_1_
  113.4 0.4 collective-permute-start.20
  113.8 0.0 collective-permute-done.19.refs_4_
  113.8 0.0 collective-permute-done.22.refs_7_
  113.8 1.2 %collective-permute-done.21.refs_6_ = bf16[4,400,128]{2,1,0:T(8,128)(2,1)S(1)} collective-permute-done((bf16[4,400,128]{2,1,0:T(8,128)(2,1)S(1)}, bf16[4,400,128]{2,1,0:T(8,128)(2,1)S(1)}, u32[]{:S(2)}, u32[]{:S(2)}) %collective-permute-start.21) | collective-permute-done | bytes 409632 | tf_op jit(solution)/shard_map/ppermute | solution.py:859
  115.0 0.6 collective-permute-done.20.refs_5_
  115.6 3.0 %unpack.1 = (f32[2,256]{1,0:T(2,128)}, f32[2,256]{1,0:T(2,128)}, f32[2,1,256,384]{3,2,1,0:T(8,128)}, f32[2,9,1,128]{3,2,1,0:T(1,128)}, f32[2,1,128]{2,1,0:T(1,12...) custom-call(bf16[4,400,128]{2,1,0:T(8,128)(2,1)S(1)} %pad_maximum_fu, ...), custom_call_target="tpu_custom_call" | custom-call | tf_op jit(solution)/shard_map/unpack/pallas_call | solution.py:976
  (3 shorter events, 0.0 us)
Async XLA Ops:
  0.6 2.1 %collective-permute-start = (bf16[2,1,256,384]{3,2,1,0:T(8,128)(2,1)}, bf16[2,1,256,384]{3,2,1,0:T(8,128)(2,1)S(1)}, u32[]{:S(2)}, u32[]{:S(2)}) collective-permute-start(bf16[2,1,256,384]{3,2,1,0:T(8,128)(2,1)} %own_wqkv_from.1), channel_id=1, source_target_pairs={{0,1},{1,0},{2,3},{3,2},{4,5},{5,4},{6,7},{7,6},{8,9},{9,8},{10,11... | collective-permute-start | bytes 1179656 | tf_op jit(solution)/shard_map/ppermute | solution.py:859
  1.2 1.6 %collective-permute-start.1 = (f32[2,9,1,128]{3,2,1,0:T(1,128)}, f32[2,9,1,128]{3,2,1,0:T(1,128)S(1)}, u32[]{:S(2)}, u32[]{:S(2)}) collective-permute-start(f32[2,9,1,128]{3,2,1,0:T(1,128)} %bitcast.2), channel_id=1, source_target_pairs={{0,1},{1,0},{2,3},{3,2},{4,5},{5,4},{6,7},{7,6},{8,9},{9,8},{10,11... | collective-permute-start | bytes 27656 | tf_op jit(solution)/shard_map/ppermute | solution.py:859
  1.2 1.5 %collective-permute-start.2 = (f32[2,1,128]{2,1,0:T(1,128)}, f32[2,1,128]{2,1,0:T(1,128)S(1)}, u32[]{:S(2)}, u32[]{:S(2)}) collective-permute-start(f32[2,1,128]{2,1,0:T(1,128)} %own_lepeb_ref.1), channel_id=1, source_target_pairs={{0,1},{1,0},{2,3},{3,2},{4,5},{5,4},{6,7},{7,6},{8,9},{9,8},{10,11... | collective-permute-start | bytes 3080 | tf_op jit(solution)/shard_map/ppermute | solution.py:859
  2.7 0.6 copy-start.4
  2.7 0.6 copy-start.3
  3.3 0.7 copy-start.2
  51.4 8.8 %copy-start.1 = (bf16[4,400,128]{2,1,0:T(8,128)(2,1)S(1)}, bf16[4,400,128]{2,1,0:T(8,128)(2,1)}, u32[]{:S(2)}) copy-start(bf16[4,400,128]{2,1,0:T(8,128)(2,1)} %get-tuple-element.55) | copy-start | bytes 1228804
  51.5 9.0 %copy-start.5 = (bf16[4,400,128]{2,1,0:T(8,128)(2,1)S(1)}, bf16[4,400,128]{2,1,0:T(8,128)(2,1)}, u32[]{:S(2)}) copy-start(bf16[4,400,128]{2,1,0:T(8,128)(2,1)} %get-tuple-element.50) | copy-start | bytes 1228804
  51.5 19.6 %copy-start = (bf16[4,400,128]{2,1,0:T(8,128)(2,1)S(1)}, bf16[4,400,128]{2,1,0:T(8,128)(2,1)}, u32[]{:S(2)}) copy-start(bf16[4,400,128]{2,1,0:T(8,128)(2,1)} %get-tuple-element.49) | copy-start | bytes 1228804
  51.5 2.0 %collective-permute-start.4 = (bf16[4,400,128]{2,1,0:T(8,128)(2,1)}, bf16[4,400,128]{2,1,0:T(8,128)(2,1)S(1)}, u32[]{:S(2)}, u32[]{:S(2)}) collective-permute-start(bf16[4,400,128]{2,1,0:T(8,128)(2,1)} %get-tuple-element.52), channel_id=1, source_target_pairs={{0,1},{1,0},{2,3},{3,2},{4,5},{5,4},{6,7},{7,6},{8,9},{9,8},{10,11... | collective-permute-start | bytes 1228808 | tf_op jit(solution)/shard_map/ppermute | solution.py:859
  51.9 5.6 %collective-permute-start.6 = (bf16[4,400,128]{2,1,0:T(8,128)(2,1)}, bf16[4,400,128]{2,1,0:T(8,128)(2,1)S(1)}, u32[]{:S(2)}, u32[]{:S(2)}) collective-permute-start(bf16[4,400,128]{2,1,0:T(8,128)(2,1)} %get-tuple-element.54), channel_id=1, source_target_pairs={{0,1},{1,0},{2,3},{3,2},{4,5},{5,4},{6,7},{7,6},{8,9},{9,8},{10,11... | collective-permute-start | bytes 1228808 | tf_op jit(solution)/shard_map/ppermute | solution.py:859
  52.1 8.2 %collective-permute-start.8 = (bf16[4,400,128]{2,1,0:T(8,128)(2,1)}, bf16[4,400,128]{2,1,0:T(8,128)(2,1)S(1)}, u32[]{:S(2)}, u32[]{:S(2)}) collective-permute-start(bf16[4,400,128]{2,1,0:T(8,128)(2,1)} %get-tuple-element.56), channel_id=1, source_target_pairs={{0,1},{1,0},{2,3},{3,2},{4,5},{5,4},{6,7},{7,6},{8,9},{9,8},{10,11... | collective-permute-start | bytes 1228808 | tf_op jit(solution)/shard_map/ppermute | solution.py:859
  54.6 8.9 %collective-permute-start.5 = (bf16[4,400,128]{2,1,0:T(8,128)(2,1)S(1)}, bf16[4,400,128]{2,1,0:T(8,128)(2,1)S(1)}, u32[]{:S(2)}, u32[]{:S(2)}) collective-permute-start(bf16[4,400,128]{2,1,0:T(8,128)(2,1)S(1)} %add_convert_fusion.3), channel_id=1, source_target_pairs={{0,2},{1,9},{2,0},{3,11},{4,6},{5,13},{6,4},{7,15},{8,10},{9,1},{1... | collective-permute-start | bytes 1228808 | tf_op jit(solution)/shard_map/ppermute | solution.py:959
  58.7 12.4 %collective-permute-start.7 = (bf16[4,400,128]{2,1,0:T(8,128)(2,1)S(1)}, bf16[4,400,128]{2,1,0:T(8,128)(2,1)S(1)}, u32[]{:S(2)}, u32[]{:S(2)}) collective-permute-start(bf16[4,400,128]{2,1,0:T(8,128)(2,1)S(1)} %add_convert_fusion.2), channel_id=1, source_target_pairs={{0,4},{1,17},{2,6},{3,19},{4,0},{5,21},{6,2},{7,23},{8,12},{9,25},... | collective-permute-start | bytes 1228808 | tf_op jit(solution)/shard_map/ppermute | solution.py:959
  60.4 10.7 %collective-permute-start.9 = (bf16[4,400,128]{2,1,0:T(8,128)(2,1)S(1)}, bf16[4,400,128]{2,1,0:T(8,128)(2,1)S(1)}, u32[]{:S(2)}, u32[]{:S(2)}) collective-permute-start(bf16[4,400,128]{2,1,0:T(8,128)(2,1)S(1)} %add_convert_fusion.1), channel_id=1, source_target_pairs={{0,6},{1,25},{2,4},{3,27},{4,2},{5,29},{6,0},{7,31},{8,14},{9,17},... | collective-permute-start | bytes 1228808 | tf_op jit(solution)/shard_map/ppermute | solution.py:959
  60.5 10.6 %collective-permute-start.3 = (bf16[4,400,128]{2,1,0:T(8,128)(2,1)S(1)}, bf16[4,400,128]{2,1,0:T(8,128)(2,1)S(1)}, u32[]{:S(2)}, u32[]{:S(2)}) collective-permute-start(bf16[4,400,128]{2,1,0:T(8,128)(2,1)S(1)} %copy-done.5), channel_id=1, source_target_pairs={{0,1},{1,0},{2,3},{3,2},{4,5},{5,4},{6,7},{7,6},{8,9},{9,8},{10,11... | collective-permute-start | bytes 1228808 | tf_op jit(solution)/shard_map/ppermute | solution.py:859
  71.4 6.6 %collective-permute-start.12 = (bf16[1,400,128]{2,1,0:T(8,128)(2,1)S(1)}, bf16[1,400,128]{2,1,0:T(8,128)(2,1)S(1)}, u32[]{:S(2)}, u32[]{:S(2)}) collective-permute-start(bf16[1,400,128]{2,1,0:T(8,128)(2,1)S(1)} %get-tuple-element.79), channel_id=1, source_target_pairs={{0,24},{1,7},{2,26},{3,5},{4,28},{5,3},{6,30},{7,1},{8,16},{9,15},... | collective-permute-start | bytes 307208 | tf_op jit(solution)/shard_map/ppermute | solution.py:959
  75.0 7.6 %collective-permute-start.11 = (bf16[1,400,128]{2,1,0:T(8,128)(2,1)S(1)}, bf16[1,400,128]{2,1,0:T(8,128)(2,1)S(1)}, u32[]{:S(2)}, u32[]{:S(2)}) collective-permute-start(bf16[1,400,128]{2,1,0:T(8,128)(2,1)S(1)} %get-tuple-element.80), channel_id=1, source_target_pairs={{0,16},{1,5},{2,18},{3,7},{4,20},{5,1},{6,22},{7,3},{8,24},{9,13},... | collective-permute-start | bytes 307208 | tf_op jit(solution)/shard_map/ppermute | solution.py:959
  75.1 7.6 %collective-permute-start.10 = (bf16[1,400,128]{2,1,0:T(8,128)(2,1)S(1)}, bf16[1,400,128]{2,1,0:T(8,128)(2,1)S(1)}, u32[]{:S(2)}, u32[]{:S(2)}) collective-permute-start(bf16[1,400,128]{2,1,0:T(8,128)(2,1)S(1)} %get-tuple-element.81), channel_id=1, source_target_pairs={{0,8},{1,3},{2,10},{3,1},{4,12},{5,7},{6,14},{7,5},{8,0},{9,11},{1... | collective-permute-start | bytes 307208 | tf_op jit(solution)/shard_map/ppermute | solution.py:959
  82.7 6.6 %collective-permute-start.15 = (bf16[1,400,128]{2,1,0:T(8,128)(2,1)S(1)}, bf16[1,400,128]{2,1,0:T(8,128)(2,1)S(1)}, u32[]{:S(2)}, u32[]{:S(2)}) collective-permute-start(bf16[1,400,128]{2,1,0:T(8,128)(2,1)S(1)} %add_convert_fusion.4), channel_id=1, source_target_pairs={{0,24},{1,25},{2,26},{3,27},{4,28},{5,29},{6,30},{7,31},{8,16},{9,... | collective-permute-start | bytes 307208 | tf_op jit(solution)/shard_map/ppermute | solution.py:959
  85.3 6.2 %collective-permute-start.14 = (bf16[1,400,128]{2,1,0:T(8,128)(2,1)S(1)}, bf16[1,400,128]{2,1,0:T(8,128)(2,1)S(1)}, u32[]{:S(2)}, u32[]{:S(2)}) collective-permute-start(bf16[1,400,128]{2,1,0:T(8,128)(2,1)S(1)} %add_convert_fusion.4), channel_id=1, source_target_pairs={{0,16},{1,17},{2,18},{3,19},{4,20},{5,21},{6,22},{7,23},{8,24},{9,... | collective-permute-start | bytes 307208 | tf_op jit(solution)/shard_map/ppermute | solution.py:959
  85.3 6.2 %collective-permute-start.13 = (bf16[1,400,128]{2,1,0:T(8,128)(2,1)S(1)}, bf16[1,400,128]{2,1,0:T(8,128)(2,1)S(1)}, u32[]{:S(2)}, u32[]{:S(2)}) collective-permute-start(bf16[1,400,128]{2,1,0:T(8,128)(2,1)S(1)} %add_convert_fusion.4), channel_id=1, source_target_pairs={{0,8},{1,9},{2,10},{3,11},{4,12},{5,13},{6,14},{7,15},{8,0},{9,1},... | collective-permute-start | bytes 307208 | tf_op jit(solution)/shard_map/ppermute | solution.py:959
  91.5 9.0 %collective-permute-start.18 = (bf16[4,400,128]{2,1,0:T(8,128)(2,1)S(1)}, bf16[4,400,128]{2,1,0:T(8,128)(2,1)S(1)}, u32[]{:S(2)}, u32[]{:S(2)}) collective-permute-start(bf16[4,400,128]{2,1,0:T(8,128)(2,1)S(1)} %pad_maximum_fusion.refs_0_), channel_id=1, source_target_pairs={{0,6},{1,7},{2,4},{3,5},{4,2},{5,3},{6,0},{7,1},{8,14},{9,15},{10,... | collective-permute-start | bytes 1228808 | tf_op jit(solution)/shard_map/ppermute | solution.py:959
  93.1 20.2 %collective-permute-start.17 = (bf16[4,400,128]{2,1,0:T(8,128)(2,1)S(1)}, bf16[4,400,128]{2,1,0:T(8,128)(2,1)S(1)}, u32[]{:S(2)}, u32[]{:S(2)}) collective-permute-start(bf16[4,400,128]{2,1,0:T(8,128)(2,1)S(1)} %pad_maximum_fusion.refs_0_), channel_id=1, source_target_pairs={{0,4},{1,5},{2,6},{3,7},{4,0},{5,1},{6,2},{7,3},{8,12},{9,13},{10,... | collective-permute-start | bytes 1228808 | tf_op jit(solution)/shard_map/ppermute | solution.py:959
  93.7 19.7 %collective-permute-start.16 = (bf16[4,400,128]{2,1,0:T(8,128)(2,1)S(1)}, bf16[4,400,128]{2,1,0:T(8,128)(2,1)S(1)}, u32[]{:S(2)}, u32[]{:S(2)}) collective-permute-start(bf16[4,400,128]{2,1,0:T(8,128)(2,1)S(1)} %pad_maximum_fusion.refs_0_), channel_id=1, source_target_pairs={{0,2},{1,3},{2,0},{3,1},{4,6},{5,7},{6,4},{7,5},{8,10},{9,11},{10,... | collective-permute-start | bytes 1228808 | tf_op jit(solution)/shard_map/ppermute | solution.py:959
  95.1 18.7 %collective-permute-start.19 = (bf16[4,400,128]{2,1,0:T(8,128)(2,1)S(1)}, bf16[4,400,128]{2,1,0:T(8,128)(2,1)S(1)}, u32[]{:S(2)}, u32[]{:S(2)}) collective-permute-start(bf16[4,400,128]{2,1,0:T(8,128)(2,1)S(1)} %pad_maximum_fusion.refs_0_), channel_id=1, source_target_pairs={{0,1},{1,0},{2,3},{3,2},{4,5},{5,4},{6,7},{7,6},{8,9},{9,8},{10,11... | collective-permute-start | bytes 1228808 | tf_op jit(solution)/shard_map/ppermute | solution.py:859
  100.5 13.2 %collective-permute-start.22 = (bf16[4,400,128]{2,1,0:T(8,128)(2,1)S(1)}, bf16[4,400,128]{2,1,0:T(8,128)(2,1)S(1)}, u32[]{:S(2)}, u32[]{:S(2)}) collective-permute-start(bf16[4,400,128]{2,1,0:T(8,128)(2,1)S(1)} %collective-permute-done.18.refs_3_), channel_id=1, source_target_pairs={{0,1},{1,0},{2,3},{3,2},{4,5},{5,4},{6,7},{7,6},{8,9},{9,8},{10,11... | collective-permute-start | bytes 1228808 | tf_op jit(solution)/shard_map/ppermute | solution.py:859
  113.3 1.7 %collective-permute-start.21 = (bf16[4,400,128]{2,1,0:T(8,128)(2,1)S(1)}, bf16[4,400,128]{2,1,0:T(8,128)(2,1)S(1)}, u32[]{:S(2)}, u32[]{:S(2)}) collective-permute-start(bf16[4,400,128]{2,1,0:T(8,128)(2,1)S(1)} %collective-permute-done.17.refs_2_), channel_id=1, source_target_pairs={{0,1},{1,0},{2,3},{3,2},{4,5},{5,4},{6,7},{7,6},{8,9},{9,8},{10,11... | collective-permute-start | bytes 1228808 | tf_op jit(solution)/shard_map/ppermute | solution.py:859
  113.4 2.2 %collective-permute-start.20 = (bf16[4,400,128]{2,1,0:T(8,128)(2,1)S(1)}, bf16[4,400,128]{2,1,0:T(8,128)(2,1)S(1)}, u32[]{:S(2)}, u32[]{:S(2)}) collective-permute-start(bf16[4,400,128]{2,1,0:T(8,128)(2,1)S(1)} %collective-permute-done.16.refs_1_), channel_id=1, source_target_pairs={{0,1},{1,0},{2,3},{3,2},{4,5},{5,4},{6,7},{7,6},{8,9},{9,8},{10,11... | collective-permute-start | bytes 1228808 | tf_op jit(solution)/shard_map/ppermute | solution.py:859
